TPU v7x, 512 devices: a whole 4x8x8 slice. The times are simulated.
512 devices in a mesh: row: 64 (over x, z, core), col: 8 (over y).
Axes of the slice: x: 4, y: 8, z: 8, core: 2. Of those that a mesh axis runs over, the one named last changes fastest.
Arguments:
- features: bfloat16 [64, 65536], P(None, ('row', 'col')), may hold values from -6 to 6
- lengthscale: float32 [64], replicated, may hold values from 5 to 12
- right_side: float32 [16, 65536], P(None, ('row', 'col')), may hold values from -40 to 40
Outputs:
- solution: float32 [16, 65536], P(None, ('row', 'col'))
- residual: float32 [16, 65536], P(None, ('row', 'col'))
All inputs are finite; a program needn't handle non-finite values.
Results may differ from a plain program's by a relative error of at most 0.0069.
Values may be sent and summed in bfloat16 or wider, within the bound.
No kernel may reach another device: no remote copies, remote signals or barrier semaphores. Data moves between devices by JAX's collectives and lax.ppermute only.
A program may use at most 64 MiB of HBM per device.

v0:
```python
import jax
import jax.numpy as jnp
from jax import lax
from jax.sharding import PartitionSpec as P

ITERS = 2


def tile_products(rows_z, rows_n, cols_z, cols_n, packed):
    count = rows_z.shape[1]
    block = min(1024, count)
    nblocks = count // block
    stacked_z = jnp.transpose(rows_z.reshape(rows_z.shape[0], nblocks, block), (1, 0, 2))
    stacked_n = rows_n.reshape(nblocks, block)

    def one_block(pair):
        block_z, block_n = pair
        inner = lax.dot_general(
            block_z, cols_z, (((0,), (0,)), ((), ())), preferred_element_type=jnp.float32
        )
        tile = jnp.exp(-0.5 * (block_n[:, None] + cols_n[None, :] - 2.0 * inner)).astype(
            jnp.bfloat16
        )
        return lax.dot_general(
            packed, tile, (((1,), (1,)), ((), ())), preferred_element_type=jnp.float32
        )

    pieces = lax.map(one_block, (stacked_z, stacked_n))
    return jnp.transpose(pieces, (1, 0, 2)).reshape(packed.shape[0], count)


def squared(values):
    wide = values.astype(jnp.float32)
    return jnp.sum(wide * wide, axis=0)


def per_device(features, lengthscale, right_side):
    inverse = 1.0 / lengthscale
    scaled = (features.astype(jnp.float32) * inverse[:, None]).astype(jnp.bfloat16)
    by_row = lax.all_gather(scaled, "row", axis=1, tiled=True)
    by_col = lax.all_gather(scaled, "col", axis=1, tiled=True)
    norms_row = squared(by_row)
    norms_col = squared(by_col)
    total = right_side.shape[1] * lax.axis_size("row") * lax.axis_size("col")
    factor = float(total) ** (-0.5)

    def local_sum(left, right):
        return jnp.sum(left * right, axis=1, keepdims=True)

    solution = jnp.zeros_like(right_side)
    residual = right_side
    direction = right_side

    def norm_of(values):
        return lax.psum(local_sum(values, values), ("row", "col"))

    norm_now = norm_of(residual)
    for step in range(ITERS):
        packed = direction.astype(jnp.bfloat16)
        sums = tile_products(
            by_row, norms_row, by_col, norms_col, lax.all_gather(packed, "col", axis=1, tiled=True)
        )
        part = lax.psum_scatter(sums, "row", scatter_dimension=1, tiled=True)
        image = direction + factor * part
        curve = lax.psum(local_sum(direction, image), ("row", "col"))
        alpha = norm_now / curve
        solution = solution + alpha * direction
        residual = residual - alpha * image
        if step + 1 < ITERS:
            norm_next = norm_of(residual)
            direction = residual + norm_next / norm_now * direction
            norm_now = norm_next
    return (solution, residual)


def solution(mesh):
    placed = (P(None, ("row", "col")), P(), P(None, ("row", "col")))
    return jax.shard_map(
        per_device,
        mesh=mesh,
        in_specs=placed,
        out_specs=(P(None, ("row", "col")), P(None, ("row", "col"))),
        check_vma=False,
    )
```

profile of v0, /device:TPU:1, one launch (start us, length us, event | category | flops | bytes accessed | tf_op | source)
XLA Modules:
  0.0 718.1 jit_solution(18070898543711563844)
XLA Ops:
  7.2 0.0 all-gather.2.cloned.1.call-start
  7.2 0.7 broadcast_divide_fusion
  7.9 1.4 multiply_convert_fusion
  9.3 0.0 all-gather.2.cloned.1.call-update
  9.3 0.0 reduce-scatter.3.cloned.1.call-start
  9.3 0.7 convert_element_type.28
  10.0 19.6 %all_gather.14 = bf16[16,1024]{1,0:T(8,128)(2,1)S(1)} all-gather(bf16[16,128]{1,0:T(8,128)(2,1)S(1)} %convert_element_type.28), channel_id=1, replica_groups=mesh['row'=64,'col'=8] {'col'}, dimensions={1}, use_global_device_ids=true | all-gather | bytes 36864 | tf_op jit(solution)/shard_map/all_gather | solution.py:61
  29.7 16.5 %all_gather.13 = bf16[64,1024]{1,0:T(8,128)(2,1)S(1)} all-gather(bf16[64,128]{1,0:T(8,128)(2,1)} %multiply_convert_fusion), channel_id=1, replica_groups=mesh['row'=64,'col'=8] {'col'}, dimensions={1}, use_global_device_ids=true | all-gather | bytes 147456 | tf_op jit(solution)/shard_map/all_gather | solution.py:41
  46.2 47.4 %all-gather.2.cloned.1.call-done = bf16[64,8192]{1,0:T(8,128)(2,1)} async-done(((bf16[64,128]{1,0:T(8,128)(2,1)}), bf16[64,8192]{1,0:T(8,128)(2,1)}) %all-gather.2.cloned.1.call-update) | async-done | bytes 1048592 | tf_op jit(solution)/shard_map/all_gather | solution.py:40
  93.7 0.0 copy-start
  93.7 1.4 copy.12
  95.0 0.2 copy-done
  95.2 0.3 multiply_reduce_fusion
  95.5 12.0 %while.20 = (s32[]{:T(128)}, f32[8,16,1024]{2,1,0:T(8,128)S(1)}, f32[8,1024]{1,0:T(8,128)S(1)}, f32[1024]{0:T(1024)S(1)}, bf16[8,64,1024]{2,1,0:T(8,128)(2,1)S(1...) while((s32[]{:T(128)}, f32[8,16,1024]{2,1,0:T(8,128)S(1)}, ...), condition=%wide.region_5.6_spmd, body=%wide.region_4.5_spmd.sunk | while | flops 173015040 | bytes 377945 | solution.py:28
  95.6 1.5 fusion.38
  97.1 1.5 fusion.38
  98.5 1.5 fusion.38
  100.0 1.5 fusion.38
  101.5 1.5 fusion.38
  103.0 1.5 fusion.38
  104.5 1.5 fusion.38
  106.0 1.5 fusion.38
  107.5 0.0 copy-start.1
  107.5 0.8 copy.9
  108.3 0.0 reduce-scatter.3.cloned.1.call-update
  108.4 0.0 reduce-scatter.5.cloned.1.call-start
  108.4 135.5 %reduce-scatter.3.cloned.1.call-done = f32[16,128]{1,0:T(8,128)} async-done(((f32[16,8192]{1,0:T(8,128)}), f32[16,128]{1,0:T(8,128)}) %reduce-scatter.3.cloned.1.call-update) | async-done | bytes 8208 | tf_op jit(solution)/shard_map/reduce_scatter | solution.py:63
  243.9 0.0 copy-done.1
  243.9 0.8 multiply_reduce_fusion.4
  244.7 100.7 %all-reduce = (f32[16,1]{0,1:T(1,128)S(1)}, f32[16,1]{0,1:T(1,128)S(1)}) all-reduce(f32[16,1]{0,1:T(1,128)S(1)} %bitcast.78, f32[16,1]{0,1:T(1,128)S(1)} %bitcast.77), channel_id=1, replica_groups=mesh['row'=64,'col'=8] {'row','col'}, use_global_device_ids=true, to_apply=%region_1.0 | all-reduce | flops 32 | bytes 256 | tf_op jit(solution)/shard_map/psum | solution.py:55
  345.4 0.9 multiply_reduce_fusion.3
  346.3 94.9 %psum.30 = f32[16,1]{0,1:T(1,128)S(1)} all-reduce(f32[16,1]{0,1:T(1,128)S(1)} %bitcast.79), channel_id=1, replica_groups=mesh['row'=64,'col'=8] {'row','col'}, use_global_device_ids=true, to_apply=%region_10.11 | all-reduce | flops 16 | bytes 128 | tf_op jit(solution)/shard_map/psum | solution.py:55
  441.2 0.8 fusion.22
  442.0 16.6 %all_gather.15 = bf16[16,1024]{1,0:T(8,128)(2,1)S(1)} all-gather(bf16[16,128]{1,0:T(8,128)(2,1)S(1)} %fusion.22), channel_id=1, replica_groups=mesh['row'=64,'col'=8] {'col'}, dimensions={1}, use_global_device_ids=true | all-gather | bytes 36864 | tf_op jit(solution)/shard_map/all_gather | solution.py:61
  458.6 11.9 %while.21 = (s32[]{:T(128)}, f32[8,16,1024]{2,1,0:T(8,128)S(1)}, f32[8,1024]{1,0:T(8,128)S(1)}, f32[1024]{0:T(1024)S(1)}, bf16[8,64,1024]{2,1,0:T(8,128)(2,1)S(1...) while((s32[]{:T(128)}, f32[8,16,1024]{2,1,0:T(8,128)S(1)}, ...), condition=%wide.region_12.13_spmd, body=%wide.region_11.12_spmd.sunk | while | flops 173015040 | bytes 377945 | solution.py:28
  458.7 1.5 fusion.42
  460.2 1.5 fusion.42
  461.7 1.5 fusion.42
  463.2 1.5 fusion.42
  464.6 1.5 fusion.42
  466.1 1.5 fusion.42
  467.6 1.5 fusion.42
  469.1 1.5 fusion.42
  470.6 0.0 copy-start.2
  470.6 0.8 copy.10
  471.4 0.0 reduce-scatter.5.cloned.1.call-update
  471.5 137.2 %reduce-scatter.5.cloned.1.call-done = f32[16,128]{1,0:T(8,128)} async-done(((f32[16,8192]{1,0:T(8,128)}), f32[16,128]{1,0:T(8,128)}) %reduce-scatter.5.cloned.1.call-update) | async-done | bytes 8208 | tf_op jit(solution)/shard_map/reduce_scatter | solution.py:63
  608.6 0.0 copy-done.2
  608.6 0.9 multiply_reduce_fusion.2
  609.5 100.7 %psum.31 = f32[16,1]{0,1:T(1,128)S(1)} all-reduce(f32[16,1]{0,1:T(1,128)S(1)} %bitcast.80), channel_id=1, replica_groups=mesh['row'=64,'col'=8] {'row','col'}, use_global_device_ids=true, to_apply=%region_15.16 | all-reduce | flops 16 | bytes 128 | tf_op jit(solution)/shard_map/psum | solution.py:65
  710.2 1.4 multiply_subtract_fusion
  (23 shorter events, 0.5 us)
Async XLA Ops:
  7.2 86.5 %all-gather.2.cloned.1.call-start = ((), (), s32[]{:S(2)}) async-start(), calls=%async_computation.2 | async-start | bytes 1064960 | tf_op jit(solution)/shard_map/all_gather | solution.py:40
  9.3 234.6 %reduce-scatter.3.cloned.1.call-start = ((), (), s32[]{:S(2)}) async-start(), calls=%async_computation.3 | async-start | bytes 532480 | tf_op jit(solution)/shard_map/reduce_scatter | solution.py:63
  93.7 1.5 copy-start
  107.5 136.4 %copy-start.1 = (f32[16,128]{1,0:T(8,128)S(1)}, f32[16,128]{1,0:T(8,128)}, u32[]{:S(2)}) copy-start(f32[16,128]{1,0:T(8,128)} %param.9) | copy-start | bytes 24580
  108.4 500.3 %reduce-scatter.5.cloned.1.call-start = ((), (), s32[]{:S(2)}) async-start(), calls=%async_computation.4 | async-start | bytes 532480 | tf_op jit(solution)/shard_map/reduce_scatter | solution.py:63
  470.6 138.0 %copy-start.2 = (f32[16,128]{1,0:T(8,128)S(1)}, f32[16,128]{1,0:T(8,128)}, u32[]{:S(2)}) copy-start(f32[16,128]{1,0:T(8,128)} %reduce-scatter.3.cloned.1.call-done) | copy-start | bytes 24580
Sparse Core Ops, SparseCore 0:
  11.1 82.4 all-gather.1
  108.5 135.3 reduce-scatter.2
  471.6 136.9 reduce-scatter.4
where the time goes:
time: 719 us; the launch traced here: 718 us
  blocking collectives  349 us (49%)
  waiting for transfers between devices  320 us (45%)
  matrix products  23.4 us (3%)
  between operations  13.8 us (2%)
  other arithmetic  7.8 us (1%)
    reduce_scatter x2, waiting for transfers between devices, per_device(): part = lax.psum_scatter(sums, 'row', scatter_dimension=1, tiled=True)  273 us
    psum x2, blocking collectives, norm_of(): return lax.psum(local_sum(values, values), ('row', 'col'))  196 us
    psum x1, blocking collectives, per_device(): curve = lax.psum(local_sum(direction, image), ('row', 'col'))  101 us
    all_gather x1, waiting for transfers between devices, per_device(): by_row = lax.all_gather(scaled, 'row', axis=1, tiled=True)  47.4 us
    all_gather x2, blocking collectives, per_device(): lax.all_gather(packed, 'col', axis=1, tiled=True)  36.2 us
    dot_general x16, matrix products, one_block(): lax.dot_general(packed, tile, (((1,), (1,)), ((), ())), preferred_element...  23.4 us
    all_gather x1, blocking collectives, per_device(): by_col = lax.all_gather(scaled, 'col', axis=1, tiled=True)  16.5 us
  transfers between devices with their start and end apart: 3, of which 3 were waited for; matrix products, arithmetic and copies ran while one was open for 0% of the time, Pallas kernels for 0%

commit v1 on v0

v1 whole, which is shorter than its diff:
```python
import functools

import jax
import jax.numpy as jnp
from jax import lax
from jax.experimental import pallas as pl
from jax.experimental.pallas import tpu as pltpu
from jax.sharding import Mesh, PartitionSpec as P

F32, BF16 = jnp.float32, jnp.bfloat16
EXTRA = 16
AXES = ("x", "z", "core", "y")
PARAMS = dict(vmem_limit_bytes=48 << 20)


def pieces(value):
    high = value.astype(BF16).astype(F32)
    middle = (value - high).astype(BF16).astype(F32)
    return high, middle, value - high - middle


def augmented(raw, inverse, offset):
    scaled = (raw.astype(F32) * inverse).astype(BF16)
    wide = scaled.astype(F32)
    half = jnp.sum(wide * wide, axis=0, keepdims=True) * -0.5
    high, middle, low = pieces(half)
    row = lax.broadcasted_iota(jnp.int32, (EXTRA, raw.shape[1]), 0)
    below = jnp.where(row < 6, 1.0, 0.0)
    for index, part in enumerate((high, middle, low)):
        below = jnp.where(row == offset + index, part, below)
    return jnp.concatenate([scaled, below.astype(BF16)], axis=0)


def first_product(feats, chunk, scale_ref, cols_ref, rows_ref, start_ref, tile_ref, sums_ref, cols, rows):
    inverse = 1.0 / scale_ref[...]
    ncols, width = cols_ref.shape[0], cols_ref.shape[2]

    @pl.when(pl.program_id(0) == 0)
    def _():
        for index in range(ncols):
            block = augmented(cols_ref[index], inverse, 0).astype(F32)
            cols[pl.ds(index * width, width), :] = jnp.transpose(block).astype(BF16)
        sums_ref[...] = start_ref[...]

    nrows = rows_ref.shape[0]
    for index in range(nrows):
        rows[:, index * width:(index + 1) * width] = augmented(rows_ref[index, :feats, :], inverse, 3)
    vectors = jnp.concatenate([rows_ref[index, feats:, :] for index in range(nrows)], axis=1)
    for begin in range(0, ncols * width, chunk):
        inner = jnp.dot(cols[begin:begin + chunk, :], rows[...], preferred_element_type=F32)
        tile = jnp.exp(inner).astype(BF16)
        tile_ref[begin:begin + chunk, :] = tile
        part = lax.dot_general(vectors, tile, (((1,), (1,)), ((), ())), preferred_element_type=F32)
        for index in range(chunk // width):
            sums_ref[begin // width + index] += part[:, index * width:(index + 1) * width]


def make_tile(scale, cols, rows, start, step=8, chunk=512):
    ncols, feats, width = cols.shape
    total, depth = rows.shape[0], feats + EXTRA
    probes = rows.shape[1] - feats
    whole = pl.BlockSpec((ncols, probes, width), lambda i: (0, 0, 0))
    return pl.pallas_call(
        functools.partial(first_product, feats, chunk),
        grid=(total // step,),
        in_specs=[
            pl.BlockSpec((feats, 1), lambda i: (0, 0)),
            pl.BlockSpec(cols.shape, lambda i: (0, 0, 0)),
            pl.BlockSpec((step,) + rows.shape[1:], lambda i: (i, 0, 0)),
            whole,
        ],
        out_specs=[pl.BlockSpec((ncols * width, step * width), lambda i: (0, i)), whole],
        out_shape=[
            jax.ShapeDtypeStruct((ncols * width, total * width), BF16),
            jax.ShapeDtypeStruct((ncols, probes, width), F32),
        ],
        scratch_shapes=[pltpu.VMEM((ncols * width, depth), BF16), pltpu.VMEM((depth, step * width), BF16)],
        compiler_params=pltpu.CompilerParams(**PARAMS),
    )(scale, cols, rows, start)


def second_product(tile_ref, rows_ref, start_ref, sums_ref):
    ncols, width = sums_ref.shape[0], sums_ref.shape[2]

    @pl.when(pl.program_id(0) == 0)
    def _():
        sums_ref[...] = start_ref[...]

    vectors = jnp.concatenate([rows_ref[index] for index in range(rows_ref.shape[0])], axis=1)
    part = lax.dot_general(vectors, tile_ref[...], (((1,), (1,)), ((), ())), preferred_element_type=F32)
    for index in range(ncols):
        sums_ref[index] += part[:, index * width:(index + 1) * width]


def use_tile(tile, rows, start, step=16):
    total, probes, width = rows.shape
    whole = pl.BlockSpec(start.shape, lambda i: (0, 0, 0))
    return pl.pallas_call(
        second_product,
        grid=(total // step,),
        in_specs=[
            pl.BlockSpec((tile.shape[0], step * width), lambda i: (0, i)),
            pl.BlockSpec((step, probes, width), lambda i: (i, 0, 0)),
            whole,
        ],
        out_specs=whole,
        out_shape=jax.ShapeDtypeStruct(start.shape, F32),
        compiler_params=pltpu.CompilerParams(**PARAMS),
    )(tile, rows, start)


def spread(factor, parts_ref, image_ref, copies_ref):
    image = jnp.sum(parts_ref[...], axis=0) * factor
    image_ref[...] = image
    small = image.astype(BF16)
    for index in range(copies_ref.shape[0]):
        copies_ref[index] = small


def moments(factor, parts_ref, right_ref, image_ref, second_ref, out_ref):
    right, image = right_ref[...], image_ref[...]
    second = jnp.sum(parts_ref[...], axis=0) * factor
    second_ref[...] = second
    lane = lax.broadcasted_iota(jnp.int32, right.shape, 1)
    row = lax.broadcasted_iota(jnp.int32, right.shape, 0)
    placed = jnp.zeros_like(right)
    pairs = ((right, right), (right, image), (image, image), (image, second), (right, second))
    for index, (left, other) in enumerate(pairs):
        value = jnp.sum(left * other, axis=1, keepdims=True)
        placed = jnp.where(lane == row + index * right.shape[0], value, placed)
    out_ref[...] = jnp.sum(placed, axis=0, keepdims=True)


def finish(all_ref, right_ref, image_ref, second_ref, solution_ref, residual_ref):
    right, image, second = right_ref[...], image_ref[...], second_ref[...]
    totals = jnp.sum(all_ref[...], axis=0, keepdims=True)
    lane = lax.broadcasted_iota(jnp.int32, right.shape, 1)
    row = lax.broadcasted_iota(jnp.int32, right.shape, 0)

    def moment(index):
        return jnp.sum(jnp.where(lane == row + index * right.shape[0], totals, 0.0), axis=1, keepdims=True)

    bb, bu, uu, uw, bw = [moment(index) for index in range(5)]
    curve = bb + bu
    alpha = bb / curve
    rest = bu / curve
    norm = rest * rest * bb - 2.0 * alpha * rest * bu + alpha * alpha * uu
    lead = rest + norm / bb
    bend = (
        lead * lead * bb - 2.0 * lead * alpha * bu + alpha * alpha * uu
        + lead * (lead * bu - alpha * uu) - alpha * (lead * bw - alpha * uw)
    )
    later = norm / bend
    direction = lead * right - alpha * image
    solution_ref[...] = alpha * right + later * direction
    residual_ref[...] = right - alpha * (right + image) - later * (direction + lead * image - alpha * second)


def per_device(features, lengthscale, right_side):
    nx, nz, ny = lax.axis_size("x"), lax.axis_size("z"), lax.axis_size("y")
    feats, width = features.shape
    probes = right_side.shape[0]
    total = width * nx * nz * ny * lax.axis_size("core")
    factor = float(total) ** (-0.5)
    block = jax.ShapeDtypeStruct(right_side.shape, F32)
    swap = [(0, 1), (1, 0)]

    def exchange(values, axes):
        return lax.all_to_all(values, axes, 0, 0, tiled=True)

    scale = lengthscale.reshape(feats, 1)
    packed = jnp.concatenate([features, right_side.astype(BF16)], axis=0)
    cols = exchange(jnp.broadcast_to(features, (ny, feats, width)), "y")
    near = exchange(jnp.broadcast_to(packed, (nx * nz, feats + probes, width)), ("x", "z"))
    far = lax.ppermute(near, "core", swap)
    zeros = jnp.zeros((ny, probes, width), F32)
    tile_near, sums = make_tile(scale, cols, near, zeros)
    tile_far, sums = make_tile(scale, cols, far, sums)

    image, copies = pl.pallas_call(
        functools.partial(spread, factor),
        out_shape=[block, jax.ShapeDtypeStruct((nx * nz, probes, width), BF16)],
    )(exchange(sums, "y"))
    near = exchange(copies, ("x", "z"))
    far = lax.ppermute(near, "core", swap)
    sums = use_tile(tile_far, far, use_tile(tile_near, near, zeros))

    second, local = pl.pallas_call(
        functools.partial(moments, factor),
        out_shape=[block, jax.ShapeDtypeStruct((1, width), F32)],
    )(exchange(sums, "y"), right_side, image)
    local = lax.psum(local, "core")
    everyone = exchange(jnp.broadcast_to(local, (nx * nz * ny, width)), ("x", "z", "y"))
    return pl.pallas_call(finish, out_shape=[block, block])(everyone, right_side, image, second)


def solution(mesh):
    fine = Mesh(mesh.devices.reshape(4, 8, 2, 8), AXES)
    placed = P(None, AXES)
    return jax.shard_map(
        per_device,
        mesh=fine,
        in_specs=(placed, P(), placed),
        out_specs=(placed, placed),
        check_vma=False,
    )
```

time: 719 us -> 149 us (0.21)
  waiting for transfers between devices: 320 us -> 7.77 us
  blocking collectives: 349 us -> 89.6 us
  Pallas kernels: 0 us -> 27 us
  matrix products: 23.4 us -> 0 us
  starting transfers between devices: 0.12 us -> 19.8 us
  between operations: 13.8 us -> 0.66 us
    psum x3 -> x1, blocking collectives: 296 us -> 3.48 us  [per_device(): local = lax.psum(local, 'core')]
    reduce_scatter x2 -> x0, waiting for transfers between devices: 273 us -> none  [per_device(): part = lax.psum_scatter(sums, 'row', scatter_dimension=1, tiled=True)]
    all_to_all x0 -> x5, blocking collectives: none -> 86.1 us  [exchange(): return lax.all_to_all(values, axes, 0, 0, tiled=True)]
    all_gather x3 -> x0, blocking collectives: 52.7 us -> none  [the longest x2 36.2 us: per_device(): lax.all_gather(packed, 'col', axis=1, tiled=True)]
    all_gather x1 -> x0, waiting for transfers between devices: 47.4 us -> none  [per_device(): by_row = lax.all_gather(scaled, 'row', axis=1, tiled=True)]
    pallas_call x0 -> x7, Pallas kernels: none -> 27 us  [the longest x2 13.1 us: make_tile(): pl.pallas_call(functools.partial(first_product, feats, chunk), grid=(tota...]
    dot_general x16 -> x0, matrix products: 23.4 us -> none  [one_block(): lax.dot_general(packed, tile, (((1,), (1,)), ((), ())), preferred_element...]
    ppermute x0 -> x2, starting transfers between devices: none -> 12.9 us  [per_device(): far = lax.ppermute(near, 'core', swap)]
  transfers between devices with their start and end apart: 3 -> 3, of which waited for: 3 -> 1; matrix products, arithmetic and copies ran while one was open for 0% -> 1% of each run, Pallas kernels for 0% -> 8%
where the time goes in v1:
time: 149 us
  blocking collectives  89.6 us (60%)
  Pallas kernels  27 us (18%)
  starting transfers between devices  19.8 us (13%)
  waiting for transfers between devices  7.77 us (5%)
  local copies, waits for them, and re-layouts  2.29 us (2%)
    all_to_all x5, blocking collectives, exchange(): return lax.all_to_all(values, axes, 0, 0, tiled=True)  86.1 us
    pallas_call x2, Pallas kernels, make_tile(): pl.pallas_call(functools.partial(first_product, feats, chunk), grid=(tota...  13.1 us
    ppermute x2, starting transfers between devices, per_device(): far = lax.ppermute(near, 'core', swap)  12.9 us
    pallas_call x2, Pallas kernels, use_tile(): pl.pallas_call(second_product, grid=(total // step,), in_specs=[pl.BlockS...  9.34 us
    all_to_all x1, waiting for transfers between devices, exchange(): return lax.all_to_all(values, axes, 0, 0, tiled=True)  7.77 us
    all_to_all x1, starting transfers between devices, exchange(): return lax.all_to_all(values, axes, 0, 0, tiled=True)  6.82 us
    psum x1, blocking collectives, per_device(): local = lax.psum(local, 'core')  3.48 us
  transfers between devices with their start and end apart: 3, of which 1 were waited for; matrix products, arithmetic and copies ran while one was open for 1% of the time, Pallas kernels for 8%

profile of v1, /device:TPU:1, one launch (start us, length us, event | category | flops | bytes accessed | tf_op | source)
XLA Modules:
  0.0 148.6 jit_solution(4278641609756256633)
XLA Ops:
  0.6 0.7 convert_element_type.3
  1.3 0.7 pad_maximum_fusion
  2.0 0.1 broadcast_in_dim.15
  2.1 29.9 %all_to_all.33.rows_ref = bf16[32,80,128]{2,1,0:T(8,128)(2,1)S(1)} all-to-all(bf16[32,80,128]{2,1,0:T(8,128)(2,1)S(1)} %broadcast_in_dim.15), channel_id=1, replica_groups=mesh['x'=4,'z'=8,'core'=2,'y'=8] {'x','z'}, dimensions={0} | all-to-all | bytes 1310720 | tf_op jit(solution)/shard_map/all_to_all | solution.py:169
  32.0 6.9 %collective-permute-start = (bf16[32,80,128]{2,1,0:T(8,128)(2,1)S(1)}, bf16[32,80,128]{2,1,0:T(8,128)(2,1)S(1)}, u32[]{:S(2)}, u32[]{:S(2)}) collective-permute-start(bf16[32,80,128]{2,1,0:T(8,128)(2,1)S(1)} %all_to_all.33.rows_ref), channel_id=1, source_target_pairs={{0,8},{8,0},{1,9},{9,1},{2,10},{10,2},{3,11},{11,3},{4,12},{12,4},... | collective-permute-start | bytes 1966088 | tf_op jit(solution)/shard_map/ppermute | solution.py:175
  39.0 1.4 broadcast_in_dim.14
  40.3 6.8 %all-to-all-start = ((bf16[8,64,128]{2,1,0:T(8,128)(2,1)}), bf16[8,64,128]{2,1,0:T(8,128)(2,1)S(1)}, u32[]{:S(2)}, u32[]{:S(2)}) async-start(bf16[8,64,128]{2,1,0:T(8,128)(2,1)} %broadcast_in_dim.14), calls=%async_computation | async-start | bytes 262144 | tf_op jit(solution)/shard_map/all_to_all | solution.py:169
  47.2 0.7 copy.8.scale_ref
  47.9 7.8 %all-to-all-done.cols_ref = bf16[8,64,128]{2,1,0:T(8,128)(2,1)S(1)} async-done(((bf16[8,64,128]{2,1,0:T(8,128)(2,1)}), bf16[8,64,128]{2,1,0:T(8,128)(2,1)S(1)}, u32[]{:S(2)}, u32[]{:S(2)}) %all-to-all-start) | async-done | bytes 131104 | tf_op jit(solution)/shard_map/all_to_all | solution.py:169
  55.7 6.5 %shard_map.50 = (bf16[1024,4096]{1,0:T(8,128)(2,1)}, f32[8,16,128]{2,1,0:T(8,128)S(1)}) custom-call(f32[64,1]{1,0:T(8,128)S(1)} %copy.8.scale_ref, bf16[8,64,128]{2,1,0:T(8,128)(2,1)S(1)} %all-to-all-done.cols_ref, bf16[32,80,128]{2,1,0:T(8,128)(2,1)S(1)} %all_to_all.33.rows_ref, f32[8,16,128]{2,1,0:T(8,128)S(1)} %broadcast_in_dim.16.start_ref), custom_call_target="tpu_custom_call" | custom-call | tf_op jit(solution)/shard_map/pallas_call | solution.py:63
  62.2 0.0 collective-permute-done.rows_ref
  62.2 6.5 %shard_map.51 = (bf16[1024,4096]{1,0:T(8,128)(2,1)}, f32[8,16,128]{2,1,0:T(8,128)S(1)}) custom-call(f32[64,1]{1,0:T(8,128)S(1)} %copy.8.scale_ref, bf16[8,64,128]{2,1,0:T(8,128)(2,1)S(1)} %all-to-all-done.cols_ref, bf16[32,80,128]{2,1,0:T(8,128)(2,1)S(1)} %collective-permute-done.rows_ref, f32[8,16,128]{2,1,0:T(8,128)S(1)} %get-tuple-element.10.start_ref), custom_call_target="tpu_custom_call" | custom-call | tf_op jit(solution)/shard_map/pallas_call | solution.py:63
  68.7 10.3 %all_to_all.34.parts_ref = f32[8,16,128]{2,1,0:T(8,128)} all-to-all(f32[8,16,128]{2,1,0:T(8,128)S(1)} %get-tuple-element.12), channel_id=1, replica_groups=mesh['x'=4,'z'=8,'core'=2,'y'=8] {'y'}, dimensions={0} | all-to-all | bytes 131072 | tf_op jit(solution)/shard_map/all_to_all | solution.py:169
  79.0 1.5 %shard_map.52 = (f32[16,128]{1,0:T(8,128)}, bf16[32,16,128]{2,1,0:T(8,128)(2,1)}) custom-call(f32[8,16,128]{2,1,0:T(8,128)} %all_to_all.34.parts_ref), custom_call_target="tpu_custom_call" | custom-call | tf_op jit(solution)/shard_map/pallas_call | solution.py:180
  80.5 13.7 %all_to_all.35.rows_ref = bf16[32,16,128]{2,1,0:T(8,128)(2,1)S(1)} all-to-all(bf16[32,16,128]{2,1,0:T(8,128)(2,1)} %get-tuple-element.13), channel_id=1, replica_groups=mesh['x'=4,'z'=8,'core'=2,'y'=8] {'x','z'}, dimensions={0} | all-to-all | bytes 262144 | tf_op jit(solution)/shard_map/all_to_all | solution.py:169
  94.2 6.0 %collective-permute-start.1 = (bf16[32,16,128]{2,1,0:T(8,128)(2,1)S(1)}, bf16[32,16,128]{2,1,0:T(8,128)(2,1)S(1)}, u32[]{:S(2)}, u32[]{:S(2)}) collective-permute-start(bf16[32,16,128]{2,1,0:T(8,128)(2,1)S(1)} %all_to_all.35.rows_ref), channel_id=1, source_target_pairs={{0,8},{8,0},{1,9},{9,1},{2,10},{10,2},{3,11},{11,3},{4,12},{12,4},... | collective-permute-start | bytes 393224 | tf_op jit(solution)/shard_map/ppermute | solution.py:185
  100.3 4.7 %shard_map.53.start_ref = f32[8,16,128]{2,1,0:T(8,128)S(1)} custom-call(bf16[1024,4096]{1,0:T(8,128)(2,1)} %get-tuple-element.14.tile_ref, bf16[32,16,128]{2,1,0:T(8,128)(2,1)S(1)} %all_to_all.35.rows_ref, f32[8,16,128]{2,1,0:T(8,128)S(1)} %broadcast_in_dim.16.start_ref), custom_call_target="tpu_custom_call" | custom-call | tf_op jit(solution)/shard_map/pallas_call | solution.py:98
  105.0 0.0 collective-permute-done.1.rows_ref
  105.0 4.7 %shard_map.54 = f32[8,16,128]{2,1,0:T(8,128)S(1)} custom-call(bf16[1024,4096]{1,0:T(8,128)(2,1)} %get-tuple-element.11.tile_ref, bf16[32,16,128]{2,1,0:T(8,128)(2,1)S(1)} %collective-permute-done.1.rows_ref, f32[8,16,128]{2,1,0:T(8,128)S(1)} %shard_map.53.start_ref), custom_call_target="tpu_custom_call" | custom-call | tf_op jit(solution)/shard_map/pallas_call | solution.py:98
  109.6 10.4 %all_to_all.36.parts_ref = f32[8,16,128]{2,1,0:T(8,128)} all-to-all(f32[8,16,128]{2,1,0:T(8,128)S(1)} %shard_map.54), channel_id=1, replica_groups=mesh['x'=4,'z'=8,'core'=2,'y'=8] {'y'}, dimensions={0} | all-to-all | bytes 131072 | tf_op jit(solution)/shard_map/all_to_all | solution.py:169
  120.1 1.5 shard_map.55
  121.5 3.5 %psum.10 = f32[128]{0:T(128)S(1)} all-reduce(f32[128]{0:T(128)} %bitcast.5), channel_id=1, replica_groups=mesh['x'=4,'z'=8,'core'=2,'y'=8] {'core'}, use_global_device_ids=true, to_apply=%region_0.0 | all-reduce | flops 128 | bytes 1024 | tf_op jit(solution)/shard_map/psum | solution.py:192
  125.0 0.1 broadcast_in_dim.17
  125.1 21.8 %all_to_all.37 = f32[256,1,128]{2,1,0:T(1,128)} all-to-all(f32[256,1,128]{2,1,0:T(1,128)S(1)} %broadcast_in_dim.17), channel_id=1, replica_groups=mesh['x'=4,'z'=8,'core'=2,'y'=8] {'x','z','y'}, dimensions={0} | all-to-all | bytes 262144 | tf_op jit(solution)/shard_map/all_to_all | solution.py:169
  146.9 1.7 %shard_map.56 = (f32[16,128]{1,0:T(8,128)}, f32[16,128]{1,0:T(8,128)}) custom-call(f32[256,128]{1,0:T(8,128)} %bitcast.3, f32[16,128]{1,0:T(8,128)} %right_ref.3, f32[16,128]{1,0:T(8,128)} %get-tuple-element.15.image_ref, f32[16,128]{1,0:T(8,128)} %get-tuple-element.17.second_ref), custom_call_target="tpu_custom_call" | custom-call | tf_op jit(solution)/shard_map/pallas_call | solution.py:194
  (1 shorter events, 0.0 us)
Async XLA Ops:
  32.0 30.2 %collective-permute-start = (bf16[32,80,128]{2,1,0:T(8,128)(2,1)S(1)}, bf16[32,80,128]{2,1,0:T(8,128)(2,1)S(1)}, u32[]{:S(2)}, u32[]{:S(2)}) collective-permute-start(bf16[32,80,128]{2,1,0:T(8,128)(2,1)S(1)} %all_to_all.33.rows_ref), channel_id=1, source_target_pairs={{0,8},{8,0},{1,9},{9,1},{2,10},{10,2},{3,11},{11,3},{4,12},{12,4},... | collective-permute-start | bytes 1966088 | tf_op jit(solution)/shard_map/ppermute | solution.py:175
  40.3 15.3 %all-to-all-start = ((bf16[8,64,128]{2,1,0:T(8,128)(2,1)}), bf16[8,64,128]{2,1,0:T(8,128)(2,1)S(1)}, u32[]{:S(2)}, u32[]{:S(2)}) async-start(bf16[8,64,128]{2,1,0:T(8,128)(2,1)} %broadcast_in_dim.14), calls=%async_computation | async-start | bytes 262144 | tf_op jit(solution)/shard_map/all_to_all | solution.py:169
  94.2 10.7 %collective-permute-start.1 = (bf16[32,16,128]{2,1,0:T(8,128)(2,1)S(1)}, bf16[32,16,128]{2,1,0:T(8,128)(2,1)S(1)}, u32[]{:S(2)}, u32[]{:S(2)}) collective-permute-start(bf16[32,16,128]{2,1,0:T(8,128)(2,1)S(1)} %all_to_all.35.rows_ref), channel_id=1, source_target_pairs={{0,8},{8,0},{1,9},{9,1},{2,10},{10,2},{3,11},{11,3},{4,12},{12,4},... | collective-permute-start | bytes 393224 | tf_op jit(solution)/shard_map/ppermute | solution.py:185

commit v2 on v0

v2 whole, which is shorter than its diff:
```python
import functools

import jax
import jax.numpy as jnp
from jax import lax
from jax.experimental import pallas as pl
from jax.experimental.pallas import tpu as pltpu
from jax.sharding import Mesh, PartitionSpec as P

F32, BF16 = jnp.float32, jnp.bfloat16
EXTRA = 16
PAD = 8
CHUNK = 256
AXES = ("x", "z", "core", "y")
VMEM = pl.BlockSpec(memory_space=pltpu.VMEM)


def call(kernel, *args, outs, limit=16, scratch=()):
    return pl.pallas_call(
        kernel,
        in_specs=[VMEM] * len(args),
        out_specs=jax.tree.map(lambda _: VMEM, outs),
        out_shape=outs,
        scratch_shapes=scratch,
        compiler_params=pltpu.CompilerParams(vmem_limit_bytes=limit << 20),
    )(*args)


def shaped(dtype, *shape):
    return jax.ShapeDtypeStruct(shape, dtype)


def pieces(value):
    high = value.astype(BF16).astype(F32)
    middle = (value - high).astype(BF16).astype(F32)
    return high, middle, value - high - middle


def augmented(raw, inverse, offset):
    scaled = (raw.astype(F32) * inverse).astype(BF16)
    wide = scaled.astype(F32)
    half = jnp.sum(wide * wide, axis=0, keepdims=True) * -0.5
    high, middle, low = pieces(half)
    row = lax.broadcasted_iota(jnp.int32, (EXTRA, raw.shape[1]), 0)
    below = jnp.where(row < 6, 1.0, 0.0)
    for index, part in enumerate((high, middle, low)):
        below = jnp.where(row == offset + index, part, below)
    return jnp.concatenate([scaled, below.astype(BF16)], axis=0)


def copies(features_ref, right_ref, cols_ref, rows_ref):
    features, right = features_ref[...], right_ref[...].astype(BF16)
    feats = features.shape[0]
    for index in range(cols_ref.shape[0]):
        cols_ref[index] = features
    for index in range(rows_ref.shape[0]):
        rows_ref[index, :feats, :] = features
        rows_ref[index, feats:, :] = right


def dot_last(left, right):
    return lax.dot_general(left, right, (((1,), (1,)), ((), ())), preferred_element_type=F32)


def first_product(scale_ref, cols_ref, near_ref, far_ref, tile_near_ref, tile_far_ref, out_ref, cols, rows, sums):
    inverse = 1.0 / scale_ref[...]
    ncols, feats, width = cols_ref.shape
    probes = near_ref.shape[1] - feats
    for index in range(ncols):
        block = augmented(cols_ref[index], inverse, 0).astype(F32)
        cols[index * width:(index + 1) * width, :] = jnp.transpose(block).astype(BF16)
    for turn, (rows_ref, tile_ref) in enumerate(((near_ref, tile_near_ref), (far_ref, tile_far_ref))):
        nrows = rows_ref.shape[0]
        for index in range(nrows):
            rows[:, index * width:(index + 1) * width] = augmented(rows_ref[index, :feats, :], inverse, 3)
        vectors = jnp.concatenate([rows_ref[index, feats:, :] for index in range(nrows)], axis=1)
        for begin in range(0, ncols * width, CHUNK):
            inner = jnp.dot(cols[begin:begin + CHUNK, :], rows[...], preferred_element_type=F32)
            tile = jnp.exp(inner).astype(BF16)
            tile_ref[begin:begin + CHUNK, :] = tile
            part = dot_last(vectors, tile)
            for index in range(CHUNK // width):
                place = begin // width + index
                piece = part[:, index * width:(index + 1) * width]
                sums[place] = piece if turn == 0 else sums[place] + piece
    for index in range(ncols):
        value = sums[index]
        high = value.astype(BF16)
        low = (value - high.astype(F32)).astype(BF16)
        for peer in range(ncols):
            out_ref[peer, index * probes:(index + 1) * probes, :] = high
        out_ref[index, ncols * probes:(ncols + 1) * probes, :] = high
        out_ref[index, (ncols + 1) * probes:, :] = low


def spread(factor, parts_ref, image_ref, out_ref):
    probes = image_ref.shape[0]
    begin = parts_ref.shape[1] - 2 * probes
    own = jnp.zeros(image_ref.shape, F32)
    for peer in range(parts_ref.shape[0]):
        own += parts_ref[peer, begin:begin + probes, :].astype(F32) + parts_ref[peer, begin + probes:, :].astype(F32)
    image = own * factor
    image_ref[...] = image
    small = image.astype(BF16)
    for index in range(out_ref.shape[0]):
        out_ref[index] = small


def placed(values, shape):
    lane = lax.broadcasted_iota(jnp.int32, shape, 1)
    row = lax.broadcasted_iota(jnp.int32, shape, 0)
    grid = jnp.zeros(shape, F32)
    for index, value in values:
        grid = jnp.where(lane == row + index * shape[0], value, grid)
    return jnp.sum(grid, axis=0, keepdims=True)


def column_images(factor, parts_ref, right_ref, image_ref, cols_ref, local_ref):
    probes = right_ref.shape[0]
    for index in range(cols_ref.shape[0]):
        total = jnp.zeros(right_ref.shape, F32)
        for peer in range(parts_ref.shape[0]):
            total += parts_ref[peer, index * probes:(index + 1) * probes, :].astype(F32)
        cols_ref[index] = total * factor
    right, image = right_ref[...], image_ref[...]
    pairs = ((right, right), (right, image), (image, image))
    sums = [(k, jnp.sum(a * b, axis=1, keepdims=True)) for k, (a, b) in enumerate(pairs)]
    local_ref[...] = placed(sums, right.shape)


def second_product(tile_ref, rows_ref, sums_ref):
    width = rows_ref.shape[2]
    vectors = jnp.concatenate([rows_ref[index] for index in range(rows_ref.shape[0])], axis=1)
    part = dot_last(vectors, tile_ref[...])
    for index in range(sums_ref.shape[0]):
        sums_ref[index] = part[:, index * width:(index + 1) * width]


def third_product(factor, tile_ref, rows_ref, start_ref, images_ref, local_ref, out_ref):
    ncols, probes, width = start_ref.shape
    vectors = jnp.concatenate([rows_ref[index] for index in range(rows_ref.shape[0])], axis=1)
    part = dot_last(vectors, tile_ref[...])
    total = jnp.zeros((probes, width), F32)
    for index in range(ncols):
        second = (start_ref[index] + part[:, index * width:(index + 1) * width]) * factor
        out_ref[index, :probes, :] = second
        total += second * images_ref[index]
    energy = placed([(3, jnp.sum(total, axis=1, keepdims=True))], (probes, width))
    row = lax.broadcasted_iota(jnp.int32, (PAD, width), 0)
    scalars = jnp.where(row == 0, energy + local_ref[...], 0.0)
    for index in range(ncols):
        out_ref[index, probes:, :] = scalars


def gathered(parts_ref, second_ref, out_ref):
    total = jnp.sum(parts_ref[...], axis=0)
    probes = second_ref.shape[0]
    second_ref[...] = total[:probes]
    out_ref[...] = jnp.broadcast_to(total[probes:probes + 1], out_ref.shape)


def finish(all_ref, right_ref, image_ref, second_ref, solution_ref, residual_ref):
    right, image, second = right_ref[...], image_ref[...], second_ref[...]
    totals = jnp.sum(all_ref[...], axis=0, keepdims=True)
    lane = lax.broadcasted_iota(jnp.int32, right.shape, 1)
    row = lax.broadcasted_iota(jnp.int32, right.shape, 0)

    def moment(index):
        return jnp.sum(jnp.where(lane == row + index * right.shape[0], totals, 0.0), axis=1, keepdims=True)

    bb, bu, uu, uw = [moment(index) for index in range(4)]
    curve = bb + bu
    alpha = bb / curve
    rest = bu / curve
    norm = rest * rest * bb - 2.0 * alpha * rest * bu + alpha * alpha * uu
    lead = rest + norm / bb
    bend = (
        lead * lead * bb - 2.0 * lead * alpha * bu + alpha * alpha * uu
        + lead * (lead * bu - alpha * uu) - alpha * (lead * uu - alpha * uw)
    )
    later = norm / bend
    direction = lead * right - alpha * image
    solution_ref[...] = alpha * right + later * direction
    residual_ref[...] = right - alpha * (right + image) - later * (direction + lead * image - alpha * second)


def per_device(features, lengthscale, right_side):
    nx, nz, ncore, ny = [lax.axis_size(axis) for axis in AXES]
    feats, width = features.shape
    probes = right_side.shape[0]
    plane = nx * nz
    factor = float(width * plane * ncore * ny) ** (-0.5)
    block = shaped(F32, probes, width)
    swap = [(0, 1), (1, 0)]

    def exchange(values, axes):
        return lax.all_to_all(values, axes, 0, 0, tiled=True)

    def held(array):
        return pltpu.with_memory_space_constraint(array, pltpu.VMEM)

    cols, rows = call(
        copies, features, right_side,
        outs=[shaped(BF16, ny, feats, width), shaped(BF16, plane, feats + probes, width)],
    )
    near = exchange(rows, ("x", "z"))
    far = lax.ppermute(near, "core", swap)
    cols = exchange(cols, "y")
    tile = pltpu.VMEM((ny * width, plane * width), BF16)
    tile_near, tile_far, parts = call(
        first_product, lengthscale.reshape(feats, 1), cols, near, far,
        outs=[tile, tile, shaped(BF16, ny, (ny + 2) * probes, width)],
        limit=24,
        scratch=[
            pltpu.VMEM((ny * width, feats + EXTRA), BF16),
            pltpu.VMEM((feats + EXTRA, plane * width), BF16),
            pltpu.VMEM((ny, probes, width), F32),
        ],
    )
    parts = exchange(parts, "y")
    image, rows = call(
        functools.partial(spread, factor), parts, outs=[block, shaped(BF16, plane, probes, width)]
    )
    near = exchange(rows, ("x", "z"))
    images, local = call(
        functools.partial(column_images, factor), parts, right_side, image,
        outs=[shaped(F32, ny, probes, width), shaped(F32, 1, width)],
    )
    far = lax.ppermute(near, "core", swap)
    sums = call(second_product, held(tile_near), near, outs=shaped(F32, ny, probes, width))
    sums = call(
        functools.partial(third_product, factor), held(tile_far), far, sums, images, local,
        outs=shaped(F32, ny, probes + PAD, width),
    )
    second, local = call(gathered, exchange(sums, "y"), outs=[block, shaped(F32, plane * ncore, width)])
    everyone = exchange(local, ("x", "z", "core"))
    return call(finish, everyone, right_side, image, second, outs=[block, block])


def solution(mesh):
    fine = Mesh(mesh.devices.reshape(4, 8, 2, 8), AXES)
    split = P(None, AXES)
    return jax.shard_map(
        per_device,
        mesh=fine,
        in_specs=(split, P(), split),
        out_specs=(split, split),
        check_vma=False,
    )
```

time: 719 us -> 129 us (0.18)
  waiting for transfers between devices: 320 us -> 7.77 us
  blocking collectives: 349 us -> 81.5 us
  matrix products: 23.4 us -> 0 us
  starting transfers between devices: 0.12 us -> 20.5 us
  Pallas kernels: 0 us -> 15.4 us
  between operations: 13.8 us -> 0.68 us
  other arithmetic: 7.8 us -> 0 us
    psum x3 -> x0, blocking collectives: 296 us -> none  [the longest x2 196 us: norm_of(): return lax.psum(local_sum(values, values), ('row', 'col'))]
    reduce_scatter x2 -> x0, waiting for transfers between devices: 273 us -> none  [per_device(): part = lax.psum_scatter(sums, 'row', scatter_dimension=1, tiled=True)]
    all_to_all x0 -> x5, blocking collectives: none -> 81.5 us  [exchange(): return lax.all_to_all(values, axes, 0, 0, tiled=True)]
    all_gather x3 -> x0, blocking collectives: 52.7 us -> none  [the longest x2 36.2 us: per_device(): lax.all_gather(packed, 'col', axis=1, tiled=True)]
    all_gather x1 -> x0, waiting for transfers between devices: 47.4 us -> none  [per_device(): by_row = lax.all_gather(scaled, 'row', axis=1, tiled=True)]
    dot_general x16 -> x0, matrix products: 23.4 us -> none  [one_block(): lax.dot_general(packed, tile, (((1,), (1,)), ((), ())), preferred_element...]
    pallas_call x0 -> x8, Pallas kernels: none -> 15.4 us  [call(): pl.pallas_call(kernel, in_specs=[VMEM] * len(args), out_specs=jax.tree.ma...]
    ppermute x0 -> x2, starting transfers between devices: none -> 13.6 us  [per_device(): far = lax.ppermute(near, 'core', swap)]
  transfers between devices with their start and end apart: 3 -> 3, of which waited for: 3 -> 1; matrix products, arithmetic and copies ran while one was open for 0% -> 1% of each run, Pallas kernels for 0% -> 2%
where the time goes in v2:
time: 129 us
  blocking collectives  81.5 us (63%)
  starting transfers between devices  20.5 us (16%)
  Pallas kernels  15.4 us (12%)
  waiting for transfers between devices  7.77 us (6%)
  local copies, waits for them, and re-layouts  2.85 us (2%)
    all_to_all x5, blocking collectives, exchange(): return lax.all_to_all(values, axes, 0, 0, tiled=True)  81.5 us
    pallas_call x8, Pallas kernels, call(): pl.pallas_call(kernel, in_specs=[VMEM] * len(args), out_specs=jax.tree.ma...  15.4 us
    ppermute x2, starting transfers between devices, per_device(): far = lax.ppermute(near, 'core', swap)  13.6 us
    all_to_all x1, waiting for transfers between devices, exchange(): return lax.all_to_all(values, axes, 0, 0, tiled=True)  7.77 us
    all_to_all x1, starting transfers between devices, exchange(): return lax.all_to_all(values, axes, 0, 0, tiled=True)  6.83 us
  transfers between devices with their start and end apart: 3, of which 1 were waited for; matrix products, arithmetic and copies ran while one was open for 1% of the time, Pallas kernels for 2%

profile of v2, /device:TPU:1, one launch (start us, length us, event | category | flops | bytes accessed | tf_op | source)
XLA Modules:
  0.0 128.7 jit_solution(5292591191326620966)
XLA Ops:
  0.6 0.0 copy-start
  0.6 0.7 copy-done
  1.3 0.0 copy-start.3
  1.3 0.7 copy-done.3
  2.0 0.7 shard_map.50
  2.8 29.9 %all_to_all.36.near_ref = bf16[32,80,128]{2,1,0:T(8,128)(2,1)S(1)} all-to-all(bf16[32,80,128]{2,1,0:T(8,128)(2,1)S(1)} %get-tuple-element.14), channel_id=1, replica_groups=mesh['x'=4,'z'=8,'core'=2,'y'=8] {'x','z'}, dimensions={0} | all-to-all | bytes 1310720 | tf_op jit(solution)/shard_map/all_to_all | solution.py:197
  32.7 6.9 %collective-permute-start = (bf16[32,80,128]{2,1,0:T(8,128)(2,1)S(1)}, bf16[32,80,128]{2,1,0:T(8,128)(2,1)S(1)}, u32[]{:S(2)}, u32[]{:S(2)}) collective-permute-start(bf16[32,80,128]{2,1,0:T(8,128)(2,1)S(1)} %all_to_all.36.near_ref), channel_id=1, source_target_pairs={{0,8},{8,0},{1,9},{9,1},{2,10},{10,2},{3,11},{11,3},{4,12},{12,4},... | collective-permute-start | bytes 1966088 | tf_op jit(solution)/shard_map/ppermute | solution.py:207
  39.6 6.8 %all-to-all-start = ((bf16[8,64,128]{2,1,0:T(8,128)(2,1)}), bf16[8,64,128]{2,1,0:T(8,128)(2,1)S(1)}, u32[]{:S(2)}, u32[]{:S(2)}) async-start(bf16[8,64,128]{2,1,0:T(8,128)(2,1)} %get-tuple-element.13), calls=%async_computation | async-start | bytes 262144 | tf_op jit(solution)/shard_map/all_to_all | solution.py:197
  46.4 0.7 copy.6.scale_ref
  47.2 7.8 %all-to-all-done.cols_ref = bf16[8,64,128]{2,1,0:T(8,128)(2,1)S(1)} async-done(((bf16[8,64,128]{2,1,0:T(8,128)(2,1)}), bf16[8,64,128]{2,1,0:T(8,128)(2,1)S(1)}, u32[]{:S(2)}, u32[]{:S(2)}) %all-to-all-start) | async-done | bytes 131104 | tf_op jit(solution)/shard_map/all_to_all | solution.py:197
  54.9 0.0 collective-permute-done.far_ref
  54.9 9.2 %shard_map.51 = (bf16[1024,4096]{1,0:T(8,128)(2,1)S(1)}, bf16[1024,4096]{1,0:T(8,128)(2,1)S(1)}, bf16[8,160,128]{2,1,0:T(8,128)(2,1)S(1)}) custom-call(f32[64,1]{1,0:T(8,128)S(1)} %copy.6.scale_ref, bf16[8,64,128]{2,1,0:T(8,128)(2,1)S(1)} %all-to-all-done.cols_ref, bf16[32,80,128]{2,1,0:T(8,128)(2,1)S(1)} %all_to_all.36.near_ref, ...), custom_call_target="tpu_custom_call" | custom-call | tf_op jit(solution)/shard_map/pallas_call | solution.py:19
  64.1 13.4 %all_to_all.37.parts_ref = bf16[8,160,128]{2,1,0:T(8,128)(2,1)S(1)} all-to-all(bf16[8,160,128]{2,1,0:T(8,128)(2,1)S(1)} %get-tuple-element.16), channel_id=1, replica_groups=mesh['x'=4,'z'=8,'core'=2,'y'=8] {'y'}, dimensions={0} | all-to-all | bytes 655360 | tf_op jit(solution)/shard_map/all_to_all | solution.py:197
  77.5 13.5 %all_to_all.38.rows_ref = bf16[32,16,128]{2,1,0:T(8,128)(2,1)S(1)} all-to-all(bf16[32,16,128]{2,1,0:T(8,128)(2,1)S(1)} %get-tuple-element.17), channel_id=1, replica_groups=mesh['x'=4,'z'=8,'core'=2,'y'=8] {'x','z'}, dimensions={0} | all-to-all | bytes 262144 | tf_op jit(solution)/shard_map/all_to_all | solution.py:197
  91.0 6.7 %collective-permute-start.1 = (bf16[32,16,128]{2,1,0:T(8,128)(2,1)S(1)}, bf16[32,16,128]{2,1,0:T(8,128)(2,1)S(1)}, u32[]{:S(2)}, u32[]{:S(2)}) collective-permute-start(bf16[32,16,128]{2,1,0:T(8,128)(2,1)S(1)} %all_to_all.38.rows_ref), channel_id=1, source_target_pairs={{0,8},{8,0},{1,9},{9,1},{2,10},{10,2},{3,11},{11,3},{4,12},{12,4},... | collective-permute-start | bytes 393224 | tf_op jit(solution)/shard_map/ppermute | solution.py:229
  97.8 0.0 copy-start.1
  97.8 0.7 copy-done.1
  98.5 0.1 shard_map.54
  98.6 0.0 copy-start.2
  98.6 2.3 %shard_map.53.start_ref = f32[8,16,128]{2,1,0:T(8,128)S(1)} custom-call(bf16[1024,4096]{1,0:T(8,128)(2,1)S(1)} %get-tuple-element.18.tile_ref, bf16[32,16,128]{2,1,0:T(8,128)(2,1)S(1)} %all_to_all.38.rows_ref), custom_call_target="tpu_custom_call" | custom-call | tf_op jit(solution)/shard_map/pallas_call | solution.py:19
  100.8 0.0 collective-permute-done.1.rows_ref
  100.8 2.4 %shard_map.55 = f32[8,24,128]{2,1,0:T(8,128)S(1)} custom-call(bf16[1024,4096]{1,0:T(8,128)(2,1)S(1)} %get-tuple-element.15.tile_ref, bf16[32,16,128]{2,1,0:T(8,128)(2,1)S(1)} %collective-permute-done.1.rows_ref, f32[8,16,128]{2,1,0:T(8,128)S(1)} %shard_map.53.start_ref, f32[8,16,128]{2,1,0:T(8,128)S(1)} %get-tuple-element.20.images_ref, ...), custom_call_target="tpu_custom_call" | custom-call | tf_op jit(solution)/shard_map/pallas_call | solution.py:19
  103.2 10.5 %all_to_all.39.parts_ref = f32[8,24,128]{2,1,0:T(8,128)S(1)} all-to-all(f32[8,24,128]{2,1,0:T(8,128)S(1)} %shard_map.55), channel_id=1, replica_groups=mesh['x'=4,'z'=8,'core'=2,'y'=8] {'y'}, dimensions={0} | all-to-all | bytes 196608 | tf_op jit(solution)/shard_map/all_to_all | solution.py:197
  113.7 14.2 %all_to_all.40 = f32[64,1,128]{2,1,0:T(1,128)S(1)} all-to-all(f32[64,1,128]{2,1,0:T(1,128)S(1)} %bitcast.6), channel_id=1, replica_groups=mesh['x'=4,'z'=8,'core'=2,'y'=8] {'x','z','core'}, dimensions={0} | all-to-all | bytes 65536 | tf_op jit(solution)/shard_map/all_to_all | solution.py:197
  127.9 0.0 copy-done.2
  127.9 0.7 shard_map.57
  (2 shorter events, 0.0 us)
Async XLA Ops:
  0.6 0.7 copy-start
  1.3 0.7 copy-start.3
  32.7 22.3 %collective-permute-start = (bf16[32,80,128]{2,1,0:T(8,128)(2,1)S(1)}, bf16[32,80,128]{2,1,0:T(8,128)(2,1)S(1)}, u32[]{:S(2)}, u32[]{:S(2)}) collective-permute-start(bf16[32,80,128]{2,1,0:T(8,128)(2,1)S(1)} %all_to_all.36.near_ref), channel_id=1, source_target_pairs={{0,8},{8,0},{1,9},{9,1},{2,10},{10,2},{3,11},{11,3},{4,12},{12,4},... | collective-permute-start | bytes 1966088 | tf_op jit(solution)/shard_map/ppermute | solution.py:207
  39.6 15.3 %all-to-all-start = ((bf16[8,64,128]{2,1,0:T(8,128)(2,1)}), bf16[8,64,128]{2,1,0:T(8,128)(2,1)S(1)}, u32[]{:S(2)}, u32[]{:S(2)}) async-start(bf16[8,64,128]{2,1,0:T(8,128)(2,1)} %get-tuple-element.13), calls=%async_computation | async-start | bytes 262144 | tf_op jit(solution)/shard_map/all_to_all | solution.py:197
  91.0 9.8 %collective-permute-start.1 = (bf16[32,16,128]{2,1,0:T(8,128)(2,1)S(1)}, bf16[32,16,128]{2,1,0:T(8,128)(2,1)S(1)}, u32[]{:S(2)}, u32[]{:S(2)}) collective-permute-start(bf16[32,16,128]{2,1,0:T(8,128)(2,1)S(1)} %all_to_all.38.rows_ref), channel_id=1, source_target_pairs={{0,8},{8,0},{1,9},{9,1},{2,10},{10,2},{3,11},{11,3},{4,12},{12,4},... | collective-permute-start | bytes 393224 | tf_op jit(solution)/shard_map/ppermute | solution.py:229
  97.8 0.7 copy-start.1
  98.6 29.4 %copy-start.2 = (f32[16,128]{1,0:T(8,128)S(1)}, f32[16,128]{1,0:T(8,128)}, u32[]{:S(2)}) copy-start(f32[16,128]{1,0:T(8,128)} %right_ref.5) | copy-start | bytes 24580

commit v3 on v2

--- a/solution.py
+++ b/solution.py
@@ -15,10 +15,10 @@
 VMEM = pl.BlockSpec(memory_space=pltpu.VMEM)
 
 
-def call(kernel, *args, outs, limit=16, scratch=()):
+def call(kernel, *args, outs, limit=16, scratch=(), specs=None):
     return pl.pallas_call(
         kernel,
-        in_specs=[VMEM] * len(args),
+        in_specs=specs or [VMEM] * len(args),
         out_specs=jax.tree.map(lambda _: VMEM, outs),
         out_shape=outs,
         scratch_shapes=scratch,
@@ -48,49 +48,73 @@
     return jnp.concatenate([scaled, below.astype(BF16)], axis=0)
 
 
-def copies(features_ref, right_ref, cols_ref, rows_ref):
-    features, right = features_ref[...], right_ref[...].astype(BF16)
+def copies(features_ref, right_ref, rows_ref, kept_ref, held, sems):
+    moves = [
+        pltpu.make_async_copy(features_ref, held, sems.at[0]),
+        pltpu.make_async_copy(right_ref, kept_ref, sems.at[1]),
+    ]
+    for move in moves:
+        move.start()
+    for move in moves:
+        move.wait()
+    features, right = held[...], kept_ref[...].astype(BF16)
     feats = features.shape[0]
-    for index in range(cols_ref.shape[0]):
-        cols_ref[index] = features
     for index in range(rows_ref.shape[0]):
         rows_ref[index, :feats, :] = features
         rows_ref[index, feats:, :] = right
 
 
+def columns(scale_ref, cols_ref, inverse_ref, out_ref):
+    ncols, feats, width = cols_ref.shape
+    lane = lax.broadcasted_iota(jnp.int32, (feats, feats), 1)
+    row = lax.broadcasted_iota(jnp.int32, (feats, feats), 0)
+    scale = jnp.sum(jnp.where(lane == row, scale_ref[...], 0.0), axis=1, keepdims=True)
+    inverse = jnp.broadcast_to(1.0 / scale, (feats, width))
+    inverse_ref[...] = inverse
+    for index in range(ncols):
+        block = augmented(cols_ref[index], inverse, 0).astype(F32)
+        out_ref[index * width:(index + 1) * width, :] = jnp.transpose(block).astype(BF16)
+
+
 def dot_last(left, right):
     return lax.dot_general(left, right, (((1,), (1,)), ((), ())), preferred_element_type=F32)
 
 
-def first_product(scale_ref, cols_ref, near_ref, far_ref, tile_near_ref, tile_far_ref, out_ref, cols, rows, sums):
-    inverse = 1.0 / scale_ref[...]
-    ncols, feats, width = cols_ref.shape
-    probes = near_ref.shape[1] - feats
-    for index in range(ncols):
-        block = augmented(cols_ref[index], inverse, 0).astype(F32)
-        cols[index * width:(index + 1) * width, :] = jnp.transpose(block).astype(BF16)
-    for turn, (rows_ref, tile_ref) in enumerate(((near_ref, tile_near_ref), (far_ref, tile_far_ref))):
-        nrows = rows_ref.shape[0]
-        for index in range(nrows):
-            rows[:, index * width:(index + 1) * width] = augmented(rows_ref[index, :feats, :], inverse, 3)
-        vectors = jnp.concatenate([rows_ref[index, feats:, :] for index in range(nrows)], axis=1)
-        for begin in range(0, ncols * width, CHUNK):
-            inner = jnp.dot(cols[begin:begin + CHUNK, :], rows[...], preferred_element_type=F32)
-            tile = jnp.exp(inner).astype(BF16)
-            tile_ref[begin:begin + CHUNK, :] = tile
-            part = dot_last(vectors, tile)
-            for index in range(CHUNK // width):
-                place = begin // width + index
-                piece = part[:, index * width:(index + 1) * width]
-                sums[place] = piece if turn == 0 else sums[place] + piece
-    for index in range(ncols):
-        value = sums[index]
+def tile_and_product(inverse_ref, cols_ref, rows_ref, tile_ref, rows, add):
+    feats, width = inverse_ref.shape
+    inverse = inverse_ref[...]
+    nrows = rows_ref.shape[0]
+    for index in range(nrows):
+        rows[:, index * width:(index + 1) * width] = augmented(rows_ref[index, :feats, :], inverse, 3)
+    vectors = jnp.concatenate([rows_ref[index, feats:, :] for index in range(nrows)], axis=1)
+    for begin in range(0, cols_ref.shape[0], CHUNK):
+        inner = jnp.dot(cols_ref[begin:begin + CHUNK, :], rows[...], preferred_element_type=F32)
+        tile = jnp.exp(inner).astype(BF16)
+        tile_ref[begin:begin + CHUNK, :] = tile
+        part = dot_last(vectors, tile)
+        for index in range(CHUNK // width):
+            add(begin // width + index, part[:, index * width:(index + 1) * width])
+
+
+def near_product(inverse_ref, cols_ref, rows_ref, tile_ref, sums_ref, rows):
+    def add(index, piece):
+        sums_ref[index] = piece
+
+    tile_and_product(inverse_ref, cols_ref, rows_ref, tile_ref, rows, add)
+
+
+def far_product(inverse_ref, cols_ref, rows_ref, sums_ref, tile_ref, out_ref, rows):
+    ncols, probes, _ = sums_ref.shape
+
+    def add(index, piece):
+        value = sums_ref[index] + piece
         high = value.astype(BF16)
-        low = (value - high.astype(F32)).astype(BF16)
         for peer in range(ncols):
             out_ref[peer, index * probes:(index + 1) * probes, :] = high
         out_ref[index, ncols * probes:(ncols + 1) * probes, :] = high
-        out_ref[index, (ncols + 1) * probes:, :] = low
+        out_ref[index, (ncols + 1) * probes:, :] = (value - high.astype(F32)).astype(BF16)
+
+    tile_and_product(inverse_ref, cols_ref, rows_ref, tile_ref, rows, add)
 
 
 def spread(factor, parts_ref, image_ref, out_ref):
@@ -199,23 +223,28 @@
     def held(array):
         return pltpu.with_memory_space_constraint(array, pltpu.VMEM)
 
-    cols, rows = call(
-        copies, features, right_side,
-        outs=[shaped(BF16, ny, feats, width), shaped(BF16, plane, feats + probes, width)],
-    )
+    rows, right = call(
+        copies, features, right_side, specs=[pl.BlockSpec(memory_space=pltpu.HBM)] * 2,
+        outs=[shaped(BF16, plane, feats + probes, width), pltpu.VMEM(block.shape, F32)],
+        scratch=[pltpu.VMEM(features.shape, BF16), pltpu.SemaphoreType.DMA((2,))],
+    )
+    right = held(right)
+    cols = lax.all_gather(features, "y")
     near = exchange(rows, ("x", "z"))
+    inverse, cols = call(
+        columns, lengthscale.reshape(1, feats), cols,
+        outs=[shaped(F32, feats, width), shaped(BF16, ny * width, feats + EXTRA)],
+    )
+    near, inverse, cols = lax.optimization_barrier((near, inverse, cols))
     far = lax.ppermute(near, "core", swap)
-    cols = exchange(cols, "y")
     tile = pltpu.VMEM((ny * width, plane * width), BF16)
-    tile_near, tile_far, parts = call(
-        first_product, lengthscale.reshape(feats, 1), cols, near, far,
-        outs=[tile, tile, shaped(BF16, ny, (ny + 2) * probes, width)],
-        limit=24,
-        scratch=[
-            pltpu.VMEM((ny * width, feats + EXTRA), BF16),
-            pltpu.VMEM((feats + EXTRA, plane * width), BF16),
-            pltpu.VMEM((ny, probes, width), F32),
-        ],
+    scratch = [pltpu.VMEM((feats + EXTRA, plane * width), BF16)]
+    tile_near, sums = call(
+        near_product, inverse, cols, near, outs=[tile, shaped(F32, ny, probes, width)], limit=24, scratch=scratch
+    )
+    tile_far, parts = call(
+        far_product, inverse, cols, far, sums, outs=[tile, shaped(BF16, ny, (ny + 2) * probes, width)],
+        limit=24, scratch=scratch,
     )
     parts = exchange(parts, "y")
     image, rows = call(
@@ -223,9 +252,10 @@
     )
     near = exchange(rows, ("x", "z"))
     images, local = call(
-        functools.partial(column_images, factor), parts, right_side, image,
+        functools.partial(column_images, factor), parts, right, image,
         outs=[shaped(F32, ny, probes, width), shaped(F32, 1, width)],
     )
+    near, images, local = lax.optimization_barrier((near, images, local))
     far = lax.ppermute(near, "core", swap)
     sums = call(second_product, held(tile_near), near, outs=shaped(F32, ny, probes, width))
     sums = call(
@@ -234,7 +264,7 @@
     )
     second, local = call(gathered, exchange(sums, "y"), outs=[block, shaped(F32, plane * ncore, width)])
     everyone = exchange(local, ("x", "z", "core"))
-    return call(finish, everyone, right_side, image, second, outs=[block, block])
+    return call(finish, everyone, right, image, second, outs=[block, block])
 
 
 def solution(mesh):

time: 129 us -> 140 us (1.085)
  blocking collectives: 81.5 us -> 64.9 us
  starting transfers between devices: 20.5 us -> 35.3 us
  local copies, waits for them, and re-layouts: 2.85 us -> 13 us
    all_to_all x5 -> x3, blocking collectives: 81.5 us -> 43.5 us  [exchange(): return lax.all_to_all(values, axes, 0, 0, tiled=True)]
    all_gather x0 -> x1, blocking collectives: none -> 21.4 us  [per_device(): cols = lax.all_gather(features, 'y')]
    all_to_all x1 -> x2, starting transfers between devices: 6.83 us -> 23.2 us  [exchange(): return lax.all_to_all(values, axes, 0, 0, tiled=True)]
    unnamed x8 -> x14, local copies, waits for them, and re-layouts: 2.1 us -> 13 us
    ppermute x2, starting transfers between devices: 13.6 us -> 12 us  [per_device(): far = lax.ppermute(near, 'core', swap)]
    all_to_all x1 -> x2, waiting for transfers between devices: 7.77 us -> 9.08 us  [exchange(): return lax.all_to_all(values, axes, 0, 0, tiled=True)]
    pallas_call x8 -> x10, Pallas kernels: 15.4 us -> 16.6 us  [call(): pl.pallas_call(kernel, in_specs=specs or [VMEM] * len(args), out_specs=ja...]
  transfers between devices with their start and end apart: 3 -> 4, of which waited for: 1 -> 1; matrix products, arithmetic and copies ran while one was open for 1% -> 0% of each run, Pallas kernels for 2% -> 5%
where the time goes in v3:
time: 140 us
  blocking collectives  64.9 us (46%)
  starting transfers between devices  35.3 us (25%)
  Pallas kernels  16.6 us (12%)
  local copies, waits for them, and re-layouts  13 us (9%)
  waiting for transfers between devices  9.08 us (6%)
    all_to_all x3, blocking collectives, exchange(): return lax.all_to_all(values, axes, 0, 0, tiled=True)  43.5 us
    all_to_all x2, starting transfers between devices, exchange(): return lax.all_to_all(values, axes, 0, 0, tiled=True)  23.2 us
    all_gather x1, blocking collectives, per_device(): cols = lax.all_gather(features, 'y')  21.4 us
    pallas_call x10, Pallas kernels, call(): pl.pallas_call(kernel, in_specs=specs or [VMEM] * len(args), out_specs=ja...  16.6 us
    unnamed x14, local copies, waits for them, and re-layouts  13 us
    ppermute x2, starting transfers between devices, per_device(): far = lax.ppermute(near, 'core', swap)  12 us
    all_to_all x2, waiting for transfers between devices, exchange(): return lax.all_to_all(values, axes, 0, 0, tiled=True)  9.08 us
  transfers between devices with their start and end apart: 4, of which 1 were waited for; matrix products, arithmetic and copies ran while one was open for 0% of the time, Pallas kernels for 5%

profile of v3, /device:TPU:1, one launch (start us, length us, event | category | flops | bytes accessed | tf_op | source)
XLA Modules:
  0.0 139.6 jit_solution(10570875624499965015)
XLA Ops:
  0.6 0.0 copy-start.4
  0.6 0.7 copy-done.4
  1.4 0.0 copy-start.5
  1.4 0.7 copy-done.5
  2.0 1.0 shard_map.50
  3.0 13.7 %all-to-all-start = ((bf16[32,80,128]{2,1,0:T(8,128)(2,1)}), bf16[32,80,128]{2,1,0:T(8,128)(2,1)S(1)}, u32[]{:S(2)}, u32[]{:S(2)}) async-start(bf16[32,80,128]{2,1,0:T(8,128)(2,1)} %get-tuple-element.22), calls=%async_computation | async-start | bytes 1310720 | tf_op jit(solution)/shard_map/all_to_all | solution.py:221
  16.7 21.4 %all-gather = bf16[512,128]{1,0:T(8,128)(2,1)S(1)} all-gather(bf16[64,128]{1,0:T(8,128)(2,1)} %features_ref.1), channel_id=2, replica_groups=mesh['x'=4,'z'=8,'core'=2,'y'=8] {'y'}, dimensions={0}, use_global_device_ids=true | all-gather | bytes 147456 | tf_op jit(solution)/shard_map/all_gather | solution.py:232
  38.2 0.0 copy-start.6
  38.2 0.7 copy-done.6
  38.8 0.2 shard_map.51
  39.1 0.0 all-to-all-done.rows_ref
  39.1 7.9 %collective-permute-start = (bf16[32,80,128]{2,1,0:T(8,128)(2,1)S(1)}, bf16[32,80,128]{2,1,0:T(8,128)(2,1)S(1)}, u32[]{:S(2)}, u32[]{:S(2)}) collective-permute-start(bf16[32,80,128]{2,1,0:T(8,128)(2,1)S(1)} %all-to-all-done.rows_ref), channel_id=1, source_target_pairs={{0,8},{8,0},{1,9},{9,1},{2,10},{10,2},{3,11},{11,3},{4,12},{12,4},... | collective-permute-start | bytes 1966088 | tf_op jit(solution)/shard_map/ppermute | solution.py:239
  47.0 4.6 %shard_map.52 = (bf16[1024,4096]{1,0:T(8,128)(2,1)S(1)}, f32[8,16,128]{2,1,0:T(8,128)S(1)}) custom-call(f32[64,128]{1,0:T(8,128)S(1)} %get-tuple-element.25.inverse_ref, bf16[1024,80]{1,0:T(8,128)(2,1)S(1)} %get-tuple-element.26.cols_ref, bf16[32,80,128]{2,1,0:T(8,128)(2,1)S(1)} %all-to-all-done.rows_ref), custom_call_target="tpu_custom_call" | custom-call | tf_op jit(solution)/shard_map/pallas_call | solution.py:19
  51.6 0.0 copy-start
  51.6 3.2 %copy-done = bf16[1024,4096]{1,0:T(8,128)(2,1)} copy-done((bf16[1024,4096]{1,0:T(8,128)(2,1)}, bf16[1024,4096]{1,0:T(8,128)(2,1)S(1)}, u32[]{:S(2)}) %copy-start) | copy-done | bytes 8388632
  54.9 0.0 collective-permute-done.rows_ref
  54.9 4.6 %shard_map.53 = (bf16[1024,4096]{1,0:T(8,128)(2,1)S(1)}, bf16[8,160,128]{2,1,0:T(8,128)(2,1)S(1)}) custom-call(f32[64,128]{1,0:T(8,128)S(1)} %get-tuple-element.25.inverse_ref, bf16[1024,80]{1,0:T(8,128)(2,1)S(1)} %get-tuple-element.26.cols_ref, bf16[32,80,128]{2,1,0:T(8,128)(2,1)S(1)} %collective-permute-done.rows_ref, ...), custom_call_target="tpu_custom_call" | custom-call | tf_op jit(solution)/shard_map/pallas_call | solution.py:19
  59.5 0.0 copy-start.2
  59.5 3.2 %copy-done.2 = bf16[1024,4096]{1,0:T(8,128)(2,1)} copy-done((bf16[1024,4096]{1,0:T(8,128)(2,1)}, bf16[1024,4096]{1,0:T(8,128)(2,1)S(1)}, u32[]{:S(2)}) %copy-start.2) | copy-done | bytes 8388632
  62.8 18.8 %all_to_all.31.parts_ref = bf16[8,160,128]{2,1,0:T(8,128)(2,1)S(1)} all-to-all(bf16[8,160,128]{2,1,0:T(8,128)(2,1)S(1)} %get-tuple-element.30), channel_id=1, replica_groups=mesh['x'=4,'z'=8,'core'=2,'y'=8] {'y'}, dimensions={0} | all-to-all | bytes 655360 | tf_op jit(solution)/shard_map/all_to_all | solution.py:221
  81.5 0.7 shard_map.54
  82.2 9.5 %all-to-all-start.2 = ((bf16[32,16,128]{2,1,0:T(8,128)(2,1)}), bf16[32,16,128]{2,1,0:T(8,128)(2,1)S(1)}, u32[]{:S(2)}, u32[]{:S(2)}) async-start(bf16[32,16,128]{2,1,0:T(8,128)(2,1)} %get-tuple-element.31), calls=%async_computation.2 | async-start | bytes 262144 | tf_op jit(solution)/shard_map/all_to_all | solution.py:221
  91.7 0.1 shard_map.55
  91.8 9.1 %all-to-all-done.2.rows_ref = bf16[32,16,128]{2,1,0:T(8,128)(2,1)S(1)} async-done(((bf16[32,16,128]{2,1,0:T(8,128)(2,1)}), bf16[32,16,128]{2,1,0:T(8,128)(2,1)S(1)}, u32[]{:S(2)}, u32[]{:S(2)}) %all-to-all-start.2) | async-done | bytes 131104 | tf_op jit(solution)/shard_map/all_to_all | solution.py:221
  100.9 4.1 %collective-permute-start.1 = (bf16[32,16,128]{2,1,0:T(8,128)(2,1)S(1)}, bf16[32,16,128]{2,1,0:T(8,128)(2,1)S(1)}, u32[]{:S(2)}, u32[]{:S(2)}) collective-permute-start(bf16[32,16,128]{2,1,0:T(8,128)(2,1)S(1)} %all-to-all-done.2.rows_ref), channel_id=1, source_target_pairs={{0,8},{8,0},{1,9},{9,1},{2,10},{10,2},{3,11},{11,3},{4,12},{12,4},... | collective-permute-start | bytes 393224 | tf_op jit(solution)/shard_map/ppermute | solution.py:259
  105.0 0.0 copy-start.1
  105.0 3.4 %copy-done.1 = bf16[1024,4096]{1,0:T(8,128)(2,1)S(1)} copy-done((bf16[1024,4096]{1,0:T(8,128)(2,1)S(1)}, bf16[1024,4096]{1,0:T(8,128)(2,1)}, u32[]{:S(2)}) %copy-start.1) | copy-done | bytes 8388632
  108.4 0.0 copy-start.3
  108.4 2.3 %shard_map.56.start_ref = f32[8,16,128]{2,1,0:T(8,128)S(1)} custom-call(bf16[1024,4096]{1,0:T(8,128)(2,1)S(1)} %copy-done.1, bf16[32,16,128]{2,1,0:T(8,128)(2,1)S(1)} %all-to-all-done.2.rows_ref), custom_call_target="tpu_custom_call" | custom-call | tf_op jit(solution)/shard_map/pallas_call | solution.py:19
  110.7 0.0 collective-permute-done.1.rows_ref
  110.7 1.1 copy-done.3
  111.8 2.4 %shard_map.57 = f32[8,24,128]{2,1,0:T(8,128)S(1)} custom-call(bf16[1024,4096]{1,0:T(8,128)(2,1)S(1)} %copy-done.3, bf16[32,16,128]{2,1,0:T(8,128)(2,1)S(1)} %collective-permute-done.1.rows_ref, f32[8,16,128]{2,1,0:T(8,128)S(1)} %shard_map.56.start_ref, f32[8,16,128]{2,1,0:T(8,128)S(1)} %get-tuple-element.38.images_ref, f32[1,128]{1,0:T(1,128)S(1)} %get-tuple-element.39.local_ref), custom_call_target="tpu_custom_call" | custom-call | tf_op jit(solution)/shard_map/pallas_call | solution.py:19
  114.2 10.5 %all_to_all.32.parts_ref = f32[8,24,128]{2,1,0:T(8,128)S(1)} all-to-all(f32[8,24,128]{2,1,0:T(8,128)S(1)} %shard_map.57), channel_id=1, replica_groups=mesh['x'=4,'z'=8,'core'=2,'y'=8] {'y'}, dimensions={0} | all-to-all | bytes 196608 | tf_op jit(solution)/shard_map/all_to_all | solution.py:221
  124.7 14.2 %all_to_all.33 = f32[64,1,128]{2,1,0:T(1,128)S(1)} all-to-all(f32[64,1,128]{2,1,0:T(1,128)S(1)} %bitcast.8), channel_id=1, replica_groups=mesh['x'=4,'z'=8,'core'=2,'y'=8] {'x','z','core'}, dimensions={0} | all-to-all | bytes 65536 | tf_op jit(solution)/shard_map/all_to_all | solution.py:221
  138.9 0.7 shard_map.59
  (1 shorter events, 0.0 us)
Async XLA Ops:
  0.6 0.7 copy-start.4
  1.4 0.7 copy-start.5
  3.0 36.1 %all-to-all-start = ((bf16[32,80,128]{2,1,0:T(8,128)(2,1)}), bf16[32,80,128]{2,1,0:T(8,128)(2,1)S(1)}, u32[]{:S(2)}, u32[]{:S(2)}) async-start(bf16[32,80,128]{2,1,0:T(8,128)(2,1)} %get-tuple-element.22), calls=%async_computation | async-start | bytes 1310720 | tf_op jit(solution)/shard_map/all_to_all | solution.py:221
  38.2 0.7 copy-start.6
  39.1 15.8 %collective-permute-start = (bf16[32,80,128]{2,1,0:T(8,128)(2,1)S(1)}, bf16[32,80,128]{2,1,0:T(8,128)(2,1)S(1)}, u32[]{:S(2)}, u32[]{:S(2)}) collective-permute-start(bf16[32,80,128]{2,1,0:T(8,128)(2,1)S(1)} %all-to-all-done.rows_ref), channel_id=1, source_target_pairs={{0,8},{8,0},{1,9},{9,1},{2,10},{10,2},{3,11},{11,3},{4,12},{12,4},... | collective-permute-start | bytes 1966088 | tf_op jit(solution)/shard_map/ppermute | solution.py:239
  51.6 3.2 %copy-start = (bf16[1024,4096]{1,0:T(8,128)(2,1)}, bf16[1024,4096]{1,0:T(8,128)(2,1)S(1)}, u32[]{:S(2)}) copy-start(bf16[1024,4096]{1,0:T(8,128)(2,1)S(1)} %get-tuple-element.37.tile_ref) | copy-start | bytes 25165828
  59.5 3.2 %copy-start.2 = (bf16[1024,4096]{1,0:T(8,128)(2,1)}, bf16[1024,4096]{1,0:T(8,128)(2,1)S(1)}, u32[]{:S(2)}) copy-start(bf16[1024,4096]{1,0:T(8,128)(2,1)S(1)} %get-tuple-element.29.tile_ref) | copy-start | bytes 25165828
  82.2 18.7 %all-to-all-start.2 = ((bf16[32,16,128]{2,1,0:T(8,128)(2,1)}), bf16[32,16,128]{2,1,0:T(8,128)(2,1)S(1)}, u32[]{:S(2)}, u32[]{:S(2)}) async-start(bf16[32,16,128]{2,1,0:T(8,128)(2,1)} %get-tuple-element.31), calls=%async_computation.2 | async-start | bytes 262144 | tf_op jit(solution)/shard_map/all_to_all | solution.py:221
  100.9 9.8 %collective-permute-start.1 = (bf16[32,16,128]{2,1,0:T(8,128)(2,1)S(1)}, bf16[32,16,128]{2,1,0:T(8,128)(2,1)S(1)}, u32[]{:S(2)}, u32[]{:S(2)}) collective-permute-start(bf16[32,16,128]{2,1,0:T(8,128)(2,1)S(1)} %all-to-all-done.2.rows_ref), channel_id=1, source_target_pairs={{0,8},{8,0},{1,9},{9,1},{2,10},{10,2},{3,11},{11,3},{4,12},{12,4},... | collective-permute-start | bytes 393224 | tf_op jit(solution)/shard_map/ppermute | solution.py:259
  105.0 3.4 %copy-start.1 = (bf16[1024,4096]{1,0:T(8,128)(2,1)S(1)}, bf16[1024,4096]{1,0:T(8,128)(2,1)}, u32[]{:S(2)}) copy-start(bf16[1024,4096]{1,0:T(8,128)(2,1)} %copy-done) | copy-start | bytes 25165828
  108.4 3.4 %copy-start.3 = (bf16[1024,4096]{1,0:T(8,128)(2,1)S(1)}, bf16[1024,4096]{1,0:T(8,128)(2,1)}, u32[]{:S(2)}) copy-start(bf16[1024,4096]{1,0:T(8,128)(2,1)} %copy-done.2) | copy-start | bytes 25165828

commit v4 on v3

--- a/solution.py
+++ b/solution.py
@@ -224,8 +224,8 @@
         return pltpu.with_memory_space_constraint(array, pltpu.VMEM)
 
     rows, right = call(
-        copies, features, right_side, specs=[pl.BlockSpec(memory_space=pltpu.HBM)] * 2,
-        outs=[shaped(BF16, plane, feats + probes, width), pltpu.VMEM(block.shape, F32)],
+        copies, *[pltpu.with_memory_space_constraint(array, pltpu.HBM) for array in (features, right_side)], specs=[pl.BlockSpec(memory_space=pltpu.HBM)] * 2,
+        outs=[pltpu.VMEM((plane, feats + probes, width), BF16), pltpu.VMEM(block.shape, F32)],
         scratch=[pltpu.VMEM(features.shape, BF16), pltpu.SemaphoreType.DMA((2,))],
     )
     right = held(right)
@@ -255,7 +255,6 @@
         functools.partial(column_images, factor), parts, right, image,
         outs=[shaped(F32, ny, probes, width), shaped(F32, 1, width)],
     )
-    near, images, local = lax.optimization_barrier((near, images, local))
     far = lax.ppermute(near, "core", swap)
     sums = call(second_product, held(tile_near), near, outs=shaped(F32, ny, probes, width))
     sums = call(

time: 140 us -> 128 us (0.914)
  blocking collectives: 64.9 us -> 83.4 us
  local copies, waits for them, and re-layouts: 13 us -> 0.66 us
  starting transfers between devices: 35.3 us -> 25.7 us
  waiting for transfers between devices: 9.08 us -> 0.01 us
    all_to_all x3 -> x4, blocking collectives: 43.5 us -> 62 us  [exchange(): return lax.all_to_all(values, axes, 0, 0, tiled=True)]
    unnamed x14 -> x2, local copies, waits for them, and re-layouts: 13 us -> 0.66 us
    all_to_all x2 -> x1, starting transfers between devices: 23.2 us -> 13.7 us  [exchange(): return lax.all_to_all(values, axes, 0, 0, tiled=True)]
    all_to_all x2 -> x1, waiting for transfers between devices: 9.08 us -> 0.01 us  [exchange(): return lax.all_to_all(values, axes, 0, 0, tiled=True)]
  transfers between devices with their start and end apart: 4 -> 3, of which waited for: 1 -> 0; matrix products, arithmetic and copies ran while one was open for 0% -> 0% of each run, Pallas kernels for 5% -> 6%
where the time goes in v4:
time: 128 us; the launch traced here: 127 us
  blocking collectives  83.4 us (65%)
  starting transfers between devices  25.7 us (20%)
  Pallas kernels  16.7 us (13%)
    all_to_all x4, blocking collectives, exchange(): return lax.all_to_all(values, axes, 0, 0, tiled=True)  62 us
    all_gather x1, blocking collectives, per_device(): cols = lax.all_gather(features, 'y')  21.4 us
    pallas_call x10, Pallas kernels, call(): pl.pallas_call(kernel, in_specs=specs or [VMEM] * len(args), out_specs=ja...  16.7 us
    all_to_all x1, starting transfers between devices, exchange(): return lax.all_to_all(values, axes, 0, 0, tiled=True)  13.7 us
    ppermute x2, starting transfers between devices, per_device(): far = lax.ppermute(near, 'core', swap)  12 us
  transfers between devices with their start and end apart: 3, of which 0 were waited for; matrix products, arithmetic and copies ran while one was open for 0% of the time, Pallas kernels for 6%

profile of v4, /device:TPU:1, one launch (start us, length us, event | category | flops | bytes accessed | tf_op | source)
XLA Modules:
  0.0 127.2 jit_solution(13615572149355430805)
XLA Ops:
  0.6 1.7 %shard_map.50 = (bf16[32,80,128]{2,1,0:T(8,128)(2,1)}, f32[16,128]{1,0:T(8,128)S(1)}) custom-call(bf16[64,128]{1,0:T(8,128)(2,1)} %features_ref.1, f32[16,128]{1,0:T(8,128)} %right_ref.1), custom_call_target="tpu_custom_call" | custom-call | tf_op jit(solution)/shard_map/pallas_call | solution.py:19
  2.3 13.7 %all-to-all-start = ((bf16[32,80,128]{2,1,0:T(8,128)(2,1)}), bf16[32,80,128]{2,1,0:T(8,128)(2,1)S(1)}, u32[]{:S(2)}, u32[]{:S(2)}) async-start(bf16[32,80,128]{2,1,0:T(8,128)(2,1)} %get-tuple-element.19), calls=%async_computation | async-start | bytes 1310720 | tf_op jit(solution)/shard_map/all_to_all | solution.py:221
  16.0 21.4 %all-gather = bf16[512,128]{1,0:T(8,128)(2,1)S(1)} all-gather(bf16[64,128]{1,0:T(8,128)(2,1)} %features_ref.1), channel_id=2, replica_groups=mesh['x'=4,'z'=8,'core'=2,'y'=8] {'y'}, dimensions={0}, use_global_device_ids=true | all-gather | bytes 147456 | tf_op jit(solution)/shard_map/all_gather | solution.py:232
  37.4 0.0 copy-start
  37.4 0.7 copy-done
  38.1 0.2 shard_map.51
  38.3 0.0 all-to-all-done.rows_ref
  38.3 7.9 %collective-permute-start = (bf16[32,80,128]{2,1,0:T(8,128)(2,1)S(1)}, bf16[32,80,128]{2,1,0:T(8,128)(2,1)S(1)}, u32[]{:S(2)}, u32[]{:S(2)}) collective-permute-start(bf16[32,80,128]{2,1,0:T(8,128)(2,1)S(1)} %all-to-all-done.rows_ref), channel_id=1, source_target_pairs={{0,8},{8,0},{1,9},{9,1},{2,10},{10,2},{3,11},{11,3},{4,12},{12,4},... | collective-permute-start | bytes 1966088 | tf_op jit(solution)/shard_map/ppermute | solution.py:239
  46.3 4.6 %shard_map.52 = (bf16[1024,4096]{1,0:T(8,128)(2,1)S(1)}, f32[8,16,128]{2,1,0:T(8,128)S(1)}) custom-call(f32[64,128]{1,0:T(8,128)S(1)} %get-tuple-element.22.inverse_ref, bf16[1024,80]{1,0:T(8,128)(2,1)S(1)} %get-tuple-element.23.cols_ref, bf16[32,80,128]{2,1,0:T(8,128)(2,1)S(1)} %all-to-all-done.rows_ref), custom_call_target="tpu_custom_call" | custom-call | tf_op jit(solution)/shard_map/pallas_call | solution.py:19
  50.9 0.0 collective-permute-done.rows_ref
  50.9 4.7 %shard_map.53 = (bf16[1024,4096]{1,0:T(8,128)(2,1)S(1)}, bf16[8,160,128]{2,1,0:T(8,128)(2,1)S(1)}) custom-call(f32[64,128]{1,0:T(8,128)S(1)} %get-tuple-element.22.inverse_ref, bf16[1024,80]{1,0:T(8,128)(2,1)S(1)} %get-tuple-element.23.cols_ref, bf16[32,80,128]{2,1,0:T(8,128)(2,1)S(1)} %collective-permute-done.rows_ref, ...), custom_call_target="tpu_custom_call" | custom-call | tf_op jit(solution)/shard_map/pallas_call | solution.py:19
  55.6 18.8 %all_to_all.31.parts_ref = bf16[8,160,128]{2,1,0:T(8,128)(2,1)S(1)} all-to-all(bf16[8,160,128]{2,1,0:T(8,128)(2,1)S(1)} %get-tuple-element.27), channel_id=1, replica_groups=mesh['x'=4,'z'=8,'core'=2,'y'=8] {'y'}, dimensions={0} | all-to-all | bytes 655360 | tf_op jit(solution)/shard_map/all_to_all | solution.py:221
  74.4 18.5 %all_to_all.32.rows_ref = bf16[32,16,128]{2,1,0:T(8,128)(2,1)S(1)} all-to-all(bf16[32,16,128]{2,1,0:T(8,128)(2,1)S(1)} %get-tuple-element.28), channel_id=1, replica_groups=mesh['x'=4,'z'=8,'core'=2,'y'=8] {'x','z'}, dimensions={0} | all-to-all | bytes 262144 | tf_op jit(solution)/shard_map/all_to_all | solution.py:221
  92.9 4.1 %collective-permute-start.1 = (bf16[32,16,128]{2,1,0:T(8,128)(2,1)S(1)}, bf16[32,16,128]{2,1,0:T(8,128)(2,1)S(1)}, u32[]{:S(2)}, u32[]{:S(2)}) collective-permute-start(bf16[32,16,128]{2,1,0:T(8,128)(2,1)S(1)} %all_to_all.32.rows_ref), channel_id=1, source_target_pairs={{0,8},{8,0},{1,9},{9,1},{2,10},{10,2},{3,11},{11,3},{4,12},{12,4},... | collective-permute-start | bytes 393224 | tf_op jit(solution)/shard_map/ppermute | solution.py:258
  97.0 0.1 shard_map.56
  97.1 2.3 %shard_map.55.start_ref = f32[8,16,128]{2,1,0:T(8,128)S(1)} custom-call(bf16[1024,4096]{1,0:T(8,128)(2,1)S(1)} %get-tuple-element.29.tile_ref, bf16[32,16,128]{2,1,0:T(8,128)(2,1)S(1)} %all_to_all.32.rows_ref), custom_call_target="tpu_custom_call" | custom-call | tf_op jit(solution)/shard_map/pallas_call | solution.py:19
  99.3 0.0 collective-permute-done.1.rows_ref
  99.3 2.4 %shard_map.57 = f32[8,24,128]{2,1,0:T(8,128)S(1)} custom-call(bf16[1024,4096]{1,0:T(8,128)(2,1)S(1)} %get-tuple-element.26.tile_ref, bf16[32,16,128]{2,1,0:T(8,128)(2,1)S(1)} %collective-permute-done.1.rows_ref, f32[8,16,128]{2,1,0:T(8,128)S(1)} %shard_map.55.start_ref, f32[8,16,128]{2,1,0:T(8,128)S(1)} %get-tuple-element.32.images_ref, ...), custom_call_target="tpu_custom_call" | custom-call | tf_op jit(solution)/shard_map/pallas_call | solution.py:19
  101.7 10.5 %all_to_all.33.parts_ref = f32[8,24,128]{2,1,0:T(8,128)S(1)} all-to-all(f32[8,24,128]{2,1,0:T(8,128)S(1)} %shard_map.57), channel_id=1, replica_groups=mesh['x'=4,'z'=8,'core'=2,'y'=8] {'y'}, dimensions={0} | all-to-all | bytes 196608 | tf_op jit(solution)/shard_map/all_to_all | solution.py:221
  112.2 14.2 %all_to_all.34 = f32[64,1,128]{2,1,0:T(1,128)S(1)} all-to-all(f32[64,1,128]{2,1,0:T(1,128)S(1)} %bitcast.8), channel_id=1, replica_groups=mesh['x'=4,'z'=8,'core'=2,'y'=8] {'x','z','core'}, dimensions={0} | all-to-all | bytes 65536 | tf_op jit(solution)/shard_map/all_to_all | solution.py:221
  126.5 0.7 shard_map.59
  (2 shorter events, 0.0 us)
Async XLA Ops:
  2.3 36.0 %all-to-all-start = ((bf16[32,80,128]{2,1,0:T(8,128)(2,1)}), bf16[32,80,128]{2,1,0:T(8,128)(2,1)S(1)}, u32[]{:S(2)}, u32[]{:S(2)}) async-start(bf16[32,80,128]{2,1,0:T(8,128)(2,1)} %get-tuple-element.19), calls=%async_computation | async-start | bytes 1310720 | tf_op jit(solution)/shard_map/all_to_all | solution.py:221
  37.4 0.7 copy-start
  38.3 12.5 %collective-permute-start = (bf16[32,80,128]{2,1,0:T(8,128)(2,1)S(1)}, bf16[32,80,128]{2,1,0:T(8,128)(2,1)S(1)}, u32[]{:S(2)}, u32[]{:S(2)}) collective-permute-start(bf16[32,80,128]{2,1,0:T(8,128)(2,1)S(1)} %all-to-all-done.rows_ref), channel_id=1, source_target_pairs={{0,8},{8,0},{1,9},{9,1},{2,10},{10,2},{3,11},{11,3},{4,12},{12,4},... | collective-permute-start | bytes 1966088 | tf_op jit(solution)/shard_map/ppermute | solution.py:239
  92.9 6.5 %collective-permute-start.1 = (bf16[32,16,128]{2,1,0:T(8,128)(2,1)S(1)}, bf16[32,16,128]{2,1,0:T(8,128)(2,1)S(1)}, u32[]{:S(2)}, u32[]{:S(2)}) collective-permute-start(bf16[32,16,128]{2,1,0:T(8,128)(2,1)S(1)} %all_to_all.32.rows_ref), channel_id=1, source_target_pairs={{0,8},{8,0},{1,9},{9,1},{2,10},{10,2},{3,11},{11,3},{4,12},{12,4},... | collective-permute-start | bytes 393224 | tf_op jit(solution)/shard_map/ppermute | solution.py:258

commit v5 on v4

--- a/solution.py
+++ b/solution.py
@@ -48,7 +48,7 @@
     return jnp.concatenate([scaled, below.astype(BF16)], axis=0)
 
 
-def copies(features_ref, right_ref, rows_ref, kept_ref, held, sems):
+def copies(features_ref, right_ref, cols_ref, rows_ref, kept_ref, held, sems):
     moves = [
         pltpu.make_async_copy(features_ref, held, sems.at[0]),
         pltpu.make_async_copy(right_ref, kept_ref, sems.at[1]),
@@ -59,6 +59,8 @@
         move.wait()
     features, right = held[...], kept_ref[...].astype(BF16)
     feats = features.shape[0]
+    for index in range(cols_ref.shape[0]):
+        cols_ref[index] = features
     for index in range(rows_ref.shape[0]):
         rows_ref[index, :feats, :] = features
         rows_ref[index, feats:, :] = right
@@ -223,13 +225,14 @@
     def held(array):
         return pltpu.with_memory_space_constraint(array, pltpu.VMEM)
 
-    rows, right = call(
+    cols, rows, right = call(
         copies, *[pltpu.with_memory_space_constraint(array, pltpu.HBM) for array in (features, right_side)], specs=[pl.BlockSpec(memory_space=pltpu.HBM)] * 2,
-        outs=[pltpu.VMEM((plane, feats + probes, width), BF16), pltpu.VMEM(block.shape, F32)],
+        outs=[shaped(BF16, ny, feats, width), pltpu.VMEM((plane, feats + probes, width), BF16), pltpu.VMEM(block.shape, F32)],
         scratch=[pltpu.VMEM(features.shape, BF16), pltpu.SemaphoreType.DMA((2,))],
     )
     right = held(right)
-    cols = lax.all_gather(features, "y")
+    cols = exchange(cols, "y")
+    rows, cols = lax.optimization_barrier((rows, cols))
     near = exchange(rows, ("x", "z"))
     inverse, cols = call(
         columns, lengthscale.reshape(1, feats), cols,

time: 128 us -> 128 us (level)
  waiting for transfers between devices: 0.01 us -> 13.8 us
  blocking collectives: 83.4 us -> 70.3 us
    all_gather x1 -> x0, blocking collectives: 21.4 us -> none  [per_device(): cols = lax.all_gather(features, 'y')]
    all_to_all x1, waiting for transfers between devices: 0.01 us -> 13.8 us  [exchange(): return lax.all_to_all(values, axes, 0, 0, tiled=True)]
    all_to_all x4 -> x5, blocking collectives: 62 us -> 70.3 us  [exchange(): return lax.all_to_all(values, axes, 0, 0, tiled=True)]
  transfers between devices with their start and end apart: 3 -> 3, of which waited for: 0 -> 1; matrix products, arithmetic and copies ran while one was open for 0% -> 0% of each run, Pallas kernels for 6% -> 6%
where the time goes in v5:
time: 128 us; the launch traced here: 127 us
  blocking collectives  70.3 us (55%)
  starting transfers between devices  25 us (20%)
  Pallas kernels  16.7 us (13%)
  waiting for transfers between devices  13.8 us (11%)
    all_to_all x5, blocking collectives, exchange(): return lax.all_to_all(values, axes, 0, 0, tiled=True)  70.3 us
    pallas_call x10, Pallas kernels, call(): pl.pallas_call(kernel, in_specs=specs or [VMEM] * len(args), out_specs=ja...  16.7 us
    all_to_all x1, waiting for transfers between devices, exchange(): return lax.all_to_all(values, axes, 0, 0, tiled=True)  13.8 us
    all_to_all x1, starting transfers between devices, exchange(): return lax.all_to_all(values, axes, 0, 0, tiled=True)  12.7 us
    ppermute x2, starting transfers between devices, per_device(): far = lax.ppermute(near, 'core', swap)  12.2 us
  transfers between devices with their start and end apart: 3, of which 1 were waited for; matrix products, arithmetic and copies ran while one was open for 0% of the time, Pallas kernels for 6%

profile of v5, /device:TPU:1, one launch (start us, length us, event | category | flops | bytes accessed | tf_op | source)
XLA Modules:
  0.0 127.1 jit_solution(9985186897509894940)
XLA Ops:
  0.6 1.7 %shard_map.50 = (bf16[8,64,128]{2,1,0:T(8,128)(2,1)S(1)}, bf16[32,80,128]{2,1,0:T(8,128)(2,1)}, f32[16,128]{1,0:T(8,128)S(1)}) custom-call(bf16[64,128]{1,0:T(8,128)(2,1)} %features_ref.1, f32[16,128]{1,0:T(8,128)} %right_ref.1), custom_call_target="tpu_custom_call" | custom-call | tf_op jit(solution)/shard_map/pallas_call | solution.py:19
  2.3 15.4 %all_to_all.36.cols_ref = bf16[8,64,128]{2,1,0:T(8,128)(2,1)S(1)} all-to-all(bf16[8,64,128]{2,1,0:T(8,128)(2,1)S(1)} %get-tuple-element.23), channel_id=1, replica_groups=mesh['x'=4,'z'=8,'core'=2,'y'=8] {'y'}, dimensions={0} | all-to-all | bytes 262144 | tf_op jit(solution)/shard_map/all_to_all | solution.py:223
  17.7 12.7 %all-to-all-start.1 = ((bf16[32,80,128]{2,1,0:T(8,128)(2,1)}), bf16[32,80,128]{2,1,0:T(8,128)(2,1)S(1)}, u32[]{:S(2)}, u32[]{:S(2)}) async-start(bf16[32,80,128]{2,1,0:T(8,128)(2,1)} %get-tuple-element.24), calls=%async_computation.1 | async-start | bytes 1310720 | tf_op jit(solution)/shard_map/all_to_all | solution.py:223
  30.4 0.0 copy-start
  30.4 0.6 copy-done
  31.1 0.2 shard_map.51
  31.3 13.8 %all-to-all-done.1.rows_ref = bf16[32,80,128]{2,1,0:T(8,128)(2,1)S(1)} async-done(((bf16[32,80,128]{2,1,0:T(8,128)(2,1)}), bf16[32,80,128]{2,1,0:T(8,128)(2,1)S(1)}, u32[]{:S(2)}, u32[]{:S(2)}) %all-to-all-start.1) | async-done | bytes 655392 | tf_op jit(solution)/shard_map/all_to_all | solution.py:223
  45.1 8.1 %collective-permute-start = (bf16[32,80,128]{2,1,0:T(8,128)(2,1)S(1)}, bf16[32,80,128]{2,1,0:T(8,128)(2,1)S(1)}, u32[]{:S(2)}, u32[]{:S(2)}) collective-permute-start(bf16[32,80,128]{2,1,0:T(8,128)(2,1)S(1)} %all-to-all-done.1.rows_ref), channel_id=1, source_target_pairs={{0,8},{8,0},{1,9},{9,1},{2,10},{10,2},{3,11},{11,3},{4,12},{12,4},... | collective-permute-start | bytes 1966088 | tf_op jit(solution)/shard_map/ppermute | solution.py:242
  53.2 4.6 %shard_map.52 = (bf16[1024,4096]{1,0:T(8,128)(2,1)S(1)}, f32[8,16,128]{2,1,0:T(8,128)S(1)}) custom-call(f32[64,128]{1,0:T(8,128)S(1)} %get-tuple-element.28.inverse_ref, bf16[1024,80]{1,0:T(8,128)(2,1)S(1)} %get-tuple-element.29.cols_ref, bf16[32,80,128]{2,1,0:T(8,128)(2,1)S(1)} %all-to-all-done.1.rows_ref), custom_call_target="tpu_custom_call" | custom-call | tf_op jit(solution)/shard_map/pallas_call | solution.py:19
  57.9 0.0 collective-permute-done.rows_ref
  57.9 4.7 %shard_map.53 = (bf16[1024,4096]{1,0:T(8,128)(2,1)S(1)}, bf16[8,160,128]{2,1,0:T(8,128)(2,1)S(1)}) custom-call(f32[64,128]{1,0:T(8,128)S(1)} %get-tuple-element.28.inverse_ref, bf16[1024,80]{1,0:T(8,128)(2,1)S(1)} %get-tuple-element.29.cols_ref, bf16[32,80,128]{2,1,0:T(8,128)(2,1)S(1)} %collective-permute-done.rows_ref, ...), custom_call_target="tpu_custom_call" | custom-call | tf_op jit(solution)/shard_map/pallas_call | solution.py:19
  62.5 16.4 %all_to_all.37.parts_ref = bf16[8,160,128]{2,1,0:T(8,128)(2,1)S(1)} all-to-all(bf16[8,160,128]{2,1,0:T(8,128)(2,1)S(1)} %get-tuple-element.33), channel_id=1, replica_groups=mesh['x'=4,'z'=8,'core'=2,'y'=8] {'y'}, dimensions={0} | all-to-all | bytes 655360 | tf_op jit(solution)/shard_map/all_to_all | solution.py:223
  79.0 13.8 %all_to_all.38.rows_ref = bf16[32,16,128]{2,1,0:T(8,128)(2,1)S(1)} all-to-all(bf16[32,16,128]{2,1,0:T(8,128)(2,1)S(1)} %get-tuple-element.34), channel_id=1, replica_groups=mesh['x'=4,'z'=8,'core'=2,'y'=8] {'x','z'}, dimensions={0} | all-to-all | bytes 262144 | tf_op jit(solution)/shard_map/all_to_all | solution.py:223
  92.8 4.1 %collective-permute-start.1 = (bf16[32,16,128]{2,1,0:T(8,128)(2,1)S(1)}, bf16[32,16,128]{2,1,0:T(8,128)(2,1)S(1)}, u32[]{:S(2)}, u32[]{:S(2)}) collective-permute-start(bf16[32,16,128]{2,1,0:T(8,128)(2,1)S(1)} %all_to_all.38.rows_ref), channel_id=1, source_target_pairs={{0,8},{8,0},{1,9},{9,1},{2,10},{10,2},{3,11},{11,3},{4,12},{12,4},... | collective-permute-start | bytes 393224 | tf_op jit(solution)/shard_map/ppermute | solution.py:261
  96.9 0.1 shard_map.56
  97.0 2.3 %shard_map.55.start_ref = f32[8,16,128]{2,1,0:T(8,128)S(1)} custom-call(bf16[1024,4096]{1,0:T(8,128)(2,1)S(1)} %get-tuple-element.35.tile_ref, bf16[32,16,128]{2,1,0:T(8,128)(2,1)S(1)} %all_to_all.38.rows_ref), custom_call_target="tpu_custom_call" | custom-call | tf_op jit(solution)/shard_map/pallas_call | solution.py:19
  99.3 0.0 collective-permute-done.1.rows_ref
  99.3 2.4 %shard_map.57 = f32[8,24,128]{2,1,0:T(8,128)S(1)} custom-call(bf16[1024,4096]{1,0:T(8,128)(2,1)S(1)} %get-tuple-element.32.tile_ref, bf16[32,16,128]{2,1,0:T(8,128)(2,1)S(1)} %collective-permute-done.1.rows_ref, f32[8,16,128]{2,1,0:T(8,128)S(1)} %shard_map.55.start_ref, f32[8,16,128]{2,1,0:T(8,128)S(1)} %get-tuple-element.38.images_ref, ...), custom_call_target="tpu_custom_call" | custom-call | tf_op jit(solution)/shard_map/pallas_call | solution.py:19
  101.6 10.5 %all_to_all.39.parts_ref = f32[8,24,128]{2,1,0:T(8,128)S(1)} all-to-all(f32[8,24,128]{2,1,0:T(8,128)S(1)} %shard_map.57), channel_id=1, replica_groups=mesh['x'=4,'z'=8,'core'=2,'y'=8] {'y'}, dimensions={0} | all-to-all | bytes 196608 | tf_op jit(solution)/shard_map/all_to_all | solution.py:223
  112.1 14.2 %all_to_all.40 = f32[64,1,128]{2,1,0:T(1,128)S(1)} all-to-all(f32[64,1,128]{2,1,0:T(1,128)S(1)} %bitcast.6), channel_id=1, replica_groups=mesh['x'=4,'z'=8,'core'=2,'y'=8] {'x','z','core'}, dimensions={0} | all-to-all | bytes 65536 | tf_op jit(solution)/shard_map/all_to_all | solution.py:223
  126.4 0.7 shard_map.59
  (2 shorter events, 0.0 us)
Async XLA Ops:
  17.7 27.4 %all-to-all-start.1 = ((bf16[32,80,128]{2,1,0:T(8,128)(2,1)}), bf16[32,80,128]{2,1,0:T(8,128)(2,1)S(1)}, u32[]{:S(2)}, u32[]{:S(2)}) async-start(bf16[32,80,128]{2,1,0:T(8,128)(2,1)} %get-tuple-element.24), calls=%async_computation.1 | async-start | bytes 1310720 | tf_op jit(solution)/shard_map/all_to_all | solution.py:223
  30.4 0.7 copy-start
  45.1 12.7 %collective-permute-start = (bf16[32,80,128]{2,1,0:T(8,128)(2,1)S(1)}, bf16[32,80,128]{2,1,0:T(8,128)(2,1)S(1)}, u32[]{:S(2)}, u32[]{:S(2)}) collective-permute-start(bf16[32,80,128]{2,1,0:T(8,128)(2,1)S(1)} %all-to-all-done.1.rows_ref), channel_id=1, source_target_pairs={{0,8},{8,0},{1,9},{9,1},{2,10},{10,2},{3,11},{11,3},{4,12},{12,4},... | collective-permute-start | bytes 1966088 | tf_op jit(solution)/shard_map/ppermute | solution.py:242
  92.8 6.5 %collective-permute-start.1 = (bf16[32,16,128]{2,1,0:T(8,128)(2,1)S(1)}, bf16[32,16,128]{2,1,0:T(8,128)(2,1)S(1)}, u32[]{:S(2)}, u32[]{:S(2)}) collective-permute-start(bf16[32,16,128]{2,1,0:T(8,128)(2,1)S(1)} %all_to_all.38.rows_ref), channel_id=1, source_target_pairs={{0,8},{8,0},{1,9},{9,1},{2,10},{10,2},{3,11},{11,3},{4,12},{12,4},... | collective-permute-start | bytes 393224 | tf_op jit(solution)/shard_map/ppermute | solution.py:261

commit v6 on v5

--- a/solution.py
+++ b/solution.py
@@ -10,7 +10,7 @@
 F32, BF16 = jnp.float32, jnp.bfloat16
 EXTRA = 16
 PAD = 8
-CHUNK = 256
+CHUNK = 1024
 AXES = ("x", "z", "core", "y")
 VMEM = pl.BlockSpec(memory_space=pltpu.VMEM)
 

time: 128 us -> 128 us (level)
  no operation moved by 1% of the time
where the time goes in v6:
time: 128 us; the launch traced here: 127 us
  blocking collectives  70.3 us (55%)
  starting transfers between devices  25 us (20%)
  Pallas kernels  16.6 us (13%)
  waiting for transfers between devices  13.8 us (11%)
    all_to_all x5, blocking collectives, exchange(): return lax.all_to_all(values, axes, 0, 0, tiled=True)  70.3 us
    pallas_call x10, Pallas kernels, call(): pl.pallas_call(kernel, in_specs=specs or [VMEM] * len(args), out_specs=ja...  16.6 us
    all_to_all x1, waiting for transfers between devices, exchange(): return lax.all_to_all(values, axes, 0, 0, tiled=True)  13.8 us
    all_to_all x1, starting transfers between devices, exchange(): return lax.all_to_all(values, axes, 0, 0, tiled=True)  12.7 us
    ppermute x2, starting transfers between devices, per_device(): far = lax.ppermute(near, 'core', swap)  12.2 us
  transfers between devices with their start and end apart: 3, of which 1 were waited for; matrix products, arithmetic and copies ran while one was open for 0% of the time, Pallas kernels for 6%

profile of v6, /device:TPU:1, one launch (start us, length us, event | category | flops | bytes accessed | tf_op | source)
XLA Modules:
  0.0 127.0 jit_solution(7364318130384847860)
XLA Ops:
  0.6 1.7 %shard_map.50 = (bf16[8,64,128]{2,1,0:T(8,128)(2,1)S(1)}, bf16[32,80,128]{2,1,0:T(8,128)(2,1)}, f32[16,128]{1,0:T(8,128)S(1)}) custom-call(bf16[64,128]{1,0:T(8,128)(2,1)} %features_ref.1, f32[16,128]{1,0:T(8,128)} %right_ref.1), custom_call_target="tpu_custom_call" | custom-call | tf_op jit(solution)/shard_map/pallas_call | solution.py:19
  2.3 15.4 %all_to_all.36.cols_ref = bf16[8,64,128]{2,1,0:T(8,128)(2,1)S(1)} all-to-all(bf16[8,64,128]{2,1,0:T(8,128)(2,1)S(1)} %get-tuple-element.23), channel_id=1, replica_groups=mesh['x'=4,'z'=8,'core'=2,'y'=8] {'y'}, dimensions={0} | all-to-all | bytes 262144 | tf_op jit(solution)/shard_map/all_to_all | solution.py:223
  17.7 12.7 %all-to-all-start.1 = ((bf16[32,80,128]{2,1,0:T(8,128)(2,1)}), bf16[32,80,128]{2,1,0:T(8,128)(2,1)S(1)}, u32[]{:S(2)}, u32[]{:S(2)}) async-start(bf16[32,80,128]{2,1,0:T(8,128)(2,1)} %get-tuple-element.24), calls=%async_computation.1 | async-start | bytes 1310720 | tf_op jit(solution)/shard_map/all_to_all | solution.py:223
  30.4 0.0 copy-start
  30.4 0.6 copy-done
  31.1 0.2 shard_map.51
  31.3 13.8 %all-to-all-done.1.rows_ref = bf16[32,80,128]{2,1,0:T(8,128)(2,1)S(1)} async-done(((bf16[32,80,128]{2,1,0:T(8,128)(2,1)}), bf16[32,80,128]{2,1,0:T(8,128)(2,1)S(1)}, u32[]{:S(2)}, u32[]{:S(2)}) %all-to-all-start.1) | async-done | bytes 655392 | tf_op jit(solution)/shard_map/all_to_all | solution.py:223
  45.1 8.1 %collective-permute-start = (bf16[32,80,128]{2,1,0:T(8,128)(2,1)S(1)}, bf16[32,80,128]{2,1,0:T(8,128)(2,1)S(1)}, u32[]{:S(2)}, u32[]{:S(2)}) collective-permute-start(bf16[32,80,128]{2,1,0:T(8,128)(2,1)S(1)} %all-to-all-done.1.rows_ref), channel_id=1, source_target_pairs={{0,8},{8,0},{1,9},{9,1},{2,10},{10,2},{3,11},{11,3},{4,12},{12,4},... | collective-permute-start | bytes 1966088 | tf_op jit(solution)/shard_map/ppermute | solution.py:242
  53.2 4.6 %shard_map.52 = (bf16[1024,4096]{1,0:T(8,128)(2,1)S(1)}, f32[8,16,128]{2,1,0:T(8,128)S(1)}) custom-call(f32[64,128]{1,0:T(8,128)S(1)} %get-tuple-element.28.inverse_ref, bf16[1024,80]{1,0:T(8,128)(2,1)S(1)} %get-tuple-element.29.cols_ref, bf16[32,80,128]{2,1,0:T(8,128)(2,1)S(1)} %all-to-all-done.1.rows_ref), custom_call_target="tpu_custom_call" | custom-call | tf_op jit(solution)/shard_map/pallas_call | solution.py:19
  57.8 0.0 collective-permute-done.rows_ref
  57.8 4.6 %shard_map.53 = (bf16[1024,4096]{1,0:T(8,128)(2,1)S(1)}, bf16[8,160,128]{2,1,0:T(8,128)(2,1)S(1)}) custom-call(f32[64,128]{1,0:T(8,128)S(1)} %get-tuple-element.28.inverse_ref, bf16[1024,80]{1,0:T(8,128)(2,1)S(1)} %get-tuple-element.29.cols_ref, bf16[32,80,128]{2,1,0:T(8,128)(2,1)S(1)} %collective-permute-done.rows_ref, ...), custom_call_target="tpu_custom_call" | custom-call | tf_op jit(solution)/shard_map/pallas_call | solution.py:19
  62.4 16.4 %all_to_all.37.parts_ref = bf16[8,160,128]{2,1,0:T(8,128)(2,1)S(1)} all-to-all(bf16[8,160,128]{2,1,0:T(8,128)(2,1)S(1)} %get-tuple-element.33), channel_id=1, replica_groups=mesh['x'=4,'z'=8,'core'=2,'y'=8] {'y'}, dimensions={0} | all-to-all | bytes 655360 | tf_op jit(solution)/shard_map/all_to_all | solution.py:223
  78.9 13.8 %all_to_all.38.rows_ref = bf16[32,16,128]{2,1,0:T(8,128)(2,1)S(1)} all-to-all(bf16[32,16,128]{2,1,0:T(8,128)(2,1)S(1)} %get-tuple-element.34), channel_id=1, replica_groups=mesh['x'=4,'z'=8,'core'=2,'y'=8] {'x','z'}, dimensions={0} | all-to-all | bytes 262144 | tf_op jit(solution)/shard_map/all_to_all | solution.py:223
  92.7 4.1 %collective-permute-start.1 = (bf16[32,16,128]{2,1,0:T(8,128)(2,1)S(1)}, bf16[32,16,128]{2,1,0:T(8,128)(2,1)S(1)}, u32[]{:S(2)}, u32[]{:S(2)}) collective-permute-start(bf16[32,16,128]{2,1,0:T(8,128)(2,1)S(1)} %all_to_all.38.rows_ref), channel_id=1, source_target_pairs={{0,8},{8,0},{1,9},{9,1},{2,10},{10,2},{3,11},{11,3},{4,12},{12,4},... | collective-permute-start | bytes 393224 | tf_op jit(solution)/shard_map/ppermute | solution.py:261
  96.8 0.1 shard_map.56
  96.9 2.3 %shard_map.55.start_ref = f32[8,16,128]{2,1,0:T(8,128)S(1)} custom-call(bf16[1024,4096]{1,0:T(8,128)(2,1)S(1)} %get-tuple-element.35.tile_ref, bf16[32,16,128]{2,1,0:T(8,128)(2,1)S(1)} %all_to_all.38.rows_ref), custom_call_target="tpu_custom_call" | custom-call | tf_op jit(solution)/shard_map/pallas_call | solution.py:19
  99.2 0.0 collective-permute-done.1.rows_ref
  99.2 2.4 %shard_map.57 = f32[8,24,128]{2,1,0:T(8,128)S(1)} custom-call(bf16[1024,4096]{1,0:T(8,128)(2,1)S(1)} %get-tuple-element.32.tile_ref, bf16[32,16,128]{2,1,0:T(8,128)(2,1)S(1)} %collective-permute-done.1.rows_ref, f32[8,16,128]{2,1,0:T(8,128)S(1)} %shard_map.55.start_ref, f32[8,16,128]{2,1,0:T(8,128)S(1)} %get-tuple-element.38.images_ref, ...), custom_call_target="tpu_custom_call" | custom-call | tf_op jit(solution)/shard_map/pallas_call | solution.py:19
  101.5 10.5 %all_to_all.39.parts_ref = f32[8,24,128]{2,1,0:T(8,128)S(1)} all-to-all(f32[8,24,128]{2,1,0:T(8,128)S(1)} %shard_map.57), channel_id=1, replica_groups=mesh['x'=4,'z'=8,'core'=2,'y'=8] {'y'}, dimensions={0} | all-to-all | bytes 196608 | tf_op jit(solution)/shard_map/all_to_all | solution.py:223
  112.0 14.2 %all_to_all.40 = f32[64,1,128]{2,1,0:T(1,128)S(1)} all-to-all(f32[64,1,128]{2,1,0:T(1,128)S(1)} %bitcast.6), channel_id=1, replica_groups=mesh['x'=4,'z'=8,'core'=2,'y'=8] {'x','z','core'}, dimensions={0} | all-to-all | bytes 65536 | tf_op jit(solution)/shard_map/all_to_all | solution.py:223
  126.3 0.7 shard_map.59
  (2 shorter events, 0.0 us)
Async XLA Ops:
  17.7 27.4 %all-to-all-start.1 = ((bf16[32,80,128]{2,1,0:T(8,128)(2,1)}), bf16[32,80,128]{2,1,0:T(8,128)(2,1)S(1)}, u32[]{:S(2)}, u32[]{:S(2)}) async-start(bf16[32,80,128]{2,1,0:T(8,128)(2,1)} %get-tuple-element.24), calls=%async_computation.1 | async-start | bytes 1310720 | tf_op jit(solution)/shard_map/all_to_all | solution.py:223
  30.4 0.7 copy-start
  45.1 12.7 %collective-permute-start = (bf16[32,80,128]{2,1,0:T(8,128)(2,1)S(1)}, bf16[32,80,128]{2,1,0:T(8,128)(2,1)S(1)}, u32[]{:S(2)}, u32[]{:S(2)}) collective-permute-start(bf16[32,80,128]{2,1,0:T(8,128)(2,1)S(1)} %all-to-all-done.1.rows_ref), channel_id=1, source_target_pairs={{0,8},{8,0},{1,9},{9,1},{2,10},{10,2},{3,11},{11,3},{4,12},{12,4},... | collective-permute-start | bytes 1966088 | tf_op jit(solution)/shard_map/ppermute | solution.py:242
  92.7 6.5 %collective-permute-start.1 = (bf16[32,16,128]{2,1,0:T(8,128)(2,1)S(1)}, bf16[32,16,128]{2,1,0:T(8,128)(2,1)S(1)}, u32[]{:S(2)}, u32[]{:S(2)}) collective-permute-start(bf16[32,16,128]{2,1,0:T(8,128)(2,1)S(1)} %all_to_all.38.rows_ref), channel_id=1, source_target_pairs={{0,8},{8,0},{1,9},{9,1},{2,10},{10,2},{3,11},{11,3},{4,12},{12,4},... | collective-permute-start | bytes 393224 | tf_op jit(solution)/shard_map/ppermute | solution.py:261

commit v7 on v3

--- a/solution.py
+++ b/solution.py
@@ -10,7 +10,7 @@
 F32, BF16 = jnp.float32, jnp.bfloat16
 EXTRA = 16
 PAD = 8
-CHUNK = 256
+CHUNK = 1024
 AXES = ("x", "z", "core", "y")
 VMEM = pl.BlockSpec(memory_space=pltpu.VMEM)
 
@@ -48,7 +48,16 @@
     return jnp.concatenate([scaled, below.astype(BF16)], axis=0)
 
 
-def copies(features_ref, right_ref, rows_ref, kept_ref, held, sems):
+def column_copies(features_ref, cols_ref, held, sem):
+    move = pltpu.make_async_copy(features_ref, held, sem)
+    move.start()
+    move.wait()
+    features = held[...]
+    for index in range(cols_ref.shape[0]):
+        cols_ref[index] = features
+
+
+def row_copies(features_ref, right_ref, rows_ref, kept_ref, held, sems):
     moves = [
         pltpu.make_async_copy(features_ref, held, sems.at[0]),
         pltpu.make_async_copy(right_ref, kept_ref, sems.at[1]),
@@ -111,18 +120,18 @@
         high = value.astype(BF16)
         for peer in range(ncols):
             out_ref[peer, index * probes:(index + 1) * probes, :] = high
-        out_ref[index, ncols * probes:(ncols + 1) * probes, :] = high
-        out_ref[index, (ncols + 1) * probes:, :] = (value - high.astype(F32)).astype(BF16)
+        out_ref[index, ncols * probes:, :] = (value - high.astype(F32)).astype(BF16)
 
     tile_and_product(inverse_ref, cols_ref, rows_ref, tile_ref, rows, add)
 
 
 def spread(factor, parts_ref, image_ref, out_ref):
     probes = image_ref.shape[0]
-    begin = parts_ref.shape[1] - 2 * probes
+    last = parts_ref.shape[1] - probes
+    mine = pl.ds(pl.multiple_of(lax.axis_index("y") * probes, probes), probes)
     own = jnp.zeros(image_ref.shape, F32)
     for peer in range(parts_ref.shape[0]):
-        own += parts_ref[peer, begin:begin + probes, :].astype(F32) + parts_ref[peer, begin + probes:, :].astype(F32)
+        own += parts_ref[peer, mine, :].astype(F32) + parts_ref[peer, last:, :].astype(F32)
     image = own * factor
     image_ref[...] = image
     small = image.astype(BF16)
@@ -139,39 +148,27 @@
     return jnp.sum(grid, axis=0, keepdims=True)
 
 
-def column_images(factor, parts_ref, right_ref, image_ref, cols_ref, local_ref):
-    probes = right_ref.shape[0]
-    for index in range(cols_ref.shape[0]):
-        total = jnp.zeros(right_ref.shape, F32)
-        for peer in range(parts_ref.shape[0]):
-            total += parts_ref[peer, index * probes:(index + 1) * probes, :].astype(F32)
-        cols_ref[index] = total * factor
-    right, image = right_ref[...], image_ref[...]
-    pairs = ((right, right), (right, image), (image, image))
-    sums = [(k, jnp.sum(a * b, axis=1, keepdims=True)) for k, (a, b) in enumerate(pairs)]
-    local_ref[...] = placed(sums, right.shape)
-
-
-def second_product(tile_ref, rows_ref, sums_ref):
-    width = rows_ref.shape[2]
-    vectors = jnp.concatenate([rows_ref[index] for index in range(rows_ref.shape[0])], axis=1)
-    part = dot_last(vectors, tile_ref[...])
-    for index in range(sums_ref.shape[0]):
-        sums_ref[index] = part[:, index * width:(index + 1) * width]
-
-
-def third_product(factor, tile_ref, rows_ref, start_ref, images_ref, local_ref, out_ref):
-    ncols, probes, width = start_ref.shape
-    vectors = jnp.concatenate([rows_ref[index] for index in range(rows_ref.shape[0])], axis=1)
-    part = dot_last(vectors, tile_ref[...])
+def second_product(factor, near_ref, far_ref, rows_ref, parts_ref, right_ref, image_ref, out_ref):
+    ncols = out_ref.shape[0]
+    probes, width = right_ref.shape
+    me = lax.axis_index("core")
+    part = jnp.zeros((probes, ncols * width), F32)
+    for half, tile_ref in ((me, near_ref), (1 - me, far_ref)):
+        vectors = jnp.concatenate([rows_ref[half, index] for index in range(rows_ref.shape[1])], axis=1)
+        part += dot_last(vectors, tile_ref[...])
     total = jnp.zeros((probes, width), F32)
     for index in range(ncols):
-        second = (start_ref[index] + part[:, index * width:(index + 1) * width]) * factor
+        first = jnp.zeros((probes, width), F32)
+        for peer in range(parts_ref.shape[0]):
+            first += parts_ref[peer, index * probes:(index + 1) * probes, :].astype(F32)
+        second = part[:, index * width:(index + 1) * width] * factor
         out_ref[index, :probes, :] = second
-        total += second * images_ref[index]
-    energy = placed([(3, jnp.sum(total, axis=1, keepdims=True))], (probes, width))
+        total += first * second
+    right, image = right_ref[...], image_ref[...]
+    products = (right * right, right * image, image * image, total * factor)
+    sums = [(index, jnp.sum(product, axis=1, keepdims=True)) for index, product in enumerate(products)]
     row = lax.broadcasted_iota(jnp.int32, (PAD, width), 0)
-    scalars = jnp.where(row == 0, energy + local_ref[...], 0.0)
+    scalars = jnp.where(row == 0, placed(sums, (probes, width)), 0.0)
     for index in range(ncols):
         out_ref[index, probes:, :] = scalars
 
@@ -223,13 +220,20 @@
     def held(array):
         return pltpu.with_memory_space_constraint(array, pltpu.VMEM)
 
+    source, given = [pltpu.with_memory_space_constraint(array, pltpu.HBM) for array in (features, right_side)]
+    far_off = pl.BlockSpec(memory_space=pltpu.HBM)
+    cols = call(
+        column_copies, source, specs=[far_off], outs=shaped(BF16, ny, feats, width),
+        scratch=[pltpu.VMEM(features.shape, BF16), pltpu.SemaphoreType.DMA],
+    )
+    cols = exchange(cols, "y")
     rows, right = call(
-        copies, features, right_side, specs=[pl.BlockSpec(memory_space=pltpu.HBM)] * 2,
+        row_copies, source, given, specs=[far_off] * 2,
         outs=[shaped(BF16, plane, feats + probes, width), pltpu.VMEM(block.shape, F32)],
         scratch=[pltpu.VMEM(features.shape, BF16), pltpu.SemaphoreType.DMA((2,))],
     )
     right = held(right)
-    cols = lax.all_gather(features, "y")
+    rows, cols = lax.optimization_barrier((rows, cols))
     near = exchange(rows, ("x", "z"))
     inverse, cols = call(
         columns, lengthscale.reshape(1, feats), cols,
@@ -243,23 +247,16 @@
         near_product, inverse, cols, near, outs=[tile, shaped(F32, ny, probes, width)], limit=24, scratch=scratch
     )
     tile_far, parts = call(
-        far_product, inverse, cols, far, sums, outs=[tile, shaped(BF16, ny, (ny + 2) * probes, width)],
+        far_product, inverse, cols, far, sums, outs=[tile, shaped(BF16, ny, (ny + 1) * probes, width)],
         limit=24, scratch=scratch,
     )
     parts = exchange(parts, "y")
     image, rows = call(
         functools.partial(spread, factor), parts, outs=[block, shaped(BF16, plane, probes, width)]
     )
-    near = exchange(rows, ("x", "z"))
-    images, local = call(
-        functools.partial(column_images, factor), parts, right, image,
-        outs=[shaped(F32, ny, probes, width), shaped(F32, 1, width)],
-    )
-    near, images, local = lax.optimization_barrier((near, images, local))
-    far = lax.ppermute(near, "core", swap)
-    sums = call(second_product, held(tile_near), near, outs=shaped(F32, ny, probes, width))
+    both = lax.all_gather(exchange(rows, ("x", "z")), "core")
     sums = call(
-        functools.partial(third_product, factor), held(tile_far), far, sums, images, local,
+        functools.partial(second_product, factor), held(tile_near), held(tile_far), both, parts, right, image,
         outs=shaped(F32, ny, probes + PAD, width),
     )
     second, local = call(gathered, exchange(sums, "y"), outs=[block, shaped(F32, plane * ncore, width)])

time: 140 us -> 126 us (0.900)
  local copies, waits for them, and re-layouts: 13 us -> 0.65 us
  waiting for transfers between devices: 9.08 us -> 20.2 us
  blocking collectives: 64.9 us -> 57.9 us
  starting transfers between devices: 35.3 us -> 28.4 us
    all_gather x1, blocking collectives: 21.4 us -> 4.02 us  [per_device(): both = lax.all_gather(exchange(rows, ('x', 'z')), 'core')]
    unnamed x14 -> x2, local copies, waits for them, and re-layouts: 13 us -> 0.65 us
    all_to_all x2, waiting for transfers between devices: 9.08 us -> 20.2 us  [exchange(): return lax.all_to_all(values, axes, 0, 0, tiled=True)]
    all_to_all x3 -> x4, blocking collectives: 43.5 us -> 53.9 us  [exchange(): return lax.all_to_all(values, axes, 0, 0, tiled=True)]
    ppermute x2 -> x1, starting transfers between devices: 12 us -> 8.09 us  [per_device(): far = lax.ppermute(near, 'core', swap)]
    all_to_all x2, starting transfers between devices: 23.2 us -> 20.3 us  [exchange(): return lax.all_to_all(values, axes, 0, 0, tiled=True)]
    pallas_call x10 -> x9, Pallas kernels: 16.6 us -> 17.7 us  [call(): pl.pallas_call(kernel, in_specs=specs or [VMEM] * len(args), out_specs=ja...]
  transfers between devices with their start and end apart: 4 -> 3, of which waited for: 1 -> 2; matrix products, arithmetic and copies ran while one was open for 0% -> 0% of each run, Pallas kernels for 5% -> 5%
where the time goes in v7:
time: 126 us; the launch traced here: 125 us
  blocking collectives  57.9 us (46%)
  starting transfers between devices  28.4 us (23%)
  waiting for transfers between devices  20.2 us (16%)
  Pallas kernels  17.7 us (14%)
    all_to_all x4, blocking collectives, exchange(): return lax.all_to_all(values, axes, 0, 0, tiled=True)  53.9 us
    all_to_all x2, starting transfers between devices, exchange(): return lax.all_to_all(values, axes, 0, 0, tiled=True)  20.3 us
    all_to_all x2, waiting for transfers between devices, exchange(): return lax.all_to_all(values, axes, 0, 0, tiled=True)  20.2 us
    pallas_call x9, Pallas kernels, call(): pl.pallas_call(kernel, in_specs=specs or [VMEM] * len(args), out_specs=ja...  17.7 us
    ppermute x1, starting transfers between devices, per_device(): far = lax.ppermute(near, 'core', swap)  8.09 us
    all_gather x1, blocking collectives, per_device(): both = lax.all_gather(exchange(rows, ('x', 'z')), 'core')  4.02 us
  transfers between devices with their start and end apart: 3, of which 2 were waited for; matrix products, arithmetic and copies ran while one was open for 0% of the time, Pallas kernels for 5%

profile of v7, /device:TPU:1, one launch (start us, length us, event | category | flops | bytes accessed | tf_op | source)
XLA Modules:
  0.0 125.5 jit_solution(8444587234123474762)
XLA Ops:
  0.6 1.4 %shard_map.51 = bf16[8,64,128]{2,1,0:T(8,128)(2,1)} custom-call(bf16[64,128]{1,0:T(8,128)(2,1)} %features_ref.3), custom_call_target="tpu_custom_call" | custom-call | tf_op jit(solution)/shard_map/pallas_call | solution.py:19
  2.0 7.7 %all-to-all-start = ((bf16[8,64,128]{2,1,0:T(8,128)(2,1)}), bf16[8,64,128]{2,1,0:T(8,128)(2,1)S(1)}, u32[]{:S(2)}, u32[]{:S(2)}) async-start(bf16[8,64,128]{2,1,0:T(8,128)(2,1)} %shard_map.51), calls=%async_computation | async-start | bytes 262144 | tf_op jit(solution)/shard_map/all_to_all | solution.py:218
  9.7 1.7 %shard_map.50 = (bf16[32,80,128]{2,1,0:T(8,128)(2,1)}, f32[16,128]{1,0:T(8,128)S(1)}) custom-call(bf16[64,128]{1,0:T(8,128)(2,1)} %features_ref.3, f32[16,128]{1,0:T(8,128)} %right_ref.1), custom_call_target="tpu_custom_call" | custom-call | tf_op jit(solution)/shard_map/pallas_call | solution.py:19
  11.3 6.4 %all-to-all-done.cols_ref = bf16[8,64,128]{2,1,0:T(8,128)(2,1)S(1)} async-done(((bf16[8,64,128]{2,1,0:T(8,128)(2,1)}), bf16[8,64,128]{2,1,0:T(8,128)(2,1)S(1)}, u32[]{:S(2)}, u32[]{:S(2)}) %all-to-all-start) | async-done | bytes 131104 | tf_op jit(solution)/shard_map/all_to_all | solution.py:218
  17.7 12.6 %all-to-all-start.1 = ((bf16[32,80,128]{2,1,0:T(8,128)(2,1)}), bf16[32,80,128]{2,1,0:T(8,128)(2,1)S(1)}, u32[]{:S(2)}, u32[]{:S(2)}) async-start(bf16[32,80,128]{2,1,0:T(8,128)(2,1)} %get-tuple-element.20), calls=%async_computation.1 | async-start | bytes 1310720 | tf_op jit(solution)/shard_map/all_to_all | solution.py:218
  30.4 0.0 copy-start
  30.4 0.6 copy-done
  31.0 0.2 shard_map.52
  31.3 13.8 %all-to-all-done.1.rows_ref = bf16[32,80,128]{2,1,0:T(8,128)(2,1)S(1)} async-done(((bf16[32,80,128]{2,1,0:T(8,128)(2,1)}), bf16[32,80,128]{2,1,0:T(8,128)(2,1)S(1)}, u32[]{:S(2)}, u32[]{:S(2)}) %all-to-all-start.1) | async-done | bytes 655392 | tf_op jit(solution)/shard_map/all_to_all | solution.py:218
  45.1 8.1 %collective-permute-start = (bf16[32,80,128]{2,1,0:T(8,128)(2,1)S(1)}, bf16[32,80,128]{2,1,0:T(8,128)(2,1)S(1)}, u32[]{:S(2)}, u32[]{:S(2)}) collective-permute-start(bf16[32,80,128]{2,1,0:T(8,128)(2,1)S(1)} %all-to-all-done.1.rows_ref), channel_id=1, source_target_pairs={{0,8},{8,0},{1,9},{9,1},{2,10},{10,2},{3,11},{11,3},{4,12},{12,4},... | collective-permute-start | bytes 1966088 | tf_op jit(solution)/shard_map/ppermute | solution.py:243
  53.1 4.6 %shard_map.53 = (bf16[1024,4096]{1,0:T(8,128)(2,1)S(1)}, f32[8,16,128]{2,1,0:T(8,128)S(1)}) custom-call(f32[64,128]{1,0:T(8,128)S(1)} %get-tuple-element.24.inverse_ref, bf16[1024,80]{1,0:T(8,128)(2,1)S(1)} %get-tuple-element.25.cols_ref, bf16[32,80,128]{2,1,0:T(8,128)(2,1)S(1)} %all-to-all-done.1.rows_ref), custom_call_target="tpu_custom_call" | custom-call | tf_op jit(solution)/shard_map/pallas_call | solution.py:19
  57.7 0.0 collective-permute-done.rows_ref
  57.7 4.6 %shard_map.54 = (bf16[1024,4096]{1,0:T(8,128)(2,1)S(1)}, bf16[8,144,128]{2,1,0:T(8,128)(2,1)S(1)}) custom-call(f32[64,128]{1,0:T(8,128)S(1)} %get-tuple-element.24.inverse_ref, bf16[1024,80]{1,0:T(8,128)(2,1)S(1)} %get-tuple-element.25.cols_ref, bf16[32,80,128]{2,1,0:T(8,128)(2,1)S(1)} %collective-permute-done.rows_ref, ...), custom_call_target="tpu_custom_call" | custom-call | tf_op jit(solution)/shard_map/pallas_call | solution.py:19
  62.3 15.3 %all_to_all.36.parts_ref = bf16[8,144,128]{2,1,0:T(8,128)(2,1)S(1)} all-to-all(bf16[8,144,128]{2,1,0:T(8,128)(2,1)S(1)} %get-tuple-element.30), channel_id=1, replica_groups=mesh['x'=4,'z'=8,'core'=2,'y'=8] {'y'}, dimensions={0} | all-to-all | bytes 589824 | tf_op jit(solution)/shard_map/all_to_all | solution.py:218
  77.7 13.8 %all_to_all.37 = bf16[32,16,128]{2,1,0:T(8,128)(2,1)S(1)} all-to-all(bf16[32,16,128]{2,1,0:T(8,128)(2,1)S(1)} %get-tuple-element.31), channel_id=1, replica_groups=mesh['x'=4,'z'=8,'core'=2,'y'=8] {'x','z'}, dimensions={0} | all-to-all | bytes 262144 | tf_op jit(solution)/shard_map/all_to_all | solution.py:218
  91.5 4.0 %all-gather = bf16[64,16,128]{2,1,0:T(8,128)(2,1)S(1)} all-gather(bf16[32,16,128]{2,1,0:T(8,128)(2,1)S(1)} %all_to_all.37), channel_id=2, replica_groups=mesh['x'=4,'z'=8,'core'=2,'y'=8] {'core'}, dimensions={0}, use_global_device_ids=true | all-gather | bytes 393216 | tf_op jit(solution)/shard_map/all_gather | solution.py:257
  95.5 4.5 %shard_map.56 = f32[8,24,128]{2,1,0:T(8,128)S(1)} custom-call(bf16[1024,4096]{1,0:T(8,128)(2,1)S(1)} %get-tuple-element.27.near_ref, bf16[1024,4096]{1,0:T(8,128)(2,1)S(1)} %get-tuple-element.29.far_ref, bf16[2,32,16,128]{3,2,1,0:T(8,128)(2,1)S(1)} %bitcast.6, bf16[8,144,128]{2,1,0:T(8,128)(2,1)S(1)} %all_to_all.36.parts_ref, ...), custom_call_target="tpu_custom_call" | custom-call | tf_op jit(solution)/shard_map/pallas_call | solution.py:19
  100.0 10.0 %all_to_all.38.parts_ref = f32[8,24,128]{2,1,0:T(8,128)S(1)} all-to-all(f32[8,24,128]{2,1,0:T(8,128)S(1)} %shard_map.56), channel_id=1, replica_groups=mesh['x'=4,'z'=8,'core'=2,'y'=8] {'y'}, dimensions={0} | all-to-all | bytes 196608 | tf_op jit(solution)/shard_map/all_to_all | solution.py:218
  110.0 14.7 %all_to_all.39 = f32[64,1,128]{2,1,0:T(1,128)S(1)} all-to-all(f32[64,1,128]{2,1,0:T(1,128)S(1)} %bitcast.8), channel_id=1, replica_groups=mesh['x'=4,'z'=8,'core'=2,'y'=8] {'x','z','core'}, dimensions={0} | all-to-all | bytes 65536 | tf_op jit(solution)/shard_map/all_to_all | solution.py:218
  124.8 0.7 shard_map.58
  (2 shorter events, 0.0 us)
Async XLA Ops:
  2.0 15.7 %all-to-all-start = ((bf16[8,64,128]{2,1,0:T(8,128)(2,1)}), bf16[8,64,128]{2,1,0:T(8,128)(2,1)S(1)}, u32[]{:S(2)}, u32[]{:S(2)}) async-start(bf16[8,64,128]{2,1,0:T(8,128)(2,1)} %shard_map.51), calls=%async_computation | async-start | bytes 262144 | tf_op jit(solution)/shard_map/all_to_all | solution.py:218
  17.7 27.3 %all-to-all-start.1 = ((bf16[32,80,128]{2,1,0:T(8,128)(2,1)}), bf16[32,80,128]{2,1,0:T(8,128)(2,1)S(1)}, u32[]{:S(2)}, u32[]{:S(2)}) async-start(bf16[32,80,128]{2,1,0:T(8,128)(2,1)} %get-tuple-element.20), calls=%async_computation.1 | async-start | bytes 1310720 | tf_op jit(solution)/shard_map/all_to_all | solution.py:218
  30.4 0.7 copy-start
  45.1 12.7 %collective-permute-start = (bf16[32,80,128]{2,1,0:T(8,128)(2,1)S(1)}, bf16[32,80,128]{2,1,0:T(8,128)(2,1)S(1)}, u32[]{:S(2)}, u32[]{:S(2)}) collective-permute-start(bf16[32,80,128]{2,1,0:T(8,128)(2,1)S(1)} %all-to-all-done.1.rows_ref), channel_id=1, source_target_pairs={{0,8},{8,0},{1,9},{9,1},{2,10},{10,2},{3,11},{11,3},{4,12},{12,4},... | collective-permute-start | bytes 1966088 | tf_op jit(solution)/shard_map/ppermute | solution.py:243

commit v8 on v7

--- a/solution.py
+++ b/solution.py
@@ -11,7 +11,8 @@
 EXTRA = 16
 PAD = 8
 CHUNK = 1024
-AXES = ("x", "z", "core", "y")
+COLS = ("ya", "yb", "yc")
+AXES = ("x", "z", "core") + COLS
 VMEM = pl.BlockSpec(memory_space=pltpu.VMEM)
 
 
@@ -46,15 +47,6 @@
     for index, part in enumerate((high, middle, low)):
         below = jnp.where(row == offset + index, part, below)
     return jnp.concatenate([scaled, below.astype(BF16)], axis=0)
-
-
-def column_copies(features_ref, cols_ref, held, sem):
-    move = pltpu.make_async_copy(features_ref, held, sem)
-    move.start()
-    move.wait()
-    features = held[...]
-    for index in range(cols_ref.shape[0]):
-        cols_ref[index] = features
 
 
 def row_copies(features_ref, right_ref, rows_ref, kept_ref, held, sems):
@@ -73,15 +65,15 @@
         rows_ref[index, feats:, :] = right
 
 
-def columns(scale_ref, cols_ref, inverse_ref, out_ref):
+def columns(order, scale_ref, cols_ref, inverse_ref, out_ref):
     ncols, feats, width = cols_ref.shape
     lane = lax.broadcasted_iota(jnp.int32, (feats, feats), 1)
     row = lax.broadcasted_iota(jnp.int32, (feats, feats), 0)
     scale = jnp.sum(jnp.where(lane == row, scale_ref[...], 0.0), axis=1, keepdims=True)
     inverse = jnp.broadcast_to(1.0 / scale, (feats, width))
     inverse_ref[...] = inverse
-    for index in range(ncols):
-        block = augmented(cols_ref[index], inverse, 0).astype(F32)
+    for place, index in enumerate(order):
+        block = augmented(cols_ref[place], inverse, 0).astype(F32)
         out_ref[index * width:(index + 1) * width, :] = jnp.transpose(block).astype(BF16)
 
 
@@ -128,7 +120,7 @@
 def spread(factor, parts_ref, image_ref, out_ref):
     probes = image_ref.shape[0]
     last = parts_ref.shape[1] - probes
-    mine = pl.ds(pl.multiple_of(lax.axis_index("y") * probes, probes), probes)
+    mine = pl.ds(pl.multiple_of(lax.axis_index(COLS) * probes, probes), probes)
     own = jnp.zeros(image_ref.shape, F32)
     for peer in range(parts_ref.shape[0]):
         own += parts_ref[peer, mine, :].astype(F32) + parts_ref[peer, last:, :].astype(F32)
@@ -206,7 +198,8 @@
 
 
 def per_device(features, lengthscale, right_side):
-    nx, nz, ncore, ny = [lax.axis_size(axis) for axis in AXES]
+    nx, nz, ncore = [lax.axis_size(axis) for axis in AXES[:3]]
+    ny = lax.axis_size(COLS)
     feats, width = features.shape
     probes = right_side.shape[0]
     plane = nx * nz
@@ -222,21 +215,19 @@
 
     source, given = [pltpu.with_memory_space_constraint(array, pltpu.HBM) for array in (features, right_side)]
     far_off = pl.BlockSpec(memory_space=pltpu.HBM)
-    cols = call(
-        column_copies, source, specs=[far_off], outs=shaped(BF16, ny, feats, width),
-        scratch=[pltpu.VMEM(features.shape, BF16), pltpu.SemaphoreType.DMA],
-    )
-    cols = exchange(cols, "y")
     rows, right = call(
         row_copies, source, given, specs=[far_off] * 2,
         outs=[shaped(BF16, plane, feats + probes, width), pltpu.VMEM(block.shape, F32)],
         scratch=[pltpu.VMEM(features.shape, BF16), pltpu.SemaphoreType.DMA((2,))],
     )
     right = held(right)
-    rows, cols = lax.optimization_barrier((rows, cols))
     near = exchange(rows, ("x", "z"))
+    cols = features[None]
+    for axis in COLS:
+        cols = lax.all_gather(cols, axis, axis=0, tiled=True)
+    order = [sum(((place >> bit) & 1) << (len(COLS) - 1 - bit) for bit in range(len(COLS))) for place in range(ny)]
     inverse, cols = call(
-        columns, lengthscale.reshape(1, feats), cols,
+        functools.partial(columns, order), lengthscale.reshape(1, feats), cols,
         outs=[shaped(F32, feats, width), shaped(BF16, ny * width, feats + EXTRA)],
     )
     near, inverse, cols = lax.optimization_barrier((near, inverse, cols))
@@ -250,7 +241,7 @@
         far_product, inverse, cols, far, sums, outs=[tile, shaped(BF16, ny, (ny + 1) * probes, width)],
         limit=24, scratch=scratch,
     )
-    parts = exchange(parts, "y")
+    parts = exchange(parts, COLS)
     image, rows = call(
         functools.partial(spread, factor), parts, outs=[block, shaped(BF16, plane, probes, width)]
     )
@@ -259,13 +250,13 @@
         functools.partial(second_product, factor), held(tile_near), held(tile_far), both, parts, right, image,
         outs=shaped(F32, ny, probes + PAD, width),
     )
-    second, local = call(gathered, exchange(sums, "y"), outs=[block, shaped(F32, plane * ncore, width)])
+    second, local = call(gathered, exchange(sums, COLS), outs=[block, shaped(F32, plane * ncore, width)])
     everyone = exchange(local, ("x", "z", "core"))
     return call(finish, everyone, right, image, second, outs=[block, block])
 
 
 def solution(mesh):
-    fine = Mesh(mesh.devices.reshape(4, 8, 2, 8), AXES)
+    fine = Mesh(mesh.devices.reshape(4, 8, 2, 2, 2, 2), AXES)
     split = P(None, AXES)
     return jax.shard_map(
         per_device,

time: 126 us -> 121 us (0.960)
  blocking collectives: 57.9 us -> 82.7 us
  waiting for transfers between devices: 20.2 us -> 0.01 us
  starting transfers between devices: 28.4 us -> 19.8 us
  Pallas kernels: 17.7 us -> 16.3 us
    all_to_all x2 -> x1, waiting for transfers between devices: 20.2 us -> 0.01 us  [exchange(): return lax.all_to_all(values, axes, 0, 0, tiled=True)]
    all_gather x0 -> x3, blocking collectives: none -> 16.3 us  [per_device(): cols = lax.all_gather(cols, axis, axis=0, tiled=True)]
    all_to_all x4, blocking collectives: 53.9 us -> 62.3 us  [exchange(): return lax.all_to_all(values, axes, 0, 0, tiled=True)]
    all_to_all x2 -> x1, starting transfers between devices: 20.3 us -> 13.7 us  [exchange(): return lax.all_to_all(values, axes, 0, 0, tiled=True)]
    ppermute x1, starting transfers between devices: 8.09 us -> 6.06 us  [per_device(): far = lax.ppermute(near, 'core', swap)]
    pallas_call x9 -> x8, Pallas kernels: 17.7 us -> 16.3 us  [call(): pl.pallas_call(kernel, in_specs=specs or [VMEM] * len(args), out_specs=ja...]
  transfers between devices with their start and end apart: 3 -> 2, of which waited for: 2 -> 0; matrix products, arithmetic and copies ran while one was open for 0% -> 0% of each run, Pallas kernels for 5% -> 4%
where the time goes in v8:
time: 121 us; the launch traced here: 120 us
  blocking collectives  82.7 us (68%)
  starting transfers between devices  19.8 us (16%)
  Pallas kernels  16.3 us (13%)
    all_to_all x4, blocking collectives, exchange(): return lax.all_to_all(values, axes, 0, 0, tiled=True)  62.3 us
    pallas_call x8, Pallas kernels, call(): pl.pallas_call(kernel, in_specs=specs or [VMEM] * len(args), out_specs=ja...  16.3 us
    all_gather x3, blocking collectives, per_device(): cols = lax.all_gather(cols, axis, axis=0, tiled=True)  16.3 us
    all_to_all x1, starting transfers between devices, exchange(): return lax.all_to_all(values, axes, 0, 0, tiled=True)  13.7 us
    ppermute x1, starting transfers between devices, per_device(): far = lax.ppermute(near, 'core', swap)  6.06 us
    all_gather x1, blocking collectives, per_device(): both = lax.all_gather(exchange(rows, ('x', 'z')), 'core')  4.05 us
  transfers between devices with their start and end apart: 2, of which 0 were waited for; matrix products, arithmetic and copies ran while one was open for 0% of the time, Pallas kernels for 4%

profile of v8, /device:TPU:1, one launch (start us, length us, event | category | flops | bytes accessed | tf_op | source)
XLA Modules:
  0.0 120.1 jit_solution(6733025376083774443)
XLA Ops:
  0.6 1.6 %shard_map.50 = (bf16[32,80,128]{2,1,0:T(8,128)(2,1)}, f32[16,128]{1,0:T(8,128)S(1)}) custom-call(bf16[64,128]{1,0:T(8,128)(2,1)} %features_ref.1, f32[16,128]{1,0:T(8,128)} %right_ref.1), custom_call_target="tpu_custom_call" | custom-call | tf_op jit(solution)/shard_map/pallas_call | solution.py:20
  2.3 13.7 %all-to-all-start = ((bf16[32,80,128]{2,1,0:T(8,128)(2,1)}), bf16[32,80,128]{2,1,0:T(8,128)(2,1)S(1)}, u32[]{:S(2)}, u32[]{:S(2)}) async-start(bf16[32,80,128]{2,1,0:T(8,128)(2,1)} %get-tuple-element.17), calls=%async_computation | async-start | bytes 1310720 | tf_op jit(solution)/shard_map/all_to_all | solution.py:211
  16.0 7.6 %all-gather = bf16[128,128]{1,0:T(8,128)(2,1)S(1)} all-gather(bf16[64,128]{1,0:T(8,128)(2,1)} %features_ref.1), channel_id=2, replica_groups=mesh['x'=4,'z'=8,'core'=2,'ya'=2,'yb'=2,'yc'=2] {'ya'}, dimensions={0}, use_global_device_ids=true | all-gather | bytes 49152 | tf_op jit(solution)/shard_map/all_gather | solution.py:227
  23.6 4.6 %all_gather.16 = bf16[4,64,128]{2,1,0:T(8,128)(2,1)S(1)} all-gather(bf16[2,64,128]{2,1,0:T(8,128)(2,1)S(1)} %bitcast.11), channel_id=1, replica_groups=mesh['x'=4,'z'=8,'core'=2,'ya'=2,'yb'=2,'yc'=2] {'yb'}, dimensions={0}, use_global_device_ids=true | all-gather | bytes 98304 | tf_op jit(solution)/shard_map/all_gather | solution.py:227
  28.3 4.1 %all_gather.17.cols_ref = bf16[8,64,128]{2,1,0:T(8,128)(2,1)S(1)} all-gather(bf16[4,64,128]{2,1,0:T(8,128)(2,1)S(1)} %all_gather.16), channel_id=1, replica_groups=mesh['x'=4,'z'=8,'core'=2,'ya'=2,'yb'=2,'yc'=2] {'yc'}, dimensions={0}, use_global_device_ids=true | all-gather | bytes 196608 | tf_op jit(solution)/shard_map/all_gather | solution.py:227
  32.3 0.0 copy-start
  32.3 0.7 copy-done
  33.0 0.2 shard_map.51
  33.2 0.0 all-to-all-done.rows_ref
  33.3 6.1 %collective-permute-start = (bf16[32,80,128]{2,1,0:T(8,128)(2,1)S(1)}, bf16[32,80,128]{2,1,0:T(8,128)(2,1)S(1)}, u32[]{:S(2)}, u32[]{:S(2)}) collective-permute-start(bf16[32,80,128]{2,1,0:T(8,128)(2,1)S(1)} %all-to-all-done.rows_ref), channel_id=1, source_target_pairs={{0,8},{8,0},{1,9},{9,1},{2,10},{10,2},{3,11},{11,3},{4,12},{12,4},... | collective-permute-start | bytes 1966088 | tf_op jit(solution)/shard_map/ppermute | solution.py:234
  39.3 4.6 %shard_map.52 = (bf16[1024,4096]{1,0:T(8,128)(2,1)S(1)}, f32[8,16,128]{2,1,0:T(8,128)S(1)}) custom-call(f32[64,128]{1,0:T(8,128)S(1)} %get-tuple-element.20.inverse_ref, bf16[1024,80]{1,0:T(8,128)(2,1)S(1)} %get-tuple-element.21.cols_ref, bf16[32,80,128]{2,1,0:T(8,128)(2,1)S(1)} %all-to-all-done.rows_ref), custom_call_target="tpu_custom_call" | custom-call | tf_op jit(solution)/shard_map/pallas_call | solution.py:20
  43.9 0.0 collective-permute-done.rows_ref
  43.9 4.6 %shard_map.53 = (bf16[1024,4096]{1,0:T(8,128)(2,1)S(1)}, bf16[8,144,128]{2,1,0:T(8,128)(2,1)S(1)}) custom-call(f32[64,128]{1,0:T(8,128)S(1)} %get-tuple-element.20.inverse_ref, bf16[1024,80]{1,0:T(8,128)(2,1)S(1)} %get-tuple-element.21.cols_ref, bf16[32,80,128]{2,1,0:T(8,128)(2,1)S(1)} %collective-permute-done.rows_ref, ...), custom_call_target="tpu_custom_call" | custom-call | tf_op jit(solution)/shard_map/pallas_call | solution.py:20
  48.5 19.3 %all_to_all.31.parts_ref = bf16[8,144,128]{2,1,0:T(8,128)(2,1)S(1)} all-to-all(bf16[8,144,128]{2,1,0:T(8,128)(2,1)S(1)} %get-tuple-element.26), channel_id=1, replica_groups=mesh['x'=4,'z'=8,'core'=2,'ya'=2,'yb'=2,'yc'=2] {'ya','yb','yc'}, dimensions={0} | all-to-all | bytes 589824 | tf_op jit(solution)/shard_map/all_to_all | solution.py:211
  67.9 18.2 %all_to_all.32 = bf16[32,16,128]{2,1,0:T(8,128)(2,1)S(1)} all-to-all(bf16[32,16,128]{2,1,0:T(8,128)(2,1)S(1)} %get-tuple-element.27), channel_id=1, replica_groups=mesh['x'=4,'z'=8,'core'=2,'ya'=2,'yb'=2,'yc'=2] {'x','z'}, dimensions={0} | all-to-all | bytes 262144 | tf_op jit(solution)/shard_map/all_to_all | solution.py:211
  86.1 4.0 %all-gather.1 = bf16[64,16,128]{2,1,0:T(8,128)(2,1)S(1)} all-gather(bf16[32,16,128]{2,1,0:T(8,128)(2,1)S(1)} %all_to_all.32), channel_id=3, replica_groups=mesh['x'=4,'z'=8,'core'=2,'ya'=2,'yb'=2,'yc'=2] {'core'}, dimensions={0}, use_global_device_ids=true | all-gather | bytes 393216 | tf_op jit(solution)/shard_map/all_gather | solution.py:248
  90.1 4.5 %shard_map.55 = f32[8,24,128]{2,1,0:T(8,128)S(1)} custom-call(bf16[1024,4096]{1,0:T(8,128)(2,1)S(1)} %get-tuple-element.23.near_ref, bf16[1024,4096]{1,0:T(8,128)(2,1)S(1)} %get-tuple-element.25.far_ref, bf16[2,32,16,128]{3,2,1,0:T(8,128)(2,1)S(1)} %bitcast.7, bf16[8,144,128]{2,1,0:T(8,128)(2,1)S(1)} %all_to_all.31.parts_ref, ...), custom_call_target="tpu_custom_call" | custom-call | tf_op jit(solution)/shard_map/pallas_call | solution.py:20
  94.6 10.0 %all_to_all.33.parts_ref = f32[8,24,128]{2,1,0:T(8,128)S(1)} all-to-all(f32[8,24,128]{2,1,0:T(8,128)S(1)} %shard_map.55), channel_id=1, replica_groups=mesh['x'=4,'z'=8,'core'=2,'ya'=2,'yb'=2,'yc'=2] {'ya','yb','yc'}, dimensions={0} | all-to-all | bytes 196608 | tf_op jit(solution)/shard_map/all_to_all | solution.py:211
  104.7 14.7 %all_to_all.34 = f32[64,1,128]{2,1,0:T(1,128)S(1)} all-to-all(f32[64,1,128]{2,1,0:T(1,128)S(1)} %bitcast.9), channel_id=1, replica_groups=mesh['x'=4,'z'=8,'core'=2,'ya'=2,'yb'=2,'yc'=2] {'x','z','core'}, dimensions={0} | all-to-all | bytes 65536 | tf_op jit(solution)/shard_map/all_to_all | solution.py:211
  119.4 0.7 shard_map.57
  (2 shorter events, 0.0 us)
Async XLA Ops:
  2.3 31.0 %all-to-all-start = ((bf16[32,80,128]{2,1,0:T(8,128)(2,1)}), bf16[32,80,128]{2,1,0:T(8,128)(2,1)S(1)}, u32[]{:S(2)}, u32[]{:S(2)}) async-start(bf16[32,80,128]{2,1,0:T(8,128)(2,1)} %get-tuple-element.17), calls=%async_computation | async-start | bytes 1310720 | tf_op jit(solution)/shard_map/all_to_all | solution.py:211
  32.3 0.7 copy-start
  33.3 10.6 %collective-permute-start = (bf16[32,80,128]{2,1,0:T(8,128)(2,1)S(1)}, bf16[32,80,128]{2,1,0:T(8,128)(2,1)S(1)}, u32[]{:S(2)}, u32[]{:S(2)}) collective-permute-start(bf16[32,80,128]{2,1,0:T(8,128)(2,1)S(1)} %all-to-all-done.rows_ref), channel_id=1, source_target_pairs={{0,8},{8,0},{1,9},{9,1},{2,10},{10,2},{3,11},{11,3},{4,12},{12,4},... | collective-permute-start | bytes 1966088 | tf_op jit(solution)/shard_map/ppermute | solution.py:234

commit v9 on v8

--- a/solution.py
+++ b/solution.py
@@ -10,7 +10,6 @@
 F32, BF16 = jnp.float32, jnp.bfloat16
 EXTRA = 16
 PAD = 8
-CHUNK = 1024
 COLS = ("ya", "yb", "yc")
 AXES = ("x", "z", "core") + COLS
 VMEM = pl.BlockSpec(memory_space=pltpu.VMEM)
@@ -65,56 +64,77 @@
         rows_ref[index, feats:, :] = right
 
 
-def columns(order, scale_ref, cols_ref, inverse_ref, out_ref):
-    ncols, feats, width = cols_ref.shape
+def put_columns(cols_ref, inverse, out_ref):
+    ncols, _, width = cols_ref.shape
+    for index in range(ncols):
+        block = augmented(cols_ref[index % 2 * 2 + index // 2], inverse, 0).astype(F32)
+        out_ref[index * width:(index + 1) * width, :] = jnp.transpose(block).astype(BF16)
+
+
+def columns(scale_ref, cols_ref, inverse_ref, out_ref):
+    _, feats, width = cols_ref.shape
     lane = lax.broadcasted_iota(jnp.int32, (feats, feats), 1)
     row = lax.broadcasted_iota(jnp.int32, (feats, feats), 0)
     scale = jnp.sum(jnp.where(lane == row, scale_ref[...], 0.0), axis=1, keepdims=True)
     inverse = jnp.broadcast_to(1.0 / scale, (feats, width))
     inverse_ref[...] = inverse
-    for place, index in enumerate(order):
-        block = augmented(cols_ref[place], inverse, 0).astype(F32)
-        out_ref[index * width:(index + 1) * width, :] = jnp.transpose(block).astype(BF16)
+    put_columns(cols_ref, inverse, out_ref)
 
 
 def dot_last(left, right):
     return lax.dot_general(left, right, (((1,), (1,)), ((), ())), preferred_element_type=F32)
 
 
-def tile_and_product(inverse_ref, cols_ref, rows_ref, tile_ref, rows, add):
+def put_rows(rows_ref, inverse, out_ref):
+    feats, width = inverse.shape
+    for index in range(rows_ref.shape[0]):
+        out_ref[:, index * width:(index + 1) * width] = augmented(rows_ref[index, :feats, :], inverse, 3)
+
+
+def vectors_of(rows_ref, feats):
+    return jnp.concatenate([rows_ref[index, feats:, :] for index in range(rows_ref.shape[0])], axis=1)
+
+
+def tile_and_product(cols_ref, rows_ref, vectors, tile_ref):
+    inner = jnp.dot(cols_ref[...], rows_ref[...], preferred_element_type=F32)
+    tile = jnp.exp(inner).astype(BF16)
+    tile_ref[...] = tile
+    return dot_last(vectors, tile)
+
+
+def own_near(inverse_ref, cols_ref, near_ref, tile_ref, sums_ref, rows_ref):
+    put_rows(near_ref, inverse_ref[...], rows_ref)
+    sums_ref[...] = tile_and_product(cols_ref, rows_ref, vectors_of(near_ref, inverse_ref.shape[0]), tile_ref)
+
+
+def other_near(inverse_ref, raw_ref, near_ref, rows_ref, tile_ref, sums_ref, cols_ref):
+    put_columns(raw_ref, inverse_ref[...], cols_ref)
+    sums_ref[...] = tile_and_product(cols_ref, rows_ref, vectors_of(near_ref, inverse_ref.shape[0]), tile_ref)
+
+
+def placing(ncols):
+    me = lax.axis_index(COLS[2])
+    half = ncols // 2
+    return [index % half * 2 + (me if index < half else 1 - me) for index in range(ncols)]
+
+
+def far_product(inverse_ref, own_ref, other_ref, far_ref, own_sums_ref, other_sums_ref, tile_ref, out_ref, rows, cols):
+    probes = own_sums_ref.shape[0]
+    ncols = out_ref.shape[0]
     feats, width = inverse_ref.shape
-    inverse = inverse_ref[...]
-    nrows = rows_ref.shape[0]
-    for index in range(nrows):
-        rows[:, index * width:(index + 1) * width] = augmented(rows_ref[index, :feats, :], inverse, 3)
-    vectors = jnp.concatenate([rows_ref[index, feats:, :] for index in range(nrows)], axis=1)
-    for begin in range(0, cols_ref.shape[0], CHUNK):
-        inner = jnp.dot(cols_ref[begin:begin + CHUNK, :], rows[...], preferred_element_type=F32)
-        tile = jnp.exp(inner).astype(BF16)
-        tile_ref[begin:begin + CHUNK, :] = tile
-        part = dot_last(vectors, tile)
-        for index in range(CHUNK // width):
-            add(begin // width + index, part[:, index * width:(index + 1) * width])
-
-
-def near_product(inverse_ref, cols_ref, rows_ref, tile_ref, sums_ref, rows):
-    def add(index, piece):
-        sums_ref[index] = piece
-
-    tile_and_product(inverse_ref, cols_ref, rows_ref, tile_ref, rows, add)
-
-
-def far_product(inverse_ref, cols_ref, rows_ref, sums_ref, tile_ref, out_ref, rows):
-    ncols, probes, _ = sums_ref.shape
-
-    def add(index, piece):
-        value = sums_ref[index] + piece
+    middle = own_ref.shape[0]
+    cols[:middle, :] = own_ref[...]
+    cols[middle:, :] = other_ref[...]
+    put_rows(far_ref, inverse_ref[...], rows)
+    part = tile_and_product(cols, rows, vectors_of(far_ref, feats), tile_ref)
+    part += jnp.concatenate([own_sums_ref[...], other_sums_ref[...]], axis=1)
+    for index, place in enumerate(placing(ncols)):
+        value = part[:, index * width:(index + 1) * width]
         high = value.astype(BF16)
+        where = pl.ds(pl.multiple_of(place * probes, probes), probes)
         for peer in range(ncols):
-            out_ref[peer, index * probes:(index + 1) * probes, :] = high
-        out_ref[index, ncols * probes:, :] = (value - high.astype(F32)).astype(BF16)
-
-    tile_and_product(inverse_ref, cols_ref, rows_ref, tile_ref, rows, add)
+            out_ref[peer, where, :] = high
+        out_ref[place, ncols * probes:, :] = (value - high.astype(F32)).astype(BF16)
 
 
 def spread(factor, parts_ref, image_ref, out_ref):
@@ -140,21 +160,23 @@
     return jnp.sum(grid, axis=0, keepdims=True)
 
 
-def second_product(factor, near_ref, far_ref, rows_ref, parts_ref, right_ref, image_ref, out_ref):
+def second_product(factor, own_ref, other_ref, far_ref, rows_ref, parts_ref, right_ref, image_ref, out_ref):
     ncols = out_ref.shape[0]
     probes, width = right_ref.shape
     me = lax.axis_index("core")
-    part = jnp.zeros((probes, ncols * width), F32)
-    for half, tile_ref in ((me, near_ref), (1 - me, far_ref)):
-        vectors = jnp.concatenate([rows_ref[half, index] for index in range(rows_ref.shape[1])], axis=1)
-        part += dot_last(vectors, tile_ref[...])
+    near, far = [
+        jnp.concatenate([rows_ref[half, index] for index in range(rows_ref.shape[1])], axis=1) for half in (me, 1 - me)
+    ]
+    part = dot_last(far, far_ref[...])
+    part += jnp.concatenate([dot_last(near, own_ref[...]), dot_last(near, other_ref[...])], axis=1)
     total = jnp.zeros((probes, width), F32)
-    for index in range(ncols):
+    for index, place in enumerate(placing(ncols)):
+        where = pl.ds(pl.multiple_of(place * probes, probes), probes)
         first = jnp.zeros((probes, width), F32)
         for peer in range(parts_ref.shape[0]):
-            first += parts_ref[peer, index * probes:(index + 1) * probes, :].astype(F32)
+            first += parts_ref[peer, where, :].astype(F32)
         second = part[:, index * width:(index + 1) * width] * factor
-        out_ref[index, :probes, :] = second
+        out_ref[place, :probes, :] = second
         total += first * second
     right, image = right_ref[...], image_ref[...]
     products = (right * right, right * image, image * image, total * factor)
@@ -222,24 +244,27 @@
     )
     right = held(right)
     near = exchange(rows, ("x", "z"))
-    cols = features[None]
-    for axis in COLS:
-        cols = lax.all_gather(cols, axis, axis=0, tiled=True)
-    order = [sum(((place >> bit) & 1) << (len(COLS) - 1 - bit) for bit in range(len(COLS))) for place in range(ny)]
-    inverse, cols = call(
-        functools.partial(columns, order), lengthscale.reshape(1, feats), cols,
-        outs=[shaped(F32, feats, width), shaped(BF16, ny * width, feats + EXTRA)],
-    )
+    raw = features[None]
+    for axis in COLS[:2]:
+        raw = lax.all_gather(raw, axis, axis=0, tiled=True)
+    other = lax.ppermute(raw, COLS[2], swap)
+    middle = ny // 2 * width
+    held_cols = shaped(BF16, middle, feats + EXTRA)
+    inverse, cols = call(columns, lengthscale.reshape(1, feats), raw, outs=[shaped(F32, feats, width), held_cols])
     near, inverse, cols = lax.optimization_barrier((near, inverse, cols))
     far = lax.ppermute(near, "core", swap)
-    tile = pltpu.VMEM((ny * width, plane * width), BF16)
-    scratch = [pltpu.VMEM((feats + EXTRA, plane * width), BF16)]
-    tile_near, sums = call(
-        near_product, inverse, cols, near, outs=[tile, shaped(F32, ny, probes, width)], limit=24, scratch=scratch
+    tile = pltpu.VMEM((middle, plane * width), BF16)
+    wide = shaped(BF16, feats + EXTRA, plane * width)
+    sums = shaped(F32, probes, middle)
+    tile_own, sums_own, rows = call(own_near, inverse, cols, near, outs=[tile, sums, wide], limit=24)
+    tile_other, sums_other, more = call(
+        other_near, inverse, other, near, rows, outs=[tile, sums, held_cols], limit=24
     )
     tile_far, parts = call(
-        far_product, inverse, cols, far, sums, outs=[tile, shaped(BF16, ny, (ny + 1) * probes, width)],
-        limit=24, scratch=scratch,
+        far_product, inverse, cols, more, far, sums_own, sums_other,
+        outs=[pltpu.VMEM((2 * middle, plane * width), BF16), shaped(BF16, ny, (ny + 1) * probes, width)],
+        limit=24,
+        scratch=[pltpu.VMEM(wide.shape, BF16), pltpu.VMEM((2 * middle, feats + EXTRA), BF16)],
     )
     parts = exchange(parts, COLS)
     image, rows = call(
@@ -247,7 +272,7 @@
     )
     both = lax.all_gather(exchange(rows, ("x", "z")), "core")
     sums = call(
-        functools.partial(second_product, factor), held(tile_near), held(tile_far), both, parts, right, image,
+        functools.partial(second_product, factor), held(tile_own), held(tile_other), held(tile_far), both, parts, right, image,
         outs=shaped(F32, ny, probes + PAD, width),
     )
     second, local = call(gathered, exchange(sums, COLS), outs=[block, shaped(F32, plane * ncore, width)])

time: 121 us -> 119 us (0.983)
  blocking collectives: 82.7 us -> 73.8 us
  starting transfers between devices: 19.8 us -> 23.8 us
  waiting for transfers between devices: 0.01 us -> 3.28 us
    all_to_all x4, blocking collectives: 62.3 us -> 55.5 us  [exchange(): return lax.all_to_all(values, axes, 0, 0, tiled=True)]
    all_gather x3 -> x2, blocking collectives: 16.3 us -> 12.2 us  [per_device(): raw = lax.all_gather(raw, axis, axis=0, tiled=True)]
    all_to_all x1, waiting for transfers between devices: 0.01 us -> 3.27 us  [exchange(): return lax.all_to_all(values, axes, 0, 0, tiled=True)]
    ppermute x0 -> x1, starting transfers between devices: none -> 3.2 us  [per_device(): other = lax.ppermute(raw, COLS[2], swap)]
    all_gather x1, blocking collectives: 4.05 us -> 6.11 us  [per_device(): both = lax.all_gather(exchange(rows, ('x', 'z')), 'core')]
    pallas_call x8 -> x9, Pallas kernels: 16.3 us -> 16.5 us  [call(): pl.pallas_call(kernel, in_specs=specs or [VMEM] * len(args), out_specs=ja...]
  transfers between devices with their start and end apart: 2 -> 3, of which waited for: 0 -> 1; matrix products, arithmetic and copies ran while one was open for 0% -> 0% of each run, Pallas kernels for 4% -> 4%
where the time goes in v9:
time: 119 us
  blocking collectives  73.8 us (62%)
  starting transfers between devices  23.8 us (20%)
  Pallas kernels  16.5 us (14%)
  waiting for transfers between devices  3.28 us (3%)
    all_to_all x4, blocking collectives, exchange(): return lax.all_to_all(values, axes, 0, 0, tiled=True)  55.5 us
    pallas_call x9, Pallas kernels, call(): pl.pallas_call(kernel, in_specs=specs or [VMEM] * len(args), out_specs=ja...  16.5 us
    all_to_all x1, starting transfers between devices, exchange(): return lax.all_to_all(values, axes, 0, 0, tiled=True)  13.7 us
    all_gather x2, blocking collectives, per_device(): raw = lax.all_gather(raw, axis, axis=0, tiled=True)  12.2 us
    ppermute x1, starting transfers between devices, per_device(): far = lax.ppermute(near, 'core', swap)  6.91 us
    all_gather x1, blocking collectives, per_device(): both = lax.all_gather(exchange(rows, ('x', 'z')), 'core')  6.11 us
    all_to_all x1, waiting for transfers between devices, exchange(): return lax.all_to_all(values, axes, 0, 0, tiled=True)  3.27 us
    ppermute x1, starting transfers between devices, per_device(): other = lax.ppermute(raw, COLS[2], swap)  3.2 us
  transfers between devices with their start and end apart: 3, of which 1 were waited for; matrix products, arithmetic and copies ran while one was open for 0% of the time, Pallas kernels for 4%

profile of v9, /device:TPU:1, one launch (start us, length us, event | category | flops | bytes accessed | tf_op | source)
XLA Modules:
  0.0 118.8 jit_solution(4952576418832822571)
XLA Ops:
  0.6 1.7 %shard_map.50 = (bf16[32,80,128]{2,1,0:T(8,128)(2,1)}, f32[16,128]{1,0:T(8,128)S(1)}) custom-call(bf16[64,128]{1,0:T(8,128)(2,1)} %features_ref.1, f32[16,128]{1,0:T(8,128)} %right_ref.1), custom_call_target="tpu_custom_call" | custom-call | tf_op jit(solution)/shard_map/pallas_call | solution.py:19
  2.3 13.7 %all-to-all-start = ((bf16[32,80,128]{2,1,0:T(8,128)(2,1)}), bf16[32,80,128]{2,1,0:T(8,128)(2,1)S(1)}, u32[]{:S(2)}, u32[]{:S(2)}) async-start(bf16[32,80,128]{2,1,0:T(8,128)(2,1)} %get-tuple-element.21), calls=%async_computation | async-start | bytes 1310720 | tf_op jit(solution)/shard_map/all_to_all | solution.py:233
  16.0 7.6 %all-gather = bf16[128,128]{1,0:T(8,128)(2,1)S(1)} all-gather(bf16[64,128]{1,0:T(8,128)(2,1)} %features_ref.1), channel_id=2, replica_groups=mesh['x'=4,'z'=8,'core'=2,'ya'=2,'yb'=2,'yc'=2] {'ya'}, dimensions={0}, use_global_device_ids=true | all-gather | bytes 49152 | tf_op jit(solution)/shard_map/all_gather | solution.py:249
  23.6 4.6 %all_gather.13.cols_ref = bf16[4,64,128]{2,1,0:T(8,128)(2,1)S(1)} all-gather(bf16[2,64,128]{2,1,0:T(8,128)(2,1)S(1)} %bitcast.11), channel_id=1, replica_groups=mesh['x'=4,'z'=8,'core'=2,'ya'=2,'yb'=2,'yc'=2] {'yb'}, dimensions={0}, use_global_device_ids=true | all-gather | bytes 98304 | tf_op jit(solution)/shard_map/all_gather | solution.py:249
  28.3 0.0 copy-start
  28.3 0.7 copy-done
  28.9 0.2 shard_map.51
  29.1 3.3 %all-to-all-done.near_ref = bf16[32,80,128]{2,1,0:T(8,128)(2,1)S(1)} async-done(((bf16[32,80,128]{2,1,0:T(8,128)(2,1)}), bf16[32,80,128]{2,1,0:T(8,128)(2,1)S(1)}, u32[]{:S(2)}, u32[]{:S(2)}) %all-to-all-start) | async-done | bytes 655392 | tf_op jit(solution)/shard_map/all_to_all | solution.py:233
  32.4 6.9 %collective-permute-start.1 = (bf16[32,80,128]{2,1,0:T(8,128)(2,1)S(1)}, bf16[32,80,128]{2,1,0:T(8,128)(2,1)S(1)}, u32[]{:S(2)}, u32[]{:S(2)}) collective-permute-start(bf16[32,80,128]{2,1,0:T(8,128)(2,1)S(1)} %all-to-all-done.near_ref), channel_id=1, source_target_pairs={{0,8},{8,0},{1,9},{9,1},{2,10},{10,2},{3,11},{11,3},{4,12},{12,4},... | collective-permute-start | bytes 1966088 | tf_op jit(solution)/shard_map/ppermute | solution.py:255
  39.3 3.2 %collective-permute-start = (bf16[4,64,128]{2,1,0:T(8,128)(2,1)S(1)}, bf16[4,64,128]{2,1,0:T(8,128)(2,1)S(1)}, u32[]{:S(2)}, u32[]{:S(2)}) collective-permute-start(bf16[4,64,128]{2,1,0:T(8,128)(2,1)S(1)} %all_gather.13.cols_ref), channel_id=1, source_target_pairs={{0,1},{1,0},{2,3},{3,2},{4,5},{5,4},{6,7},{7,6},{8,9},{9,8},{10,11... | collective-permute-start | bytes 196616 | tf_op jit(solution)/shard_map/ppermute | solution.py:250
  42.5 2.4 %shard_map.52 = (bf16[512,4096]{1,0:T(8,128)(2,1)S(1)}, f32[16,512]{1,0:T(8,128)S(1)}, bf16[80,4096]{1,0:T(8,128)(2,1)S(1)}) custom-call(f32[64,128]{1,0:T(8,128)S(1)} %get-tuple-element.24.inverse_ref, bf16[512,80]{1,0:T(8,128)(2,1)S(1)} %get-tuple-element.25.cols_ref.own_ref, bf16[32,80,128]{2,1,0:T(8,128)(2,1)S(1)} %all-to-all-done.near_ref), custom_call_target="tpu_custom_call" | custom-call | tf_op jit(solution)/shard_map/pallas_call | solution.py:19
  44.9 0.0 collective-permute-done.raw_ref
  44.9 2.4 %shard_map.53 = (bf16[512,4096]{1,0:T(8,128)(2,1)S(1)}, f32[16,512]{1,0:T(8,128)S(1)}, bf16[512,80]{1,0:T(8,128)(2,1)S(1)}) custom-call(f32[64,128]{1,0:T(8,128)S(1)} %get-tuple-element.24.inverse_ref, bf16[4,64,128]{2,1,0:T(8,128)(2,1)S(1)} %collective-permute-done.raw_ref, bf16[32,80,128]{2,1,0:T(8,128)(2,1)S(1)} %all-to-all-done.near_ref, ...), custom_call_target="tpu_custom_call" | custom-call | tf_op jit(solution)/shard_map/pallas_call | solution.py:19
  47.3 0.0 collective-permute-done.1.far_ref
  47.3 4.6 %shard_map.54 = (bf16[1024,4096]{1,0:T(8,128)(2,1)S(1)}, bf16[8,144,128]{2,1,0:T(8,128)(2,1)S(1)}) custom-call(f32[64,128]{1,0:T(8,128)S(1)} %get-tuple-element.24.inverse_ref, bf16[512,80]{1,0:T(8,128)(2,1)S(1)} %get-tuple-element.25.cols_ref.own_ref, bf16[512,80]{1,0:T(8,128)(2,1)S(1)} %get-tuple-element.30.other_ref, ...), custom_call_target="tpu_custom_call" | custom-call | tf_op jit(solution)/shard_map/pallas_call | solution.py:19
  51.9 17.3 %all_to_all.31.parts_ref = bf16[8,144,128]{2,1,0:T(8,128)(2,1)S(1)} all-to-all(bf16[8,144,128]{2,1,0:T(8,128)(2,1)S(1)} %get-tuple-element.34), channel_id=1, replica_groups=mesh['x'=4,'z'=8,'core'=2,'ya'=2,'yb'=2,'yc'=2] {'ya','yb','yc'}, dimensions={0} | all-to-all | bytes 589824 | tf_op jit(solution)/shard_map/all_to_all | solution.py:233
  69.2 13.5 %all_to_all.32 = bf16[32,16,128]{2,1,0:T(8,128)(2,1)S(1)} all-to-all(bf16[32,16,128]{2,1,0:T(8,128)(2,1)S(1)} %get-tuple-element.35), channel_id=1, replica_groups=mesh['x'=4,'z'=8,'core'=2,'ya'=2,'yb'=2,'yc'=2] {'x','z'}, dimensions={0} | all-to-all | bytes 262144 | tf_op jit(solution)/shard_map/all_to_all | solution.py:233
  82.8 6.1 %all-gather.1 = bf16[64,16,128]{2,1,0:T(8,128)(2,1)S(1)} all-gather(bf16[32,16,128]{2,1,0:T(8,128)(2,1)S(1)} %all_to_all.32), channel_id=3, replica_groups=mesh['x'=4,'z'=8,'core'=2,'ya'=2,'yb'=2,'yc'=2] {'core'}, dimensions={0}, use_global_device_ids=true | all-gather | bytes 393216 | tf_op jit(solution)/shard_map/all_gather | solution.py:273
  88.9 4.5 %shard_map.56 = f32[8,24,128]{2,1,0:T(8,128)S(1)} custom-call(bf16[512,4096]{1,0:T(8,128)(2,1)S(1)} %get-tuple-element.27.own_ref, bf16[512,4096]{1,0:T(8,128)(2,1)S(1)} %get-tuple-element.29.other_ref, bf16[1024,4096]{1,0:T(8,128)(2,1)S(1)} %get-tuple-element.33.far_ref, bf16[2,32,16,128]{3,2,1,0:T(8,128)(2,1)S(1)} %bitcast.7, ...), custom_call_target="tpu_custom_call" | custom-call | tf_op jit(solution)/shard_map/pallas_call | solution.py:19
  93.4 10.0 %all_to_all.33.parts_ref = f32[8,24,128]{2,1,0:T(8,128)S(1)} all-to-all(f32[8,24,128]{2,1,0:T(8,128)S(1)} %shard_map.56), channel_id=1, replica_groups=mesh['x'=4,'z'=8,'core'=2,'ya'=2,'yb'=2,'yc'=2] {'ya','yb','yc'}, dimensions={0} | all-to-all | bytes 196608 | tf_op jit(solution)/shard_map/all_to_all | solution.py:233
  103.4 14.7 %all_to_all.34 = f32[64,1,128]{2,1,0:T(1,128)S(1)} all-to-all(f32[64,1,128]{2,1,0:T(1,128)S(1)} %bitcast.9), channel_id=1, replica_groups=mesh['x'=4,'z'=8,'core'=2,'ya'=2,'yb'=2,'yc'=2] {'x','z','core'}, dimensions={0} | all-to-all | bytes 65536 | tf_op jit(solution)/shard_map/all_to_all | solution.py:233
  118.1 0.7 shard_map.58
  (2 shorter events, 0.0 us)
Async XLA Ops:
  2.3 30.1 %all-to-all-start = ((bf16[32,80,128]{2,1,0:T(8,128)(2,1)}), bf16[32,80,128]{2,1,0:T(8,128)(2,1)S(1)}, u32[]{:S(2)}, u32[]{:S(2)}) async-start(bf16[32,80,128]{2,1,0:T(8,128)(2,1)} %get-tuple-element.21), calls=%async_computation | async-start | bytes 1310720 | tf_op jit(solution)/shard_map/all_to_all | solution.py:233
  28.3 0.7 copy-start
  32.4 14.9 %collective-permute-start.1 = (bf16[32,80,128]{2,1,0:T(8,128)(2,1)S(1)}, bf16[32,80,128]{2,1,0:T(8,128)(2,1)S(1)}, u32[]{:S(2)}, u32[]{:S(2)}) collective-permute-start(bf16[32,80,128]{2,1,0:T(8,128)(2,1)S(1)} %all-to-all-done.near_ref), channel_id=1, source_target_pairs={{0,8},{8,0},{1,9},{9,1},{2,10},{10,2},{3,11},{11,3},{4,12},{12,4},... | collective-permute-start | bytes 1966088 | tf_op jit(solution)/shard_map/ppermute | solution.py:255
  39.3 5.6 %collective-permute-start = (bf16[4,64,128]{2,1,0:T(8,128)(2,1)S(1)}, bf16[4,64,128]{2,1,0:T(8,128)(2,1)S(1)}, u32[]{:S(2)}, u32[]{:S(2)}) collective-permute-start(bf16[4,64,128]{2,1,0:T(8,128)(2,1)S(1)} %all_gather.13.cols_ref), channel_id=1, source_target_pairs={{0,1},{1,0},{2,3},{3,2},{4,5},{5,4},{6,7},{7,6},{8,9},{9,8},{10,11... | collective-permute-start | bytes 196616 | tf_op jit(solution)/shard_map/ppermute | solution.py:250

commit v10 on v8

--- a/solution.py
+++ b/solution.py
@@ -65,14 +65,17 @@
         rows_ref[index, feats:, :] = right
 
 
-def columns(order, scale_ref, cols_ref, inverse_ref, out_ref):
+def columns(scale_ref, cols_ref, inverse_ref, out_ref):
     ncols, feats, width = cols_ref.shape
     lane = lax.broadcasted_iota(jnp.int32, (feats, feats), 1)
     row = lax.broadcasted_iota(jnp.int32, (feats, feats), 0)
     scale = jnp.sum(jnp.where(lane == row, scale_ref[...], 0.0), axis=1, keepdims=True)
     inverse = jnp.broadcast_to(1.0 / scale, (feats, width))
     inverse_ref[...] = inverse
-    for place, index in enumerate(order):
+    ya, yb = [lax.axis_index(axis) for axis in COLS[:2]]
+    for index in range(ncols):
+        first, middle, last = index // 4, index // 2 % 2, index % 2
+        place = last * 4 + (1 - ya if first else ya) * 2 + (1 - yb if middle else yb)
         block = augmented(cols_ref[place], inverse, 0).astype(F32)
         out_ref[index * width:(index + 1) * width, :] = jnp.transpose(block).astype(BF16)
 
@@ -222,12 +225,12 @@
     )
     right = held(right)
     near = exchange(rows, ("x", "z"))
-    cols = features[None]
-    for axis in COLS:
-        cols = lax.all_gather(cols, axis, axis=0, tiled=True)
-    order = [sum(((place >> bit) & 1) << (len(COLS) - 1 - bit) for bit in range(len(COLS))) for place in range(ny)]
+    cols = jnp.stack([features] + [
+        lax.ppermute(features, COLS[:2], [(index, index ^ other) for index in range(4)]) for other in (1, 2, 3)
+    ])
+    cols = lax.all_gather(cols, COLS[2], axis=0, tiled=True)
     inverse, cols = call(
-        functools.partial(columns, order), lengthscale.reshape(1, feats), cols,
+        columns, lengthscale.reshape(1, feats), cols,
         outs=[shaped(F32, feats, width), shaped(BF16, ny * width, feats + EXTRA)],
     )
     near, inverse, cols = lax.optimization_barrier((near, inverse, cols))

time: 121 us -> 123 us (1.017)
  blocking collectives: 82.7 us -> 66.1 us
  starting transfers between devices: 19.8 us -> 31 us
  waiting for transfers between devices: 0.01 us -> 6.73 us
    all_gather x3 -> x1, blocking collectives: 16.3 us -> 3.79 us  [per_device(): cols = lax.all_gather(cols, COLS[2], axis=0, tiled=True)]
    ppermute x0 -> x3, starting transfers between devices: none -> 11.8 us  [per_device(): lax.ppermute(features, COLS[:2], [(index, index ^ other) for index in ran...]
    ppermute x0 -> x3, waiting for transfers between devices: none -> 6.72 us  [per_device(): lax.ppermute(features, COLS[:2], [(index, index ^ other) for index in ran...]
    all_to_all x4, blocking collectives: 62.3 us -> 58.3 us  [exchange(): return lax.all_to_all(values, axes, 0, 0, tiled=True)]
  transfers between devices with their start and end apart: 2 -> 5, of which waited for: 0 -> 1; matrix products, arithmetic and copies ran while one was open for 0% -> 1% of each run, Pallas kernels for 4% -> 4%
where the time goes in v10:
time: 123 us; the launch traced here: 122 us
  blocking collectives  66.1 us (54%)
  starting transfers between devices  31 us (25%)
  Pallas kernels  16.3 us (13%)
  waiting for transfers between devices  6.73 us (5%)
    all_to_all x4, blocking collectives, exchange(): return lax.all_to_all(values, axes, 0, 0, tiled=True)  58.3 us
    pallas_call x8, Pallas kernels, call(): pl.pallas_call(kernel, in_specs=specs or [VMEM] * len(args), out_specs=ja...  16.3 us
    all_to_all x1, starting transfers between devices, exchange(): return lax.all_to_all(values, axes, 0, 0, tiled=True)  13.7 us
    ppermute x3, starting transfers between devices, per_device(): lax.ppermute(features, COLS[:2], [(index, index ^ other) for index in ran...  11.8 us
    ppermute x3, waiting for transfers between devices, per_device(): lax.ppermute(features, COLS[:2], [(index, index ^ other) for index in ran...  6.72 us
    ppermute x1, starting transfers between devices, per_device(): far = lax.ppermute(near, 'core', swap)  5.46 us
    all_gather x1, blocking collectives, per_device(): both = lax.all_gather(exchange(rows, ('x', 'z')), 'core')  4.02 us
    all_gather x1, blocking collectives, per_device(): cols = lax.all_gather(cols, COLS[2], axis=0, tiled=True)  3.79 us
  transfers between devices with their start and end apart: 5, of which 1 were waited for; matrix products, arithmetic and copies ran while one was open for 1% of the time, Pallas kernels for 4%

profile of v10, /device:TPU:1, one launch (start us, length us, event | category | flops | bytes accessed | tf_op | source)
XLA Modules:
  0.0 122.3 jit_solution(10952324933739905281)
XLA Ops:
  0.6 1.7 %shard_map.50 = (bf16[32,80,128]{2,1,0:T(8,128)(2,1)}, f32[16,128]{1,0:T(8,128)S(1)}) custom-call(bf16[64,128]{1,0:T(8,128)(2,1)} %features_ref.1, f32[16,128]{1,0:T(8,128)} %right_ref.1), custom_call_target="tpu_custom_call" | custom-call | tf_op jit(solution)/shard_map/pallas_call | solution.py:20
  2.3 13.7 %all-to-all-start = ((bf16[32,80,128]{2,1,0:T(8,128)(2,1)}), bf16[32,80,128]{2,1,0:T(8,128)(2,1)S(1)}, u32[]{:S(2)}, u32[]{:S(2)}) async-start(bf16[32,80,128]{2,1,0:T(8,128)(2,1)} %get-tuple-element.17), calls=%async_computation | async-start | bytes 1310720 | tf_op jit(solution)/shard_map/all_to_all | solution.py:214
  16.0 4.2 %collective-permute-start = (bf16[64,128]{1,0:T(8,128)(2,1)}, bf16[64,128]{1,0:T(8,128)(2,1)S(1)}, u32[]{:S(2)}, u32[]{:S(2)}) collective-permute-start(bf16[64,128]{1,0:T(8,128)(2,1)} %features_ref.1), channel_id=1, source_target_pairs={{0,2},{2,0},{4,6},{6,4},{1,3},{3,1},{5,7},{7,5},{8,10},{10,8},{12,... | collective-permute-start | bytes 49160 | tf_op jit(solution)/shard_map/ppermute | solution.py:229
  20.3 5.4 %collective-permute-start.2 = (bf16[64,128]{1,0:T(8,128)(2,1)}, bf16[64,128]{1,0:T(8,128)(2,1)S(1)}, u32[]{:S(2)}, u32[]{:S(2)}) collective-permute-start(bf16[64,128]{1,0:T(8,128)(2,1)} %features_ref.1), channel_id=1, source_target_pairs={{0,6},{2,4},{4,2},{6,0},{1,7},{3,5},{5,3},{7,1},{8,14},{10,12},{12... | collective-permute-start | bytes 49160 | tf_op jit(solution)/shard_map/ppermute | solution.py:229
  25.7 2.2 %collective-permute-start.1 = (bf16[64,128]{1,0:T(8,128)(2,1)}, bf16[64,128]{1,0:T(8,128)(2,1)S(1)}, u32[]{:S(2)}, u32[]{:S(2)}) collective-permute-start(bf16[64,128]{1,0:T(8,128)(2,1)} %features_ref.1), channel_id=1, source_target_pairs={{0,4},{2,6},{4,0},{6,2},{1,5},{3,7},{5,1},{7,3},{8,12},{10,14},{12... | collective-permute-start | bytes 49160 | tf_op jit(solution)/shard_map/ppermute | solution.py:229
  27.8 0.0 collective-permute-done
  27.9 0.0 collective-permute-done.2
  27.9 6.7 %collective-permute-done.1 = bf16[64,128]{1,0:T(8,128)(2,1)S(1)} collective-permute-done((bf16[64,128]{1,0:T(8,128)(2,1)}, bf16[64,128]{1,0:T(8,128)(2,1)S(1)}, u32[]{:S(2)}, u32[]{:S(2)}) %collective-permute-start.1) | collective-permute-done | bytes 16416 | tf_op jit(solution)/shard_map/ppermute | solution.py:229
  34.6 0.7 pad_maximum_fusion
  35.3 3.8 %all_gather.9.cols_ref = bf16[8,64,128]{2,1,0:T(8,128)(2,1)S(1)} all-gather(bf16[4,64,128]{2,1,0:T(8,128)(2,1)S(1)} %pad_maximum_fusion), channel_id=1, replica_groups=mesh['x'=4,'z'=8,'core'=2,'ya'=2,'yb'=2,'yc'=2] {'yc'}, dimensions={0}, use_global_device_ids=true | all-gather | bytes 196608 | tf_op jit(solution)/shard_map/all_gather | solution.py:231
  39.1 0.0 copy-start
  39.1 0.7 copy-done
  39.8 0.2 shard_map.51
  40.0 0.0 all-to-all-done.rows_ref
  40.0 5.5 %collective-permute-start.3 = (bf16[32,80,128]{2,1,0:T(8,128)(2,1)S(1)}, bf16[32,80,128]{2,1,0:T(8,128)(2,1)S(1)}, u32[]{:S(2)}, u32[]{:S(2)}) collective-permute-start(bf16[32,80,128]{2,1,0:T(8,128)(2,1)S(1)} %all-to-all-done.rows_ref), channel_id=1, source_target_pairs={{0,8},{8,0},{1,9},{9,1},{2,10},{10,2},{3,11},{11,3},{4,12},{12,4},... | collective-permute-start | bytes 1966088 | tf_op jit(solution)/shard_map/ppermute | solution.py:237
  45.5 4.6 %shard_map.52 = (bf16[1024,4096]{1,0:T(8,128)(2,1)S(1)}, f32[8,16,128]{2,1,0:T(8,128)S(1)}) custom-call(f32[64,128]{1,0:T(8,128)S(1)} %get-tuple-element.20.inverse_ref, bf16[1024,80]{1,0:T(8,128)(2,1)S(1)} %get-tuple-element.21.cols_ref, bf16[32,80,128]{2,1,0:T(8,128)(2,1)S(1)} %all-to-all-done.rows_ref), custom_call_target="tpu_custom_call" | custom-call | tf_op jit(solution)/shard_map/pallas_call | solution.py:20
  50.1 0.0 collective-permute-done.3.rows_ref
  50.1 4.6 %shard_map.53 = (bf16[1024,4096]{1,0:T(8,128)(2,1)S(1)}, bf16[8,144,128]{2,1,0:T(8,128)(2,1)S(1)}) custom-call(f32[64,128]{1,0:T(8,128)S(1)} %get-tuple-element.20.inverse_ref, bf16[1024,80]{1,0:T(8,128)(2,1)S(1)} %get-tuple-element.21.cols_ref, bf16[32,80,128]{2,1,0:T(8,128)(2,1)S(1)} %collective-permute-done.3.rows_ref, ...), custom_call_target="tpu_custom_call" | custom-call | tf_op jit(solution)/shard_map/pallas_call | solution.py:20
  54.7 15.1 %all_to_all.31.parts_ref = bf16[8,144,128]{2,1,0:T(8,128)(2,1)S(1)} all-to-all(bf16[8,144,128]{2,1,0:T(8,128)(2,1)S(1)} %get-tuple-element.26), channel_id=1, replica_groups=mesh['x'=4,'z'=8,'core'=2,'ya'=2,'yb'=2,'yc'=2] {'ya','yb','yc'}, dimensions={0} | all-to-all | bytes 589824 | tf_op jit(solution)/shard_map/all_to_all | solution.py:214
  69.8 18.5 %all_to_all.32 = bf16[32,16,128]{2,1,0:T(8,128)(2,1)S(1)} all-to-all(bf16[32,16,128]{2,1,0:T(8,128)(2,1)S(1)} %get-tuple-element.27), channel_id=1, replica_groups=mesh['x'=4,'z'=8,'core'=2,'ya'=2,'yb'=2,'yc'=2] {'x','z'}, dimensions={0} | all-to-all | bytes 262144 | tf_op jit(solution)/shard_map/all_to_all | solution.py:214
  88.3 4.0 %all-gather = bf16[64,16,128]{2,1,0:T(8,128)(2,1)S(1)} all-gather(bf16[32,16,128]{2,1,0:T(8,128)(2,1)S(1)} %all_to_all.32), channel_id=2, replica_groups=mesh['x'=4,'z'=8,'core'=2,'ya'=2,'yb'=2,'yc'=2] {'core'}, dimensions={0}, use_global_device_ids=true | all-gather | bytes 393216 | tf_op jit(solution)/shard_map/all_gather | solution.py:251
  92.3 4.5 %shard_map.55 = f32[8,24,128]{2,1,0:T(8,128)S(1)} custom-call(bf16[1024,4096]{1,0:T(8,128)(2,1)S(1)} %get-tuple-element.23.near_ref, bf16[1024,4096]{1,0:T(8,128)(2,1)S(1)} %get-tuple-element.25.far_ref, bf16[2,32,16,128]{3,2,1,0:T(8,128)(2,1)S(1)} %bitcast.10, bf16[8,144,128]{2,1,0:T(8,128)(2,1)S(1)} %all_to_all.31.parts_ref, ...), custom_call_target="tpu_custom_call" | custom-call | tf_op jit(solution)/shard_map/pallas_call | solution.py:20
  96.8 10.0 %all_to_all.33.parts_ref = f32[8,24,128]{2,1,0:T(8,128)S(1)} all-to-all(f32[8,24,128]{2,1,0:T(8,128)S(1)} %shard_map.55), channel_id=1, replica_groups=mesh['x'=4,'z'=8,'core'=2,'ya'=2,'yb'=2,'yc'=2] {'ya','yb','yc'}, dimensions={0} | all-to-all | bytes 196608 | tf_op jit(solution)/shard_map/all_to_all | solution.py:214
  106.8 14.7 %all_to_all.34 = f32[64,1,128]{2,1,0:T(1,128)S(1)} all-to-all(f32[64,1,128]{2,1,0:T(1,128)S(1)} %bitcast.12), channel_id=1, replica_groups=mesh['x'=4,'z'=8,'core'=2,'ya'=2,'yb'=2,'yc'=2] {'x','z','core'}, dimensions={0} | all-to-all | bytes 65536 | tf_op jit(solution)/shard_map/all_to_all | solution.py:214
  121.5 0.7 shard_map.57
  (2 shorter events, 0.0 us)
Async XLA Ops:
  2.3 37.7 %all-to-all-start = ((bf16[32,80,128]{2,1,0:T(8,128)(2,1)}), bf16[32,80,128]{2,1,0:T(8,128)(2,1)S(1)}, u32[]{:S(2)}, u32[]{:S(2)}) async-start(bf16[32,80,128]{2,1,0:T(8,128)(2,1)} %get-tuple-element.17), calls=%async_computation | async-start | bytes 1310720 | tf_op jit(solution)/shard_map/all_to_all | solution.py:214
  16.0 11.8 %collective-permute-start = (bf16[64,128]{1,0:T(8,128)(2,1)}, bf16[64,128]{1,0:T(8,128)(2,1)S(1)}, u32[]{:S(2)}, u32[]{:S(2)}) collective-permute-start(bf16[64,128]{1,0:T(8,128)(2,1)} %features_ref.1), channel_id=1, source_target_pairs={{0,2},{2,0},{4,6},{6,4},{1,3},{3,1},{5,7},{7,5},{8,10},{10,8},{12,... | collective-permute-start | bytes 49160 | tf_op jit(solution)/shard_map/ppermute | solution.py:229
  20.3 7.6 %collective-permute-start.2 = (bf16[64,128]{1,0:T(8,128)(2,1)}, bf16[64,128]{1,0:T(8,128)(2,1)S(1)}, u32[]{:S(2)}, u32[]{:S(2)}) collective-permute-start(bf16[64,128]{1,0:T(8,128)(2,1)} %features_ref.1), channel_id=1, source_target_pairs={{0,6},{2,4},{4,2},{6,0},{1,7},{3,5},{5,3},{7,1},{8,14},{10,12},{12... | collective-permute-start | bytes 49160 | tf_op jit(solution)/shard_map/ppermute | solution.py:229
  25.7 8.9 %collective-permute-start.1 = (bf16[64,128]{1,0:T(8,128)(2,1)}, bf16[64,128]{1,0:T(8,128)(2,1)S(1)}, u32[]{:S(2)}, u32[]{:S(2)}) collective-permute-start(bf16[64,128]{1,0:T(8,128)(2,1)} %features_ref.1), channel_id=1, source_target_pairs={{0,4},{2,6},{4,0},{6,2},{1,5},{3,7},{5,1},{7,3},{8,12},{10,14},{12... | collective-permute-start | bytes 49160 | tf_op jit(solution)/shard_map/ppermute | solution.py:229
  39.1 0.7 copy-start
  40.0 10.0 %collective-permute-start.3 = (bf16[32,80,128]{2,1,0:T(8,128)(2,1)S(1)}, bf16[32,80,128]{2,1,0:T(8,128)(2,1)S(1)}, u32[]{:S(2)}, u32[]{:S(2)}) collective-permute-start(bf16[32,80,128]{2,1,0:T(8,128)(2,1)S(1)} %all-to-all-done.rows_ref), channel_id=1, source_target_pairs={{0,8},{8,0},{1,9},{9,1},{2,10},{10,2},{3,11},{11,3},{4,12},{12,4},... | collective-permute-start | bytes 1966088 | tf_op jit(solution)/shard_map/ppermute | solution.py:237

commit v11 on v8

--- a/solution.py
+++ b/solution.py
@@ -49,10 +49,11 @@
     return jnp.concatenate([scaled, below.astype(BF16)], axis=0)
 
 
-def row_copies(features_ref, right_ref, rows_ref, kept_ref, held, sems):
+def row_copies(features_ref, right_ref, scale_ref, rows_ref, kept_ref, inverse_ref, held, scales, sems):
     moves = [
         pltpu.make_async_copy(features_ref, held, sems.at[0]),
         pltpu.make_async_copy(right_ref, kept_ref, sems.at[1]),
+        pltpu.make_async_copy(scale_ref, scales, sems.at[2]),
     ]
     for move in moves:
         move.start()
@@ -63,17 +64,16 @@
     for index in range(rows_ref.shape[0]):
         rows_ref[index, :feats, :] = features
         rows_ref[index, feats:, :] = right
-
-
-def columns(order, scale_ref, cols_ref, inverse_ref, out_ref):
-    ncols, feats, width = cols_ref.shape
     lane = lax.broadcasted_iota(jnp.int32, (feats, feats), 1)
     row = lax.broadcasted_iota(jnp.int32, (feats, feats), 0)
-    scale = jnp.sum(jnp.where(lane == row, scale_ref[...], 0.0), axis=1, keepdims=True)
-    inverse = jnp.broadcast_to(1.0 / scale, (feats, width))
-    inverse_ref[...] = inverse
+    scale = jnp.sum(jnp.where(lane == row, scales[...], 0.0), axis=1, keepdims=True)
+    inverse_ref[...] = jnp.broadcast_to(1.0 / scale, inverse_ref.shape)
+
+
+def columns(order, inverse_ref, cols_ref, out_ref):
+    width = cols_ref.shape[2]
     for place, index in enumerate(order):
-        block = augmented(cols_ref[place], inverse, 0).astype(F32)
+        block = augmented(cols_ref[place], inverse_ref[...], 0).astype(F32)
         out_ref[index * width:(index + 1) * width, :] = jnp.transpose(block).astype(BF16)
 
 
@@ -213,24 +213,28 @@
     def held(array):
         return pltpu.with_memory_space_constraint(array, pltpu.VMEM)
 
-    source, given = [pltpu.with_memory_space_constraint(array, pltpu.HBM) for array in (features, right_side)]
+    given = [
+        pltpu.with_memory_space_constraint(array, pltpu.HBM)
+        for array in (features, right_side, lengthscale.reshape(1, feats))
+    ]
     far_off = pl.BlockSpec(memory_space=pltpu.HBM)
-    rows, right = call(
-        row_copies, source, given, specs=[far_off] * 2,
-        outs=[shaped(BF16, plane, feats + probes, width), pltpu.VMEM(block.shape, F32)],
-        scratch=[pltpu.VMEM(features.shape, BF16), pltpu.SemaphoreType.DMA((2,))],
-    )
-    right = held(right)
+    rows, right, inverse = call(
+        row_copies, *given, specs=[far_off] * 3,
+        outs=[
+            shaped(BF16, plane, feats + probes, width), pltpu.VMEM(block.shape, F32), pltpu.VMEM((feats, width), F32),
+        ],
+        scratch=[pltpu.VMEM(features.shape, BF16), pltpu.VMEM((1, feats), F32), pltpu.SemaphoreType.DMA((3,))],
+    )
+    right, inverse = held(right), held(inverse)
     near = exchange(rows, ("x", "z"))
     cols = features[None]
     for axis in COLS:
         cols = lax.all_gather(cols, axis, axis=0, tiled=True)
     order = [sum(((place >> bit) & 1) << (len(COLS) - 1 - bit) for bit in range(len(COLS))) for place in range(ny)]
-    inverse, cols = call(
-        functools.partial(columns, order), lengthscale.reshape(1, feats), cols,
-        outs=[shaped(F32, feats, width), shaped(BF16, ny * width, feats + EXTRA)],
-    )
-    near, inverse, cols = lax.optimization_barrier((near, inverse, cols))
+    cols = call(
+        functools.partial(columns, order), inverse, cols, outs=shaped(BF16, ny * width, feats + EXTRA)
+    )
+    near, cols = lax.optimization_barrier((near, cols))
     far = lax.ppermute(near, "core", swap)
     tile = pltpu.VMEM((ny * width, plane * width), BF16)
     scratch = [pltpu.VMEM((feats + EXTRA, plane * width), BF16)]

time: 121 us -> 120 us (level)
  no operation moved by 1% of the time
where the time goes in v11:
time: 120 us; the launch traced here: 119 us
  blocking collectives  81.9 us (68%)
  starting transfers between devices  20.5 us (17%)
  Pallas kernels  16.3 us (14%)
    all_to_all x4, blocking collectives, exchange(): return lax.all_to_all(values, axes, 0, 0, tiled=True)  61.6 us
    all_gather x3, blocking collectives, per_device(): cols = lax.all_gather(cols, axis, axis=0, tiled=True)  16.3 us
    pallas_call x8, Pallas kernels, call(): pl.pallas_call(kernel, in_specs=specs or [VMEM] * len(args), out_specs=ja...  16.3 us
    all_to_all x1, starting transfers between devices, exchange(): return lax.all_to_all(values, axes, 0, 0, tiled=True)  13.7 us
    ppermute x1, starting transfers between devices, per_device(): far = lax.ppermute(near, 'core', swap)  6.8 us
    all_gather x1, blocking collectives, per_device(): both = lax.all_gather(exchange(rows, ('x', 'z')), 'core')  4.05 us
  transfers between devices with their start and end apart: 2, of which 0 were waited for; matrix products, arithmetic and copies ran while one was open for 0% of the time, Pallas kernels for 4%

profile of v11, /device:TPU:1, one launch (start us, length us, event | category | flops | bytes accessed | tf_op | source)
XLA Modules:
  0.0 119.4 jit_solution(13300962706293632632)
XLA Ops:
  0.6 1.7 %shard_map.50 = (bf16[32,80,128]{2,1,0:T(8,128)(2,1)}, f32[16,128]{1,0:T(8,128)S(1)}, f32[64,128]{1,0:T(8,128)S(1)}) custom-call(bf16[64,128]{1,0:T(8,128)(2,1)} %features_ref.1, f32[16,128]{1,0:T(8,128)} %right_ref.1, f32[1,64]{1,0:T(1,128)} %bitcast.11), custom_call_target="tpu_custom_call" | custom-call | tf_op jit(solution)/shard_map/pallas_call | solution.py:20
  2.3 13.7 %all-to-all-start = ((bf16[32,80,128]{2,1,0:T(8,128)(2,1)}), bf16[32,80,128]{2,1,0:T(8,128)(2,1)S(1)}, u32[]{:S(2)}, u32[]{:S(2)}) async-start(bf16[32,80,128]{2,1,0:T(8,128)(2,1)} %get-tuple-element.16), calls=%async_computation | async-start | bytes 1310720 | tf_op jit(solution)/shard_map/all_to_all | solution.py:211
  16.0 7.6 %all-gather = bf16[128,128]{1,0:T(8,128)(2,1)S(1)} all-gather(bf16[64,128]{1,0:T(8,128)(2,1)} %features_ref.1), channel_id=2, replica_groups=mesh['x'=4,'z'=8,'core'=2,'ya'=2,'yb'=2,'yc'=2] {'ya'}, dimensions={0}, use_global_device_ids=true | all-gather | bytes 49152 | tf_op jit(solution)/shard_map/all_gather | solution.py:232
  23.7 4.6 %all_gather.16 = bf16[4,64,128]{2,1,0:T(8,128)(2,1)S(1)} all-gather(bf16[2,64,128]{2,1,0:T(8,128)(2,1)S(1)} %bitcast.10), channel_id=1, replica_groups=mesh['x'=4,'z'=8,'core'=2,'ya'=2,'yb'=2,'yc'=2] {'yb'}, dimensions={0}, use_global_device_ids=true | all-gather | bytes 98304 | tf_op jit(solution)/shard_map/all_gather | solution.py:232
  28.3 4.1 %all_gather.17.cols_ref = bf16[8,64,128]{2,1,0:T(8,128)(2,1)S(1)} all-gather(bf16[4,64,128]{2,1,0:T(8,128)(2,1)S(1)} %all_gather.16), channel_id=1, replica_groups=mesh['x'=4,'z'=8,'core'=2,'ya'=2,'yb'=2,'yc'=2] {'yc'}, dimensions={0}, use_global_device_ids=true | all-gather | bytes 196608 | tf_op jit(solution)/shard_map/all_gather | solution.py:232
  32.4 0.2 shard_map.51.cols_ref
  32.5 0.0 all-to-all-done.rows_ref
  32.5 6.8 %collective-permute-start = (bf16[32,80,128]{2,1,0:T(8,128)(2,1)S(1)}, bf16[32,80,128]{2,1,0:T(8,128)(2,1)S(1)}, u32[]{:S(2)}, u32[]{:S(2)}) collective-permute-start(bf16[32,80,128]{2,1,0:T(8,128)(2,1)S(1)} %all-to-all-done.rows_ref), channel_id=1, source_target_pairs={{0,8},{8,0},{1,9},{9,1},{2,10},{10,2},{3,11},{11,3},{4,12},{12,4},... | collective-permute-start | bytes 1966088 | tf_op jit(solution)/shard_map/ppermute | solution.py:238
  39.3 4.6 %shard_map.52 = (bf16[1024,4096]{1,0:T(8,128)(2,1)S(1)}, f32[8,16,128]{2,1,0:T(8,128)S(1)}) custom-call(f32[64,128]{1,0:T(8,128)S(1)} %get-tuple-element.15.inverse_ref, bf16[1024,80]{1,0:T(8,128)(2,1)S(1)} %shard_map.51.cols_ref, bf16[32,80,128]{2,1,0:T(8,128)(2,1)S(1)} %all-to-all-done.rows_ref), custom_call_target="tpu_custom_call" | custom-call | tf_op jit(solution)/shard_map/pallas_call | solution.py:20
  43.9 0.0 collective-permute-done.rows_ref
  43.9 4.6 %shard_map.53 = (bf16[1024,4096]{1,0:T(8,128)(2,1)S(1)}, bf16[8,144,128]{2,1,0:T(8,128)(2,1)S(1)}) custom-call(f32[64,128]{1,0:T(8,128)S(1)} %get-tuple-element.15.inverse_ref, bf16[1024,80]{1,0:T(8,128)(2,1)S(1)} %shard_map.51.cols_ref, bf16[32,80,128]{2,1,0:T(8,128)(2,1)S(1)} %collective-permute-done.rows_ref, f32[8,16,128]{2,1,0:T(8,128)S(1)} %get-tuple-element.20.sums_ref), custom_call_target="tpu_custom_call" | custom-call | tf_op jit(solution)/shard_map/pallas_call | solution.py:20
  48.5 19.3 %all_to_all.31.parts_ref = bf16[8,144,128]{2,1,0:T(8,128)(2,1)S(1)} all-to-all(bf16[8,144,128]{2,1,0:T(8,128)(2,1)S(1)} %get-tuple-element.22), channel_id=1, replica_groups=mesh['x'=4,'z'=8,'core'=2,'ya'=2,'yb'=2,'yc'=2] {'ya','yb','yc'}, dimensions={0} | all-to-all | bytes 589824 | tf_op jit(solution)/shard_map/all_to_all | solution.py:211
  67.9 17.5 %all_to_all.32 = bf16[32,16,128]{2,1,0:T(8,128)(2,1)S(1)} all-to-all(bf16[32,16,128]{2,1,0:T(8,128)(2,1)S(1)} %get-tuple-element.23), channel_id=1, replica_groups=mesh['x'=4,'z'=8,'core'=2,'ya'=2,'yb'=2,'yc'=2] {'x','z'}, dimensions={0} | all-to-all | bytes 262144 | tf_op jit(solution)/shard_map/all_to_all | solution.py:211
  85.4 4.0 %all-gather.1 = bf16[64,16,128]{2,1,0:T(8,128)(2,1)S(1)} all-gather(bf16[32,16,128]{2,1,0:T(8,128)(2,1)S(1)} %all_to_all.32), channel_id=3, replica_groups=mesh['x'=4,'z'=8,'core'=2,'ya'=2,'yb'=2,'yc'=2] {'core'}, dimensions={0}, use_global_device_ids=true | all-gather | bytes 393216 | tf_op jit(solution)/shard_map/all_gather | solution.py:252
  89.4 4.5 %shard_map.55 = f32[8,24,128]{2,1,0:T(8,128)S(1)} custom-call(bf16[1024,4096]{1,0:T(8,128)(2,1)S(1)} %get-tuple-element.19.near_ref, bf16[1024,4096]{1,0:T(8,128)(2,1)S(1)} %get-tuple-element.21.far_ref, bf16[2,32,16,128]{3,2,1,0:T(8,128)(2,1)S(1)} %bitcast.7, bf16[8,144,128]{2,1,0:T(8,128)(2,1)S(1)} %all_to_all.31.parts_ref, ...), custom_call_target="tpu_custom_call" | custom-call | tf_op jit(solution)/shard_map/pallas_call | solution.py:20
  93.9 10.0 %all_to_all.33.parts_ref = f32[8,24,128]{2,1,0:T(8,128)S(1)} all-to-all(f32[8,24,128]{2,1,0:T(8,128)S(1)} %shard_map.55), channel_id=1, replica_groups=mesh['x'=4,'z'=8,'core'=2,'ya'=2,'yb'=2,'yc'=2] {'ya','yb','yc'}, dimensions={0} | all-to-all | bytes 196608 | tf_op jit(solution)/shard_map/all_to_all | solution.py:211
  103.9 14.7 %all_to_all.34 = f32[64,1,128]{2,1,0:T(1,128)S(1)} all-to-all(f32[64,1,128]{2,1,0:T(1,128)S(1)} %bitcast.9), channel_id=1, replica_groups=mesh['x'=4,'z'=8,'core'=2,'ya'=2,'yb'=2,'yc'=2] {'x','z','core'}, dimensions={0} | all-to-all | bytes 65536 | tf_op jit(solution)/shard_map/all_to_all | solution.py:211
  118.7 0.7 shard_map.57
  (2 shorter events, 0.0 us)
Async XLA Ops:
  2.3 30.2 %all-to-all-start = ((bf16[32,80,128]{2,1,0:T(8,128)(2,1)}), bf16[32,80,128]{2,1,0:T(8,128)(2,1)S(1)}, u32[]{:S(2)}, u32[]{:S(2)}) async-start(bf16[32,80,128]{2,1,0:T(8,128)(2,1)} %get-tuple-element.16), calls=%async_computation | async-start | bytes 1310720 | tf_op jit(solution)/shard_map/all_to_all | solution.py:211
  32.5 11.4 %collective-permute-start = (bf16[32,80,128]{2,1,0:T(8,128)(2,1)S(1)}, bf16[32,80,128]{2,1,0:T(8,128)(2,1)S(1)}, u32[]{:S(2)}, u32[]{:S(2)}) collective-permute-start(bf16[32,80,128]{2,1,0:T(8,128)(2,1)S(1)} %all-to-all-done.rows_ref), channel_id=1, source_target_pairs={{0,8},{8,0},{1,9},{9,1},{2,10},{10,2},{3,11},{11,3},{4,12},{12,4},... | collective-permute-start | bytes 1966088 | tf_op jit(solution)/shard_map/ppermute | solution.py:238

commit v12 on v9

--- a/solution.py
+++ b/solution.py
@@ -48,10 +48,11 @@
     return jnp.concatenate([scaled, below.astype(BF16)], axis=0)
 
 
-def row_copies(features_ref, right_ref, rows_ref, kept_ref, held, sems):
+def row_copies(features_ref, right_ref, scale_ref, rows_ref, kept_ref, inverse_ref, held, scales, sems):
     moves = [
         pltpu.make_async_copy(features_ref, held, sems.at[0]),
         pltpu.make_async_copy(right_ref, kept_ref, sems.at[1]),
+        pltpu.make_async_copy(scale_ref, scales, sems.at[2]),
     ]
     for move in moves:
         move.start()
@@ -62,6 +63,10 @@
     for index in range(rows_ref.shape[0]):
         rows_ref[index, :feats, :] = features
         rows_ref[index, feats:, :] = right
+    lane = lax.broadcasted_iota(jnp.int32, (feats, feats), 1)
+    row = lax.broadcasted_iota(jnp.int32, (feats, feats), 0)
+    scale = jnp.sum(jnp.where(lane == row, scales[...], 0.0), axis=1, keepdims=True)
+    inverse_ref[...] = jnp.broadcast_to(1.0 / scale, inverse_ref.shape)
 
 
 def put_columns(cols_ref, inverse, out_ref):
@@ -71,14 +76,8 @@
         out_ref[index * width:(index + 1) * width, :] = jnp.transpose(block).astype(BF16)
 
 
-def columns(scale_ref, cols_ref, inverse_ref, out_ref):
-    _, feats, width = cols_ref.shape
-    lane = lax.broadcasted_iota(jnp.int32, (feats, feats), 1)
-    row = lax.broadcasted_iota(jnp.int32, (feats, feats), 0)
-    scale = jnp.sum(jnp.where(lane == row, scale_ref[...], 0.0), axis=1, keepdims=True)
-    inverse = jnp.broadcast_to(1.0 / scale, (feats, width))
-    inverse_ref[...] = inverse
-    put_columns(cols_ref, inverse, out_ref)
+def columns(inverse_ref, cols_ref, out_ref):
+    put_columns(cols_ref, inverse_ref[...], out_ref)
 
 
 def dot_last(left, right):
@@ -235,14 +234,19 @@
     def held(array):
         return pltpu.with_memory_space_constraint(array, pltpu.VMEM)
 
-    source, given = [pltpu.with_memory_space_constraint(array, pltpu.HBM) for array in (features, right_side)]
+    given = [
+        pltpu.with_memory_space_constraint(array, pltpu.HBM)
+        for array in (features, right_side, lengthscale.reshape(1, feats))
+    ]
     far_off = pl.BlockSpec(memory_space=pltpu.HBM)
-    rows, right = call(
-        row_copies, source, given, specs=[far_off] * 2,
-        outs=[shaped(BF16, plane, feats + probes, width), pltpu.VMEM(block.shape, F32)],
-        scratch=[pltpu.VMEM(features.shape, BF16), pltpu.SemaphoreType.DMA((2,))],
-    )
-    right = held(right)
+    rows, right, inverse = call(
+        row_copies, *given, specs=[far_off] * 3,
+        outs=[
+            shaped(BF16, plane, feats + probes, width), pltpu.VMEM(block.shape, F32), pltpu.VMEM((feats, width), F32),
+        ],
+        scratch=[pltpu.VMEM(features.shape, BF16), pltpu.VMEM((1, feats), F32), pltpu.SemaphoreType.DMA((3,))],
+    )
+    right, inverse = held(right), held(inverse)
     near = exchange(rows, ("x", "z"))
     raw = features[None]
     for axis in COLS[:2]:
@@ -250,8 +254,8 @@
     other = lax.ppermute(raw, COLS[2], swap)
     middle = ny // 2 * width
     held_cols = shaped(BF16, middle, feats + EXTRA)
-    inverse, cols = call(columns, lengthscale.reshape(1, feats), raw, outs=[shaped(F32, feats, width), held_cols])
-    near, inverse, cols = lax.optimization_barrier((near, inverse, cols))
+    cols = call(columns, inverse, raw, outs=held_cols)
+    near, cols = lax.optimization_barrier((near, cols))
     far = lax.ppermute(near, "core", swap)
     tile = pltpu.VMEM((middle, plane * width), BF16)
     wide = shaped(BF16, feats + EXTRA, plane * width)

time: 119 us -> 119 us (level)
  no operation moved by 1% of the time
where the time goes in v12:
time: 119 us
  blocking collectives  73.8 us (62%)
  starting transfers between devices  23.8 us (20%)
  Pallas kernels  16.4 us (14%)
  waiting for transfers between devices  4.01 us (3%)
    all_to_all x4, blocking collectives, exchange(): return lax.all_to_all(values, axes, 0, 0, tiled=True)  55.5 us
    pallas_call x9, Pallas kernels, call(): pl.pallas_call(kernel, in_specs=specs or [VMEM] * len(args), out_specs=ja...  16.4 us
    all_to_all x1, starting transfers between devices, exchange(): return lax.all_to_all(values, axes, 0, 0, tiled=True)  13.7 us
    all_gather x2, blocking collectives, per_device(): raw = lax.all_gather(raw, axis, axis=0, tiled=True)  12.2 us
    ppermute x1, starting transfers between devices, per_device(): far = lax.ppermute(near, 'core', swap)  6.91 us
    all_gather x1, blocking collectives, per_device(): both = lax.all_gather(exchange(rows, ('x', 'z')), 'core')  6.11 us
    all_to_all x1, waiting for transfers between devices, exchange(): return lax.all_to_all(values, axes, 0, 0, tiled=True)  4.01 us
    ppermute x1, starting transfers between devices, per_device(): other = lax.ppermute(raw, COLS[2], swap)  3.2 us
  transfers between devices with their start and end apart: 3, of which 1 were waited for; matrix products, arithmetic and copies ran while one was open for 0% of the time, Pallas kernels for 4%

profile of v12, /device:TPU:1, one launch (start us, length us, event | category | flops | bytes accessed | tf_op | source)
XLA Modules:
  0.0 118.8 jit_solution(16066344099091604722)
XLA Ops:
  0.6 1.7 %shard_map.50 = (bf16[32,80,128]{2,1,0:T(8,128)(2,1)}, f32[16,128]{1,0:T(8,128)S(1)}, f32[64,128]{1,0:T(8,128)S(1)}) custom-call(bf16[64,128]{1,0:T(8,128)(2,1)} %features_ref.1, f32[16,128]{1,0:T(8,128)} %right_ref.1, f32[1,64]{1,0:T(1,128)} %bitcast.11), custom_call_target="tpu_custom_call" | custom-call | tf_op jit(solution)/shard_map/pallas_call | solution.py:19
  2.3 13.7 %all-to-all-start = ((bf16[32,80,128]{2,1,0:T(8,128)(2,1)}), bf16[32,80,128]{2,1,0:T(8,128)(2,1)S(1)}, u32[]{:S(2)}, u32[]{:S(2)}) async-start(bf16[32,80,128]{2,1,0:T(8,128)(2,1)} %get-tuple-element.20), calls=%async_computation | async-start | bytes 1310720 | tf_op jit(solution)/shard_map/all_to_all | solution.py:232
  16.0 7.6 %all-gather = bf16[128,128]{1,0:T(8,128)(2,1)S(1)} all-gather(bf16[64,128]{1,0:T(8,128)(2,1)} %features_ref.1), channel_id=2, replica_groups=mesh['x'=4,'z'=8,'core'=2,'ya'=2,'yb'=2,'yc'=2] {'ya'}, dimensions={0}, use_global_device_ids=true | all-gather | bytes 49152 | tf_op jit(solution)/shard_map/all_gather | solution.py:253
  23.7 4.6 %all_gather.13.cols_ref = bf16[4,64,128]{2,1,0:T(8,128)(2,1)S(1)} all-gather(bf16[2,64,128]{2,1,0:T(8,128)(2,1)S(1)} %bitcast.10), channel_id=1, replica_groups=mesh['x'=4,'z'=8,'core'=2,'ya'=2,'yb'=2,'yc'=2] {'yb'}, dimensions={0}, use_global_device_ids=true | all-gather | bytes 98304 | tf_op jit(solution)/shard_map/all_gather | solution.py:253
  28.3 0.1 shard_map.51.cols_ref.own_ref
  28.4 4.0 %all-to-all-done.near_ref = bf16[32,80,128]{2,1,0:T(8,128)(2,1)S(1)} async-done(((bf16[32,80,128]{2,1,0:T(8,128)(2,1)}), bf16[32,80,128]{2,1,0:T(8,128)(2,1)S(1)}, u32[]{:S(2)}, u32[]{:S(2)}) %all-to-all-start) | async-done | bytes 655392 | tf_op jit(solution)/shard_map/all_to_all | solution.py:232
  32.4 6.9 %collective-permute-start.1 = (bf16[32,80,128]{2,1,0:T(8,128)(2,1)S(1)}, bf16[32,80,128]{2,1,0:T(8,128)(2,1)S(1)}, u32[]{:S(2)}, u32[]{:S(2)}) collective-permute-start(bf16[32,80,128]{2,1,0:T(8,128)(2,1)S(1)} %all-to-all-done.near_ref), channel_id=1, source_target_pairs={{0,8},{8,0},{1,9},{9,1},{2,10},{10,2},{3,11},{11,3},{4,12},{12,4},... | collective-permute-start | bytes 1966088 | tf_op jit(solution)/shard_map/ppermute | solution.py:259
  39.3 3.2 %collective-permute-start = (bf16[4,64,128]{2,1,0:T(8,128)(2,1)S(1)}, bf16[4,64,128]{2,1,0:T(8,128)(2,1)S(1)}, u32[]{:S(2)}, u32[]{:S(2)}) collective-permute-start(bf16[4,64,128]{2,1,0:T(8,128)(2,1)S(1)} %all_gather.13.cols_ref), channel_id=1, source_target_pairs={{0,1},{1,0},{2,3},{3,2},{4,5},{5,4},{6,7},{7,6},{8,9},{9,8},{10,11... | collective-permute-start | bytes 196616 | tf_op jit(solution)/shard_map/ppermute | solution.py:254
  42.5 2.4 %shard_map.52 = (bf16[512,4096]{1,0:T(8,128)(2,1)S(1)}, f32[16,512]{1,0:T(8,128)S(1)}, bf16[80,4096]{1,0:T(8,128)(2,1)S(1)}) custom-call(f32[64,128]{1,0:T(8,128)S(1)} %get-tuple-element.19.inverse_ref, bf16[512,80]{1,0:T(8,128)(2,1)S(1)} %shard_map.51.cols_ref.own_ref, bf16[32,80,128]{2,1,0:T(8,128)(2,1)S(1)} %all-to-all-done.near_ref), custom_call_target="tpu_custom_call" | custom-call | tf_op jit(solution)/shard_map/pallas_call | solution.py:19
  44.9 0.0 collective-permute-done.raw_ref
  45.0 2.4 %shard_map.53 = (bf16[512,4096]{1,0:T(8,128)(2,1)S(1)}, f32[16,512]{1,0:T(8,128)S(1)}, bf16[512,80]{1,0:T(8,128)(2,1)S(1)}) custom-call(f32[64,128]{1,0:T(8,128)S(1)} %get-tuple-element.19.inverse_ref, bf16[4,64,128]{2,1,0:T(8,128)(2,1)S(1)} %collective-permute-done.raw_ref, bf16[32,80,128]{2,1,0:T(8,128)(2,1)S(1)} %all-to-all-done.near_ref, ...), custom_call_target="tpu_custom_call" | custom-call | tf_op jit(solution)/shard_map/pallas_call | solution.py:19
  47.3 0.0 collective-permute-done.1.far_ref
  47.3 4.6 %shard_map.54 = (bf16[1024,4096]{1,0:T(8,128)(2,1)S(1)}, bf16[8,144,128]{2,1,0:T(8,128)(2,1)S(1)}) custom-call(f32[64,128]{1,0:T(8,128)S(1)} %get-tuple-element.19.inverse_ref, bf16[512,80]{1,0:T(8,128)(2,1)S(1)} %shard_map.51.cols_ref.own_ref, bf16[512,80]{1,0:T(8,128)(2,1)S(1)} %get-tuple-element.26.other_ref, ...), custom_call_target="tpu_custom_call" | custom-call | tf_op jit(solution)/shard_map/pallas_call | solution.py:19
  52.0 17.3 %all_to_all.31.parts_ref = bf16[8,144,128]{2,1,0:T(8,128)(2,1)S(1)} all-to-all(bf16[8,144,128]{2,1,0:T(8,128)(2,1)S(1)} %get-tuple-element.30), channel_id=1, replica_groups=mesh['x'=4,'z'=8,'core'=2,'ya'=2,'yb'=2,'yc'=2] {'ya','yb','yc'}, dimensions={0} | all-to-all | bytes 589824 | tf_op jit(solution)/shard_map/all_to_all | solution.py:232
  69.2 13.5 %all_to_all.32 = bf16[32,16,128]{2,1,0:T(8,128)(2,1)S(1)} all-to-all(bf16[32,16,128]{2,1,0:T(8,128)(2,1)S(1)} %get-tuple-element.31), channel_id=1, replica_groups=mesh['x'=4,'z'=8,'core'=2,'ya'=2,'yb'=2,'yc'=2] {'x','z'}, dimensions={0} | all-to-all | bytes 262144 | tf_op jit(solution)/shard_map/all_to_all | solution.py:232
  82.8 6.1 %all-gather.1 = bf16[64,16,128]{2,1,0:T(8,128)(2,1)S(1)} all-gather(bf16[32,16,128]{2,1,0:T(8,128)(2,1)S(1)} %all_to_all.32), channel_id=3, replica_groups=mesh['x'=4,'z'=8,'core'=2,'ya'=2,'yb'=2,'yc'=2] {'core'}, dimensions={0}, use_global_device_ids=true | all-gather | bytes 393216 | tf_op jit(solution)/shard_map/all_gather | solution.py:277
  88.9 4.5 %shard_map.56 = f32[8,24,128]{2,1,0:T(8,128)S(1)} custom-call(bf16[512,4096]{1,0:T(8,128)(2,1)S(1)} %get-tuple-element.23.own_ref, bf16[512,4096]{1,0:T(8,128)(2,1)S(1)} %get-tuple-element.25.other_ref, bf16[1024,4096]{1,0:T(8,128)(2,1)S(1)} %get-tuple-element.29.far_ref, bf16[2,32,16,128]{3,2,1,0:T(8,128)(2,1)S(1)} %bitcast.7, ...), custom_call_target="tpu_custom_call" | custom-call | tf_op jit(solution)/shard_map/pallas_call | solution.py:19
  93.4 10.0 %all_to_all.33.parts_ref = f32[8,24,128]{2,1,0:T(8,128)S(1)} all-to-all(f32[8,24,128]{2,1,0:T(8,128)S(1)} %shard_map.56), channel_id=1, replica_groups=mesh['x'=4,'z'=8,'core'=2,'ya'=2,'yb'=2,'yc'=2] {'ya','yb','yc'}, dimensions={0} | all-to-all | bytes 196608 | tf_op jit(solution)/shard_map/all_to_all | solution.py:232
  103.4 14.7 %all_to_all.34 = f32[64,1,128]{2,1,0:T(1,128)S(1)} all-to-all(f32[64,1,128]{2,1,0:T(1,128)S(1)} %bitcast.9), channel_id=1, replica_groups=mesh['x'=4,'z'=8,'core'=2,'ya'=2,'yb'=2,'yc'=2] {'x','z','core'}, dimensions={0} | all-to-all | bytes 65536 | tf_op jit(solution)/shard_map/all_to_all | solution.py:232
  118.1 0.7 shard_map.58
  (2 shorter events, 0.0 us)
Async XLA Ops:
  2.3 30.1 %all-to-all-start = ((bf16[32,80,128]{2,1,0:T(8,128)(2,1)}), bf16[32,80,128]{2,1,0:T(8,128)(2,1)S(1)}, u32[]{:S(2)}, u32[]{:S(2)}) async-start(bf16[32,80,128]{2,1,0:T(8,128)(2,1)} %get-tuple-element.20), calls=%async_computation | async-start | bytes 1310720 | tf_op jit(solution)/shard_map/all_to_all | solution.py:232
  32.4 14.9 %collective-permute-start.1 = (bf16[32,80,128]{2,1,0:T(8,128)(2,1)S(1)}, bf16[32,80,128]{2,1,0:T(8,128)(2,1)S(1)}, u32[]{:S(2)}, u32[]{:S(2)}) collective-permute-start(bf16[32,80,128]{2,1,0:T(8,128)(2,1)S(1)} %all-to-all-done.near_ref), channel_id=1, source_target_pairs={{0,8},{8,0},{1,9},{9,1},{2,10},{10,2},{3,11},{11,3},{4,12},{12,4},... | collective-permute-start | bytes 1966088 | tf_op jit(solution)/shard_map/ppermute | solution.py:259
  39.3 5.6 %collective-permute-start = (bf16[4,64,128]{2,1,0:T(8,128)(2,1)S(1)}, bf16[4,64,128]{2,1,0:T(8,128)(2,1)S(1)}, u32[]{:S(2)}, u32[]{:S(2)}) collective-permute-start(bf16[4,64,128]{2,1,0:T(8,128)(2,1)S(1)} %all_gather.13.cols_ref), channel_id=1, source_target_pairs={{0,1},{1,0},{2,3},{3,2},{4,5},{5,4},{6,7},{7,6},{8,9},{9,8},{10,11... | collective-permute-start | bytes 196616 | tf_op jit(solution)/shard_map/ppermute | solution.py:254

commit v13 on v9

--- a/solution.py
+++ b/solution.py
@@ -165,7 +165,7 @@
     probes, width = right_ref.shape
     me = lax.axis_index("core")
     near, far = [
-        jnp.concatenate([rows_ref[half, index] for index in range(rows_ref.shape[1])], axis=1) for half in (me, 1 - me)
+        jnp.concatenate([rows_ref[index + half] for index in range(0, rows_ref.shape[0], 2)], axis=1) for half in (me, 1 - me)
     ]
     part = dot_last(far, far_ref[...])
     part += jnp.concatenate([dot_last(near, own_ref[...]), dot_last(near, other_ref[...])], axis=1)
@@ -268,9 +268,9 @@
     )
     parts = exchange(parts, COLS)
     image, rows = call(
-        functools.partial(spread, factor), parts, outs=[block, shaped(BF16, plane, probes, width)]
-    )
-    both = lax.all_gather(exchange(rows, ("x", "z")), "core")
+        functools.partial(spread, factor), parts, outs=[block, shaped(BF16, plane * ncore, probes, width)]
+    )
+    both = exchange(rows, ("x", "z", "core"))
     sums = call(
         functools.partial(second_product, factor), held(tile_own), held(tile_other), held(tile_far), both, parts, right, image,
         outs=shaped(F32, ny, probes + PAD, width),

time: 119 us -> 121 us (1.017)
  blocking collectives: 73.8 us -> 75.5 us
    all_to_all x4, blocking collectives: 55.5 us -> 63.2 us  [exchange(): return lax.all_to_all(values, axes, 0, 0, tiled=True)]
    all_gather x1 -> x0, blocking collectives: 6.11 us -> none  [per_device(): both = lax.all_gather(exchange(rows, ('x', 'z')), 'core')]
where the time goes in v13:
time: 121 us; the launch traced here: 120 us
  blocking collectives  75.5 us (62%)
  starting transfers between devices  23.8 us (20%)
  Pallas kernels  16.5 us (14%)
  waiting for transfers between devices  3.28 us (3%)
    all_to_all x4, blocking collectives, exchange(): return lax.all_to_all(values, axes, 0, 0, tiled=True)  63.2 us
    pallas_call x9, Pallas kernels, call(): pl.pallas_call(kernel, in_specs=specs or [VMEM] * len(args), out_specs=ja...  16.5 us
    all_to_all x1, starting transfers between devices, exchange(): return lax.all_to_all(values, axes, 0, 0, tiled=True)  13.7 us
    all_gather x2, blocking collectives, per_device(): raw = lax.all_gather(raw, axis, axis=0, tiled=True)  12.2 us
    ppermute x1, starting transfers between devices, per_device(): far = lax.ppermute(near, 'core', swap)  6.91 us
    all_to_all x1, waiting for transfers between devices, exchange(): return lax.all_to_all(values, axes, 0, 0, tiled=True)  3.27 us
    ppermute x1, starting transfers between devices, per_device(): other = lax.ppermute(raw, COLS[2], swap)  3.2 us
  transfers between devices with their start and end apart: 3, of which 1 were waited for; matrix products, arithmetic and copies ran while one was open for 0% of the time, Pallas kernels for 4%

profile of v13, /device:TPU:1, one launch (start us, length us, event | category | flops | bytes accessed | tf_op | source)
XLA Modules:
  0.0 120.4 jit_solution(13334596808654274296)
XLA Ops:
  0.6 1.7 %shard_map.50 = (bf16[32,80,128]{2,1,0:T(8,128)(2,1)}, f32[16,128]{1,0:T(8,128)S(1)}) custom-call(bf16[64,128]{1,0:T(8,128)(2,1)} %features_ref.1, f32[16,128]{1,0:T(8,128)} %right_ref.1), custom_call_target="tpu_custom_call" | custom-call | tf_op jit(solution)/shard_map/pallas_call | solution.py:19
  2.3 13.7 %all-to-all-start = ((bf16[32,80,128]{2,1,0:T(8,128)(2,1)}), bf16[32,80,128]{2,1,0:T(8,128)(2,1)S(1)}, u32[]{:S(2)}, u32[]{:S(2)}) async-start(bf16[32,80,128]{2,1,0:T(8,128)(2,1)} %get-tuple-element.21), calls=%async_computation | async-start | bytes 1310720 | tf_op jit(solution)/shard_map/all_to_all | solution.py:233
  16.0 7.6 %all-gather = bf16[128,128]{1,0:T(8,128)(2,1)S(1)} all-gather(bf16[64,128]{1,0:T(8,128)(2,1)} %features_ref.1), channel_id=2, replica_groups=mesh['x'=4,'z'=8,'core'=2,'ya'=2,'yb'=2,'yc'=2] {'ya'}, dimensions={0}, use_global_device_ids=true | all-gather | bytes 49152 | tf_op jit(solution)/shard_map/all_gather | solution.py:249
  23.6 4.6 %all_gather.7.cols_ref = bf16[4,64,128]{2,1,0:T(8,128)(2,1)S(1)} all-gather(bf16[2,64,128]{2,1,0:T(8,128)(2,1)S(1)} %bitcast.9), channel_id=1, replica_groups=mesh['x'=4,'z'=8,'core'=2,'ya'=2,'yb'=2,'yc'=2] {'yb'}, dimensions={0}, use_global_device_ids=true | all-gather | bytes 98304 | tf_op jit(solution)/shard_map/all_gather | solution.py:249
  28.3 0.0 copy-start
  28.3 0.7 copy-done
  28.9 0.2 shard_map.51
  29.1 3.3 %all-to-all-done.near_ref = bf16[32,80,128]{2,1,0:T(8,128)(2,1)S(1)} async-done(((bf16[32,80,128]{2,1,0:T(8,128)(2,1)}), bf16[32,80,128]{2,1,0:T(8,128)(2,1)S(1)}, u32[]{:S(2)}, u32[]{:S(2)}) %all-to-all-start) | async-done | bytes 655392 | tf_op jit(solution)/shard_map/all_to_all | solution.py:233
  32.4 6.9 %collective-permute-start.1 = (bf16[32,80,128]{2,1,0:T(8,128)(2,1)S(1)}, bf16[32,80,128]{2,1,0:T(8,128)(2,1)S(1)}, u32[]{:S(2)}, u32[]{:S(2)}) collective-permute-start(bf16[32,80,128]{2,1,0:T(8,128)(2,1)S(1)} %all-to-all-done.near_ref), channel_id=1, source_target_pairs={{0,8},{8,0},{1,9},{9,1},{2,10},{10,2},{3,11},{11,3},{4,12},{12,4},... | collective-permute-start | bytes 1966088 | tf_op jit(solution)/shard_map/ppermute | solution.py:255
  39.3 3.2 %collective-permute-start = (bf16[4,64,128]{2,1,0:T(8,128)(2,1)S(1)}, bf16[4,64,128]{2,1,0:T(8,128)(2,1)S(1)}, u32[]{:S(2)}, u32[]{:S(2)}) collective-permute-start(bf16[4,64,128]{2,1,0:T(8,128)(2,1)S(1)} %all_gather.7.cols_ref), channel_id=1, source_target_pairs={{0,1},{1,0},{2,3},{3,2},{4,5},{5,4},{6,7},{7,6},{8,9},{9,8},{10,11... | collective-permute-start | bytes 196616 | tf_op jit(solution)/shard_map/ppermute | solution.py:250
  42.5 2.4 %shard_map.52 = (bf16[512,4096]{1,0:T(8,128)(2,1)S(1)}, f32[16,512]{1,0:T(8,128)S(1)}, bf16[80,4096]{1,0:T(8,128)(2,1)S(1)}) custom-call(f32[64,128]{1,0:T(8,128)S(1)} %get-tuple-element.24.inverse_ref, bf16[512,80]{1,0:T(8,128)(2,1)S(1)} %get-tuple-element.25.cols_ref.own_ref, bf16[32,80,128]{2,1,0:T(8,128)(2,1)S(1)} %all-to-all-done.near_ref), custom_call_target="tpu_custom_call" | custom-call | tf_op jit(solution)/shard_map/pallas_call | solution.py:19
  44.9 0.0 collective-permute-done.raw_ref
  44.9 2.4 %shard_map.53 = (bf16[512,4096]{1,0:T(8,128)(2,1)S(1)}, f32[16,512]{1,0:T(8,128)S(1)}, bf16[512,80]{1,0:T(8,128)(2,1)S(1)}) custom-call(f32[64,128]{1,0:T(8,128)S(1)} %get-tuple-element.24.inverse_ref, bf16[4,64,128]{2,1,0:T(8,128)(2,1)S(1)} %collective-permute-done.raw_ref, bf16[32,80,128]{2,1,0:T(8,128)(2,1)S(1)} %all-to-all-done.near_ref, ...), custom_call_target="tpu_custom_call" | custom-call | tf_op jit(solution)/shard_map/pallas_call | solution.py:19
  47.3 0.0 collective-permute-done.1.far_ref
  47.3 4.6 %shard_map.54 = (bf16[1024,4096]{1,0:T(8,128)(2,1)S(1)}, bf16[8,144,128]{2,1,0:T(8,128)(2,1)S(1)}) custom-call(f32[64,128]{1,0:T(8,128)S(1)} %get-tuple-element.24.inverse_ref, bf16[512,80]{1,0:T(8,128)(2,1)S(1)} %get-tuple-element.25.cols_ref.own_ref, bf16[512,80]{1,0:T(8,128)(2,1)S(1)} %get-tuple-element.30.other_ref, ...), custom_call_target="tpu_custom_call" | custom-call | tf_op jit(solution)/shard_map/pallas_call | solution.py:19
  51.9 17.3 %all_to_all.31.parts_ref = bf16[8,144,128]{2,1,0:T(8,128)(2,1)S(1)} all-to-all(bf16[8,144,128]{2,1,0:T(8,128)(2,1)S(1)} %get-tuple-element.34), channel_id=1, replica_groups=mesh['x'=4,'z'=8,'core'=2,'ya'=2,'yb'=2,'yc'=2] {'ya','yb','yc'}, dimensions={0} | all-to-all | bytes 589824 | tf_op jit(solution)/shard_map/all_to_all | solution.py:233
  69.3 19.7 %all_to_all.32.rows_ref = bf16[64,16,128]{2,1,0:T(8,128)(2,1)S(1)} all-to-all(bf16[64,16,128]{2,1,0:T(8,128)(2,1)S(1)} %get-tuple-element.35), channel_id=1, replica_groups=mesh['x'=4,'z'=8,'core'=2,'ya'=2,'yb'=2,'yc'=2] {'x','z','core'}, dimensions={0} | all-to-all | bytes 524288 | tf_op jit(solution)/shard_map/all_to_all | solution.py:233
  88.9 4.5 %shard_map.56 = f32[8,24,128]{2,1,0:T(8,128)S(1)} custom-call(bf16[512,4096]{1,0:T(8,128)(2,1)S(1)} %get-tuple-element.27.own_ref, bf16[512,4096]{1,0:T(8,128)(2,1)S(1)} %get-tuple-element.29.other_ref, bf16[1024,4096]{1,0:T(8,128)(2,1)S(1)} %get-tuple-element.33.far_ref, bf16[64,16,128]{2,1,0:T(8,128)(2,1)S(1)} %all_to_all.32.rows_ref, ...), custom_call_target="tpu_custom_call" | custom-call | tf_op jit(solution)/shard_map/pallas_call | solution.py:19
  93.4 9.9 %all_to_all.33.parts_ref = f32[8,24,128]{2,1,0:T(8,128)S(1)} all-to-all(f32[8,24,128]{2,1,0:T(8,128)S(1)} %shard_map.56), channel_id=1, replica_groups=mesh['x'=4,'z'=8,'core'=2,'ya'=2,'yb'=2,'yc'=2] {'ya','yb','yc'}, dimensions={0} | all-to-all | bytes 196608 | tf_op jit(solution)/shard_map/all_to_all | solution.py:233
  103.3 16.4 %all_to_all.34 = f32[64,1,128]{2,1,0:T(1,128)S(1)} all-to-all(f32[64,1,128]{2,1,0:T(1,128)S(1)} %bitcast.7), channel_id=1, replica_groups=mesh['x'=4,'z'=8,'core'=2,'ya'=2,'yb'=2,'yc'=2] {'x','z','core'}, dimensions={0} | all-to-all | bytes 65536 | tf_op jit(solution)/shard_map/all_to_all | solution.py:233
  119.7 0.7 shard_map.58
  (2 shorter events, 0.0 us)
Async XLA Ops:
  2.3 30.1 %all-to-all-start = ((bf16[32,80,128]{2,1,0:T(8,128)(2,1)}), bf16[32,80,128]{2,1,0:T(8,128)(2,1)S(1)}, u32[]{:S(2)}, u32[]{:S(2)}) async-start(bf16[32,80,128]{2,1,0:T(8,128)(2,1)} %get-tuple-element.21), calls=%async_computation | async-start | bytes 1310720 | tf_op jit(solution)/shard_map/all_to_all | solution.py:233
  28.3 0.7 copy-start
  32.4 14.9 %collective-permute-start.1 = (bf16[32,80,128]{2,1,0:T(8,128)(2,1)S(1)}, bf16[32,80,128]{2,1,0:T(8,128)(2,1)S(1)}, u32[]{:S(2)}, u32[]{:S(2)}) collective-permute-start(bf16[32,80,128]{2,1,0:T(8,128)(2,1)S(1)} %all-to-all-done.near_ref), channel_id=1, source_target_pairs={{0,8},{8,0},{1,9},{9,1},{2,10},{10,2},{3,11},{11,3},{4,12},{12,4},... | collective-permute-start | bytes 1966088 | tf_op jit(solution)/shard_map/ppermute | solution.py:255
  39.3 5.6 %collective-permute-start = (bf16[4,64,128]{2,1,0:T(8,128)(2,1)S(1)}, bf16[4,64,128]{2,1,0:T(8,128)(2,1)S(1)}, u32[]{:S(2)}, u32[]{:S(2)}) collective-permute-start(bf16[4,64,128]{2,1,0:T(8,128)(2,1)S(1)} %all_gather.7.cols_ref), channel_id=1, source_target_pairs={{0,1},{1,0},{2,3},{3,2},{4,5},{5,4},{6,7},{7,6},{8,9},{9,8},{10,11... | collective-permute-start | bytes 196616 | tf_op jit(solution)/shard_map/ppermute | solution.py:250

commit v14 on v12

--- a/solution.py
+++ b/solution.py
@@ -101,14 +101,9 @@
     return dot_last(vectors, tile)
 
 
-def own_near(inverse_ref, cols_ref, near_ref, tile_ref, sums_ref, rows_ref):
-    put_rows(near_ref, inverse_ref[...], rows_ref)
-    sums_ref[...] = tile_and_product(cols_ref, rows_ref, vectors_of(near_ref, inverse_ref.shape[0]), tile_ref)
-
-
-def other_near(inverse_ref, raw_ref, near_ref, rows_ref, tile_ref, sums_ref, cols_ref):
-    put_columns(raw_ref, inverse_ref[...], cols_ref)
-    sums_ref[...] = tile_and_product(cols_ref, rows_ref, vectors_of(near_ref, inverse_ref.shape[0]), tile_ref)
+def own_half(inverse_ref, cols_ref, rows_in_ref, tile_ref, sums_ref, rows_ref):
+    put_rows(rows_in_ref, inverse_ref[...], rows_ref)
+    sums_ref[...] = tile_and_product(cols_ref, rows_ref, vectors_of(rows_in_ref, inverse_ref.shape[0]), tile_ref)
 
 
 def placing(ncols):
@@ -117,16 +112,18 @@
     return [index % half * 2 + (me if index < half else 1 - me) for index in range(ncols)]
 
 
-def far_product(inverse_ref, own_ref, other_ref, far_ref, own_sums_ref, other_sums_ref, tile_ref, out_ref, rows, cols):
-    probes = own_sums_ref.shape[0]
+def other_half(
+    inverse_ref, raw_ref, near_ref, far_ref, near_rows_ref, far_rows_ref, near_sums_ref, far_sums_ref,
+    near_tile_ref, far_tile_ref, out_ref, cols,
+):
+    probes = near_sums_ref.shape[0]
     ncols = out_ref.shape[0]
     feats, width = inverse_ref.shape
-    middle = own_ref.shape[0]
-    cols[:middle, :] = own_ref[...]
-    cols[middle:, :] = other_ref[...]
-    put_rows(far_ref, inverse_ref[...], rows)
-    part = tile_and_product(cols, rows, vectors_of(far_ref, feats), tile_ref)
-    part += jnp.concatenate([own_sums_ref[...], other_sums_ref[...]], axis=1)
+    put_columns(raw_ref, inverse_ref[...], cols)
+    own = near_sums_ref[...] + far_sums_ref[...]
+    other = tile_and_product(cols, near_rows_ref, vectors_of(near_ref, feats), near_tile_ref)
+    other += tile_and_product(cols, far_rows_ref, vectors_of(far_ref, feats), far_tile_ref)
+    part = jnp.concatenate([own, other], axis=1)
     for index, place in enumerate(placing(ncols)):
         value = part[:, index * width:(index + 1) * width]
         high = value.astype(BF16)
@@ -159,15 +156,17 @@
     return jnp.sum(grid, axis=0, keepdims=True)
 
 
-def second_product(factor, own_ref, other_ref, far_ref, rows_ref, parts_ref, right_ref, image_ref, out_ref):
+def second_product(factor, own_ref, own_far_ref, other_ref, other_far_ref, rows_ref, parts_ref, right_ref, image_ref, out_ref):
     ncols = out_ref.shape[0]
     probes, width = right_ref.shape
     me = lax.axis_index("core")
     near, far = [
         jnp.concatenate([rows_ref[half, index] for index in range(rows_ref.shape[1])], axis=1) for half in (me, 1 - me)
     ]
-    part = dot_last(far, far_ref[...])
-    part += jnp.concatenate([dot_last(near, own_ref[...]), dot_last(near, other_ref[...])], axis=1)
+    part = jnp.concatenate([
+        dot_last(near, own_ref[...]) + dot_last(far, own_far_ref[...]),
+        dot_last(near, other_ref[...]) + dot_last(far, other_far_ref[...]),
+    ], axis=1)
     total = jnp.zeros((probes, width), F32)
     for index, place in enumerate(placing(ncols)):
         where = pl.ds(pl.multiple_of(place * probes, probes), probes)
@@ -260,15 +259,13 @@
     tile = pltpu.VMEM((middle, plane * width), BF16)
     wide = shaped(BF16, feats + EXTRA, plane * width)
     sums = shaped(F32, probes, middle)
-    tile_own, sums_own, rows = call(own_near, inverse, cols, near, outs=[tile, sums, wide], limit=24)
-    tile_other, sums_other, more = call(
-        other_near, inverse, other, near, rows, outs=[tile, sums, held_cols], limit=24
-    )
-    tile_far, parts = call(
-        far_product, inverse, cols, more, far, sums_own, sums_other,
-        outs=[pltpu.VMEM((2 * middle, plane * width), BF16), shaped(BF16, ny, (ny + 1) * probes, width)],
+    tile_own, sums_near, rows_near = call(own_half, inverse, cols, near, outs=[tile, sums, wide], limit=24)
+    tile_own_far, sums_far, rows_far = call(own_half, inverse, cols, far, outs=[tile, sums, wide], limit=24)
+    tile_other, tile_other_far, parts = call(
+        other_half, inverse, other, near, far, rows_near, rows_far, sums_near, sums_far,
+        outs=[tile, tile, shaped(BF16, ny, (ny + 1) * probes, width)],
         limit=24,
-        scratch=[pltpu.VMEM(wide.shape, BF16), pltpu.VMEM((2 * middle, feats + EXTRA), BF16)],
+        scratch=[pltpu.VMEM((middle, feats + EXTRA), BF16)],
     )
     parts = exchange(parts, COLS)
     image, rows = call(
@@ -276,7 +273,7 @@
     )
     both = lax.all_gather(exchange(rows, ("x", "z")), "core")
     sums = call(
-        functools.partial(second_product, factor), held(tile_own), held(tile_other), held(tile_far), both, parts, right, image,
+        functools.partial(second_product, factor), held(tile_own), held(tile_own_far), held(tile_other), held(tile_other_far), both, parts, right, image,
         outs=shaped(F32, ny, probes + PAD, width),
     )
     second, local = call(gathered, exchange(sums, COLS), outs=[block, shaped(F32, plane * ncore, width)])

time: 119 us -> 118 us (level)
    all_gather x1, blocking collectives: 6.11 us -> 4.51 us  [per_device(): both = lax.all_gather(exchange(rows, ('x', 'z')), 'core')]
where the time goes in v14:
time: 118 us
  blocking collectives  73 us (62%)
  starting transfers between devices  23.8 us (20%)
  Pallas kernels  16.4 us (14%)
  waiting for transfers between devices  4.01 us (3%)
    all_to_all x4, blocking collectives, exchange(): return lax.all_to_all(values, axes, 0, 0, tiled=True)  56.2 us
    pallas_call x9, Pallas kernels, call(): pl.pallas_call(kernel, in_specs=specs or [VMEM] * len(args), out_specs=ja...  16.4 us
    all_to_all x1, starting transfers between devices, exchange(): return lax.all_to_all(values, axes, 0, 0, tiled=True)  13.7 us
    all_gather x2, blocking collectives, per_device(): raw = lax.all_gather(raw, axis, axis=0, tiled=True)  12.2 us
    ppermute x1, starting transfers between devices, per_device(): far = lax.ppermute(near, 'core', swap)  6.91 us
    all_gather x1, blocking collectives, per_device(): both = lax.all_gather(exchange(rows, ('x', 'z')), 'core')  4.51 us
    all_to_all x1, waiting for transfers between devices, exchange(): return lax.all_to_all(values, axes, 0, 0, tiled=True)  4.01 us
    ppermute x1, starting transfers between devices, per_device(): other = lax.ppermute(raw, COLS[2], swap)  3.2 us
  transfers between devices with their start and end apart: 3, of which 1 were waited for; matrix products, arithmetic and copies ran while one was open for 0% of the time, Pallas kernels for 4%

profile of v14, /device:TPU:1, one launch (start us, length us, event | category | flops | bytes accessed | tf_op | source)
XLA Modules:
  0.0 117.9 jit_solution(10612251791718832665)
XLA Ops:
  0.6 1.7 %shard_map.50 = (bf16[32,80,128]{2,1,0:T(8,128)(2,1)}, f32[16,128]{1,0:T(8,128)S(1)}, f32[64,128]{1,0:T(8,128)S(1)}) custom-call(bf16[64,128]{1,0:T(8,128)(2,1)} %features_ref.1, f32[16,128]{1,0:T(8,128)} %right_ref.1, f32[1,64]{1,0:T(1,128)} %bitcast.11), custom_call_target="tpu_custom_call" | custom-call | tf_op jit(solution)/shard_map/pallas_call | solution.py:19
  2.3 13.7 %all-to-all-start = ((bf16[32,80,128]{2,1,0:T(8,128)(2,1)}), bf16[32,80,128]{2,1,0:T(8,128)(2,1)S(1)}, u32[]{:S(2)}, u32[]{:S(2)}) async-start(bf16[32,80,128]{2,1,0:T(8,128)(2,1)} %get-tuple-element.21), calls=%async_computation | async-start | bytes 1310720 | tf_op jit(solution)/shard_map/all_to_all | solution.py:231
  16.0 7.6 %all-gather = bf16[128,128]{1,0:T(8,128)(2,1)S(1)} all-gather(bf16[64,128]{1,0:T(8,128)(2,1)} %features_ref.1), channel_id=2, replica_groups=mesh['x'=4,'z'=8,'core'=2,'ya'=2,'yb'=2,'yc'=2] {'ya'}, dimensions={0}, use_global_device_ids=true | all-gather | bytes 49152 | tf_op jit(solution)/shard_map/all_gather | solution.py:252
  23.7 4.6 %all_gather.13.cols_ref = bf16[4,64,128]{2,1,0:T(8,128)(2,1)S(1)} all-gather(bf16[2,64,128]{2,1,0:T(8,128)(2,1)S(1)} %bitcast.10), channel_id=1, replica_groups=mesh['x'=4,'z'=8,'core'=2,'ya'=2,'yb'=2,'yc'=2] {'yb'}, dimensions={0}, use_global_device_ids=true | all-gather | bytes 98304 | tf_op jit(solution)/shard_map/all_gather | solution.py:252
  28.3 0.1 shard_map.51.cols_ref
  28.4 4.0 %all-to-all-done.rows_in_ref.near_ref = bf16[32,80,128]{2,1,0:T(8,128)(2,1)S(1)} async-done(((bf16[32,80,128]{2,1,0:T(8,128)(2,1)}), bf16[32,80,128]{2,1,0:T(8,128)(2,1)S(1)}, u32[]{:S(2)}, u32[]{:S(2)}) %all-to-all-start) | async-done | bytes 655392 | tf_op jit(solution)/shard_map/all_to_all | solution.py:231
  32.4 6.9 %collective-permute-start = (bf16[32,80,128]{2,1,0:T(8,128)(2,1)S(1)}, bf16[32,80,128]{2,1,0:T(8,128)(2,1)S(1)}, u32[]{:S(2)}, u32[]{:S(2)}) collective-permute-start(bf16[32,80,128]{2,1,0:T(8,128)(2,1)S(1)} %all-to-all-done.rows_in_ref.near_ref), channel_id=1, source_target_pairs={{0,8},{8,0},{1,9},{9,1},{2,10},{10,2},{3,11},{11,3},{4,12},{12,4},... | collective-permute-start | bytes 1966088 | tf_op jit(solution)/shard_map/ppermute | solution.py:258
  39.3 3.2 %collective-permute-start.1 = (bf16[4,64,128]{2,1,0:T(8,128)(2,1)S(1)}, bf16[4,64,128]{2,1,0:T(8,128)(2,1)S(1)}, u32[]{:S(2)}, u32[]{:S(2)}) collective-permute-start(bf16[4,64,128]{2,1,0:T(8,128)(2,1)S(1)} %all_gather.13.cols_ref), channel_id=1, source_target_pairs={{0,1},{1,0},{2,3},{3,2},{4,5},{5,4},{6,7},{7,6},{8,9},{9,8},{10,11... | collective-permute-start | bytes 196616 | tf_op jit(solution)/shard_map/ppermute | solution.py:253
  42.5 2.4 %shard_map.52 = (bf16[512,4096]{1,0:T(8,128)(2,1)S(1)}, f32[16,512]{1,0:T(8,128)S(1)}, bf16[80,4096]{1,0:T(8,128)(2,1)S(1)}) custom-call(f32[64,128]{1,0:T(8,128)S(1)} %get-tuple-element.20.inverse_ref, bf16[512,80]{1,0:T(8,128)(2,1)S(1)} %shard_map.51.cols_ref, bf16[32,80,128]{2,1,0:T(8,128)(2,1)S(1)} %all-to-all-done.rows_in_ref.near_ref), custom_call_target="tpu_custom_call" | custom-call | tf_op jit(solution)/shard_map/pallas_call | solution.py:19
  44.9 0.0 collective-permute-done.rows_in_ref.far_ref
  45.0 2.4 %shard_map.53 = (bf16[512,4096]{1,0:T(8,128)(2,1)S(1)}, f32[16,512]{1,0:T(8,128)S(1)}, bf16[80,4096]{1,0:T(8,128)(2,1)S(1)}) custom-call(f32[64,128]{1,0:T(8,128)S(1)} %get-tuple-element.20.inverse_ref, bf16[512,80]{1,0:T(8,128)(2,1)S(1)} %shard_map.51.cols_ref, bf16[32,80,128]{2,1,0:T(8,128)(2,1)S(1)} %collective-permute-done.rows_in_ref.far_ref), custom_call_target="tpu_custom_call" | custom-call | tf_op jit(solution)/shard_map/pallas_call | solution.py:19
  47.4 0.0 collective-permute-done.1.raw_ref
  47.4 4.6 %shard_map.54 = (bf16[512,4096]{1,0:T(8,128)(2,1)S(1)}, bf16[512,4096]{1,0:T(8,128)(2,1)S(1)}, bf16[8,144,128]{2,1,0:T(8,128)(2,1)S(1)}) custom-call(f32[64,128]{1,0:T(8,128)S(1)} %get-tuple-element.20.inverse_ref, bf16[4,64,128]{2,1,0:T(8,128)(2,1)S(1)} %collective-permute-done.1.raw_ref, bf16[32,80,128]{2,1,0:T(8,128)(2,1)S(1)} %all-to-all-done.rows_in_ref.near_ref, ...), custom_call_target="tpu_custom_call" | custom-call | tf_op jit(solution)/shard_map/pallas_call | solution.py:19
  51.9 18.1 %all_to_all.31.parts_ref = bf16[8,144,128]{2,1,0:T(8,128)(2,1)S(1)} all-to-all(bf16[8,144,128]{2,1,0:T(8,128)(2,1)S(1)} %get-tuple-element.32), channel_id=1, replica_groups=mesh['x'=4,'z'=8,'core'=2,'ya'=2,'yb'=2,'yc'=2] {'ya','yb','yc'}, dimensions={0} | all-to-all | bytes 589824 | tf_op jit(solution)/shard_map/all_to_all | solution.py:231
  70.0 13.5 %all_to_all.32 = bf16[32,16,128]{2,1,0:T(8,128)(2,1)S(1)} all-to-all(bf16[32,16,128]{2,1,0:T(8,128)(2,1)S(1)} %get-tuple-element.33), channel_id=1, replica_groups=mesh['x'=4,'z'=8,'core'=2,'ya'=2,'yb'=2,'yc'=2] {'x','z'}, dimensions={0} | all-to-all | bytes 262144 | tf_op jit(solution)/shard_map/all_to_all | solution.py:231
  83.6 4.5 %all-gather.1 = bf16[64,16,128]{2,1,0:T(8,128)(2,1)S(1)} all-gather(bf16[32,16,128]{2,1,0:T(8,128)(2,1)S(1)} %all_to_all.32), channel_id=3, replica_groups=mesh['x'=4,'z'=8,'core'=2,'ya'=2,'yb'=2,'yc'=2] {'core'}, dimensions={0}, use_global_device_ids=true | all-gather | bytes 393216 | tf_op jit(solution)/shard_map/all_gather | solution.py:274
  88.1 4.5 %shard_map.56 = f32[8,24,128]{2,1,0:T(8,128)S(1)} custom-call(bf16[512,4096]{1,0:T(8,128)(2,1)S(1)} %get-tuple-element.24.own_ref, bf16[512,4096]{1,0:T(8,128)(2,1)S(1)} %get-tuple-element.25.own_far_ref, bf16[512,4096]{1,0:T(8,128)(2,1)S(1)} %get-tuple-element.30.other_ref, bf16[512,4096]{1,0:T(8,128)(2,1)S(1)} %get-tuple-element.31.other_far_ref, ...), custom_call_target="tpu_custom_call" | custom-call | tf_op jit(solution)/shard_map/pallas_call | solution.py:19
  92.5 10.0 %all_to_all.33.parts_ref = f32[8,24,128]{2,1,0:T(8,128)S(1)} all-to-all(f32[8,24,128]{2,1,0:T(8,128)S(1)} %shard_map.56), channel_id=1, replica_groups=mesh['x'=4,'z'=8,'core'=2,'ya'=2,'yb'=2,'yc'=2] {'ya','yb','yc'}, dimensions={0} | all-to-all | bytes 196608 | tf_op jit(solution)/shard_map/all_to_all | solution.py:231
  102.6 14.6 %all_to_all.34 = f32[64,1,128]{2,1,0:T(1,128)S(1)} all-to-all(f32[64,1,128]{2,1,0:T(1,128)S(1)} %bitcast.9), channel_id=1, replica_groups=mesh['x'=4,'z'=8,'core'=2,'ya'=2,'yb'=2,'yc'=2] {'x','z','core'}, dimensions={0} | all-to-all | bytes 65536 | tf_op jit(solution)/shard_map/all_to_all | solution.py:231
  117.2 0.7 shard_map.58
  (2 shorter events, 0.0 us)
Async XLA Ops:
  2.3 30.1 %all-to-all-start = ((bf16[32,80,128]{2,1,0:T(8,128)(2,1)}), bf16[32,80,128]{2,1,0:T(8,128)(2,1)S(1)}, u32[]{:S(2)}, u32[]{:S(2)}) async-start(bf16[32,80,128]{2,1,0:T(8,128)(2,1)} %get-tuple-element.21), calls=%async_computation | async-start | bytes 1310720 | tf_op jit(solution)/shard_map/all_to_all | solution.py:231
  32.4 12.5 %collective-permute-start = (bf16[32,80,128]{2,1,0:T(8,128)(2,1)S(1)}, bf16[32,80,128]{2,1,0:T(8,128)(2,1)S(1)}, u32[]{:S(2)}, u32[]{:S(2)}) collective-permute-start(bf16[32,80,128]{2,1,0:T(8,128)(2,1)S(1)} %all-to-all-done.rows_in_ref.near_ref), channel_id=1, source_target_pairs={{0,8},{8,0},{1,9},{9,1},{2,10},{10,2},{3,11},{11,3},{4,12},{12,4},... | collective-permute-start | bytes 1966088 | tf_op jit(solution)/shard_map/ppermute | solution.py:258
  39.3 8.0 %collective-permute-start.1 = (bf16[4,64,128]{2,1,0:T(8,128)(2,1)S(1)}, bf16[4,64,128]{2,1,0:T(8,128)(2,1)S(1)}, u32[]{:S(2)}, u32[]{:S(2)}) collective-permute-start(bf16[4,64,128]{2,1,0:T(8,128)(2,1)S(1)} %all_gather.13.cols_ref), channel_id=1, source_target_pairs={{0,1},{1,0},{2,3},{3,2},{4,5},{5,4},{6,7},{7,6},{8,9},{9,8},{10,11... | collective-permute-start | bytes 196616 | tf_op jit(solution)/shard_map/ppermute | solution.py:253

commit v15 on v14

--- a/solution.py
+++ b/solution.py
@@ -15,11 +15,11 @@
 VMEM = pl.BlockSpec(memory_space=pltpu.VMEM)
 
 
-def call(kernel, *args, outs, limit=16, scratch=(), specs=None):
+def call(kernel, *args, outs, limit=16, scratch=(), specs=None, out_specs=None):
     return pl.pallas_call(
         kernel,
         in_specs=specs or [VMEM] * len(args),
-        out_specs=jax.tree.map(lambda _: VMEM, outs),
+        out_specs=out_specs or jax.tree.map(lambda _: VMEM, outs),
         out_shape=outs,
         scratch_shapes=scratch,
         compiler_params=pltpu.CompilerParams(vmem_limit_bytes=limit << 20),
@@ -48,7 +48,7 @@
     return jnp.concatenate([scaled, below.astype(BF16)], axis=0)
 
 
-def row_copies(features_ref, right_ref, scale_ref, rows_ref, kept_ref, inverse_ref, held, scales, sems):
+def row_copies(features_ref, right_ref, scale_ref, rows_ref, kept_ref, inverse_ref, held, scales, sems, packed, out_sems):
     moves = [
         pltpu.make_async_copy(features_ref, held, sems.at[0]),
         pltpu.make_async_copy(right_ref, kept_ref, sems.at[1]),
@@ -58,15 +58,20 @@
         move.start()
     for move in moves:
         move.wait()
-    features, right = held[...], kept_ref[...].astype(BF16)
-    feats = features.shape[0]
-    for index in range(rows_ref.shape[0]):
-        rows_ref[index, :feats, :] = features
-        rows_ref[index, feats:, :] = right
+    feats = held.shape[0]
+    packed[:feats, :] = held[...]
+    packed[feats:, :] = kept_ref[...].astype(BF16)
+    sent = [
+        pltpu.make_async_copy(packed, rows_ref.at[index], out_sems.at[index]) for index in range(rows_ref.shape[0])
+    ]
+    for move in sent:
+        move.start()
     lane = lax.broadcasted_iota(jnp.int32, (feats, feats), 1)
     row = lax.broadcasted_iota(jnp.int32, (feats, feats), 0)
     scale = jnp.sum(jnp.where(lane == row, scales[...], 0.0), axis=1, keepdims=True)
     inverse_ref[...] = jnp.broadcast_to(1.0 / scale, inverse_ref.shape)
+    for move in sent:
+        move.wait()
 
 
 def put_columns(cols_ref, inverse, out_ref):
@@ -243,7 +248,9 @@
         outs=[
             shaped(BF16, plane, feats + probes, width), pltpu.VMEM(block.shape, F32), pltpu.VMEM((feats, width), F32),
         ],
-        scratch=[pltpu.VMEM(features.shape, BF16), pltpu.VMEM((1, feats), F32), pltpu.SemaphoreType.DMA((3,))],
+        scratch=[pltpu.VMEM(features.shape, BF16), pltpu.VMEM((1, feats), F32), pltpu.SemaphoreType.DMA((3,)),
+                 pltpu.VMEM((feats + probes, width), BF16), pltpu.SemaphoreType.DMA((plane,))],
+        out_specs=[far_off, VMEM, VMEM],
     )
     right, inverse = held(right), held(inverse)
     near = exchange(rows, ("x", "z"))

time: 118 us -> 119 us (level)
  no operation moved by 1% of the time
where the time goes in v15:
time: 119 us; the launch traced here: 118 us
  blocking collectives  73 us (61%)
  starting transfers between devices  23.8 us (20%)
  Pallas kernels  16.6 us (14%)
  waiting for transfers between devices  4.01 us (3%)
    all_to_all x4, blocking collectives, exchange(): return lax.all_to_all(values, axes, 0, 0, tiled=True)  56.2 us
    pallas_call x9, Pallas kernels, call(): pl.pallas_call(kernel, in_specs=specs or [VMEM] * len(args), out_specs=ou...  16.6 us
    all_to_all x1, starting transfers between devices, exchange(): return lax.all_to_all(values, axes, 0, 0, tiled=True)  13.7 us
    all_gather x2, blocking collectives, per_device(): raw = lax.all_gather(raw, axis, axis=0, tiled=True)  12.2 us
    ppermute x1, starting transfers between devices, per_device(): far = lax.ppermute(near, 'core', swap)  6.91 us
    all_gather x1, blocking collectives, per_device(): both = lax.all_gather(exchange(rows, ('x', 'z')), 'core')  4.51 us
    all_to_all x1, waiting for transfers between devices, exchange(): return lax.all_to_all(values, axes, 0, 0, tiled=True)  4.01 us
    ppermute x1, starting transfers between devices, per_device(): other = lax.ppermute(raw, COLS[2], swap)  3.2 us
  transfers between devices with their start and end apart: 3, of which 1 were waited for; matrix products, arithmetic and copies ran while one was open for 0% of the time, Pallas kernels for 4%

profile of v15, /device:TPU:1, one launch (start us, length us, event | category | flops | bytes accessed | tf_op | source)
XLA Modules:
  0.0 118.1 jit_solution(4695678390450727001)
XLA Ops:
  0.6 1.9 %shard_map.50 = (bf16[32,80,128]{2,1,0:T(8,128)(2,1)}, f32[16,128]{1,0:T(8,128)S(1)}, f32[64,128]{1,0:T(8,128)S(1)}) custom-call(bf16[64,128]{1,0:T(8,128)(2,1)} %features_ref.1, f32[16,128]{1,0:T(8,128)} %right_ref.1, f32[1,64]{1,0:T(1,128)} %bitcast.11), custom_call_target="tpu_custom_call" | custom-call | tf_op jit(solution)/shard_map/pallas_call | solution.py:19
  2.5 13.7 %all-to-all-start = ((bf16[32,80,128]{2,1,0:T(8,128)(2,1)}), bf16[32,80,128]{2,1,0:T(8,128)(2,1)S(1)}, u32[]{:S(2)}, u32[]{:S(2)}) async-start(bf16[32,80,128]{2,1,0:T(8,128)(2,1)} %get-tuple-element.21), calls=%async_computation | async-start | bytes 1310720 | tf_op jit(solution)/shard_map/all_to_all | solution.py:236
  16.2 7.6 %all-gather = bf16[128,128]{1,0:T(8,128)(2,1)S(1)} all-gather(bf16[64,128]{1,0:T(8,128)(2,1)} %features_ref.1), channel_id=2, replica_groups=mesh['x'=4,'z'=8,'core'=2,'ya'=2,'yb'=2,'yc'=2] {'ya'}, dimensions={0}, use_global_device_ids=true | all-gather | bytes 49152 | tf_op jit(solution)/shard_map/all_gather | solution.py:259
  23.9 4.6 %all_gather.13.cols_ref = bf16[4,64,128]{2,1,0:T(8,128)(2,1)S(1)} all-gather(bf16[2,64,128]{2,1,0:T(8,128)(2,1)S(1)} %bitcast.10), channel_id=1, replica_groups=mesh['x'=4,'z'=8,'core'=2,'ya'=2,'yb'=2,'yc'=2] {'yb'}, dimensions={0}, use_global_device_ids=true | all-gather | bytes 98304 | tf_op jit(solution)/shard_map/all_gather | solution.py:259
  28.5 0.1 shard_map.51.cols_ref
  28.6 4.0 %all-to-all-done.rows_in_ref.near_ref = bf16[32,80,128]{2,1,0:T(8,128)(2,1)S(1)} async-done(((bf16[32,80,128]{2,1,0:T(8,128)(2,1)}), bf16[32,80,128]{2,1,0:T(8,128)(2,1)S(1)}, u32[]{:S(2)}, u32[]{:S(2)}) %all-to-all-start) | async-done | bytes 655392 | tf_op jit(solution)/shard_map/all_to_all | solution.py:236
  32.6 6.9 %collective-permute-start = (bf16[32,80,128]{2,1,0:T(8,128)(2,1)S(1)}, bf16[32,80,128]{2,1,0:T(8,128)(2,1)S(1)}, u32[]{:S(2)}, u32[]{:S(2)}) collective-permute-start(bf16[32,80,128]{2,1,0:T(8,128)(2,1)S(1)} %all-to-all-done.rows_in_ref.near_ref), channel_id=1, source_target_pairs={{0,8},{8,0},{1,9},{9,1},{2,10},{10,2},{3,11},{11,3},{4,12},{12,4},... | collective-permute-start | bytes 1966088 | tf_op jit(solution)/shard_map/ppermute | solution.py:265
  39.6 3.2 %collective-permute-start.1 = (bf16[4,64,128]{2,1,0:T(8,128)(2,1)S(1)}, bf16[4,64,128]{2,1,0:T(8,128)(2,1)S(1)}, u32[]{:S(2)}, u32[]{:S(2)}) collective-permute-start(bf16[4,64,128]{2,1,0:T(8,128)(2,1)S(1)} %all_gather.13.cols_ref), channel_id=1, source_target_pairs={{0,1},{1,0},{2,3},{3,2},{4,5},{5,4},{6,7},{7,6},{8,9},{9,8},{10,11... | collective-permute-start | bytes 196616 | tf_op jit(solution)/shard_map/ppermute | solution.py:260
  42.8 2.4 %shard_map.52 = (bf16[512,4096]{1,0:T(8,128)(2,1)S(1)}, f32[16,512]{1,0:T(8,128)S(1)}, bf16[80,4096]{1,0:T(8,128)(2,1)S(1)}) custom-call(f32[64,128]{1,0:T(8,128)S(1)} %get-tuple-element.20.inverse_ref, bf16[512,80]{1,0:T(8,128)(2,1)S(1)} %shard_map.51.cols_ref, bf16[32,80,128]{2,1,0:T(8,128)(2,1)S(1)} %all-to-all-done.rows_in_ref.near_ref), custom_call_target="tpu_custom_call" | custom-call | tf_op jit(solution)/shard_map/pallas_call | solution.py:19
  45.2 0.0 collective-permute-done.rows_in_ref.far_ref
  45.2 2.4 %shard_map.53 = (bf16[512,4096]{1,0:T(8,128)(2,1)S(1)}, f32[16,512]{1,0:T(8,128)S(1)}, bf16[80,4096]{1,0:T(8,128)(2,1)S(1)}) custom-call(f32[64,128]{1,0:T(8,128)S(1)} %get-tuple-element.20.inverse_ref, bf16[512,80]{1,0:T(8,128)(2,1)S(1)} %shard_map.51.cols_ref, bf16[32,80,128]{2,1,0:T(8,128)(2,1)S(1)} %collective-permute-done.rows_in_ref.far_ref), custom_call_target="tpu_custom_call" | custom-call | tf_op jit(solution)/shard_map/pallas_call | solution.py:19
  47.6 0.0 collective-permute-done.1.raw_ref
  47.6 4.6 %shard_map.54 = (bf16[512,4096]{1,0:T(8,128)(2,1)S(1)}, bf16[512,4096]{1,0:T(8,128)(2,1)S(1)}, bf16[8,144,128]{2,1,0:T(8,128)(2,1)S(1)}) custom-call(f32[64,128]{1,0:T(8,128)S(1)} %get-tuple-element.20.inverse_ref, bf16[4,64,128]{2,1,0:T(8,128)(2,1)S(1)} %collective-permute-done.1.raw_ref, bf16[32,80,128]{2,1,0:T(8,128)(2,1)S(1)} %all-to-all-done.rows_in_ref.near_ref, ...), custom_call_target="tpu_custom_call" | custom-call | tf_op jit(solution)/shard_map/pallas_call | solution.py:19
  52.1 18.1 %all_to_all.31.parts_ref = bf16[8,144,128]{2,1,0:T(8,128)(2,1)S(1)} all-to-all(bf16[8,144,128]{2,1,0:T(8,128)(2,1)S(1)} %get-tuple-element.32), channel_id=1, replica_groups=mesh['x'=4,'z'=8,'core'=2,'ya'=2,'yb'=2,'yc'=2] {'ya','yb','yc'}, dimensions={0} | all-to-all | bytes 589824 | tf_op jit(solution)/shard_map/all_to_all | solution.py:236
  70.2 13.5 %all_to_all.32 = bf16[32,16,128]{2,1,0:T(8,128)(2,1)S(1)} all-to-all(bf16[32,16,128]{2,1,0:T(8,128)(2,1)S(1)} %get-tuple-element.33), channel_id=1, replica_groups=mesh['x'=4,'z'=8,'core'=2,'ya'=2,'yb'=2,'yc'=2] {'x','z'}, dimensions={0} | all-to-all | bytes 262144 | tf_op jit(solution)/shard_map/all_to_all | solution.py:236
  83.8 4.5 %all-gather.1 = bf16[64,16,128]{2,1,0:T(8,128)(2,1)S(1)} all-gather(bf16[32,16,128]{2,1,0:T(8,128)(2,1)S(1)} %all_to_all.32), channel_id=3, replica_groups=mesh['x'=4,'z'=8,'core'=2,'ya'=2,'yb'=2,'yc'=2] {'core'}, dimensions={0}, use_global_device_ids=true | all-gather | bytes 393216 | tf_op jit(solution)/shard_map/all_gather | solution.py:281
  88.3 4.5 %shard_map.56 = f32[8,24,128]{2,1,0:T(8,128)S(1)} custom-call(bf16[512,4096]{1,0:T(8,128)(2,1)S(1)} %get-tuple-element.24.own_ref, bf16[512,4096]{1,0:T(8,128)(2,1)S(1)} %get-tuple-element.25.own_far_ref, bf16[512,4096]{1,0:T(8,128)(2,1)S(1)} %get-tuple-element.30.other_ref, bf16[512,4096]{1,0:T(8,128)(2,1)S(1)} %get-tuple-element.31.other_far_ref, ...), custom_call_target="tpu_custom_call" | custom-call | tf_op jit(solution)/shard_map/pallas_call | solution.py:19
  92.8 10.0 %all_to_all.33.parts_ref = f32[8,24,128]{2,1,0:T(8,128)S(1)} all-to-all(f32[8,24,128]{2,1,0:T(8,128)S(1)} %shard_map.56), channel_id=1, replica_groups=mesh['x'=4,'z'=8,'core'=2,'ya'=2,'yb'=2,'yc'=2] {'ya','yb','yc'}, dimensions={0} | all-to-all | bytes 196608 | tf_op jit(solution)/shard_map/all_to_all | solution.py:236
  102.8 14.6 %all_to_all.34 = f32[64,1,128]{2,1,0:T(1,128)S(1)} all-to-all(f32[64,1,128]{2,1,0:T(1,128)S(1)} %bitcast.9), channel_id=1, replica_groups=mesh['x'=4,'z'=8,'core'=2,'ya'=2,'yb'=2,'yc'=2] {'x','z','core'}, dimensions={0} | all-to-all | bytes 65536 | tf_op jit(solution)/shard_map/all_to_all | solution.py:236
  117.4 0.7 shard_map.58
  (2 shorter events, 0.0 us)
Async XLA Ops:
  2.5 30.1 %all-to-all-start = ((bf16[32,80,128]{2,1,0:T(8,128)(2,1)}), bf16[32,80,128]{2,1,0:T(8,128)(2,1)S(1)}, u32[]{:S(2)}, u32[]{:S(2)}) async-start(bf16[32,80,128]{2,1,0:T(8,128)(2,1)} %get-tuple-element.21), calls=%async_computation | async-start | bytes 1310720 | tf_op jit(solution)/shard_map/all_to_all | solution.py:236
  32.6 12.5 %collective-permute-start = (bf16[32,80,128]{2,1,0:T(8,128)(2,1)S(1)}, bf16[32,80,128]{2,1,0:T(8,128)(2,1)S(1)}, u32[]{:S(2)}, u32[]{:S(2)}) collective-permute-start(bf16[32,80,128]{2,1,0:T(8,128)(2,1)S(1)} %all-to-all-done.rows_in_ref.near_ref), channel_id=1, source_target_pairs={{0,8},{8,0},{1,9},{9,1},{2,10},{10,2},{3,11},{11,3},{4,12},{12,4},... | collective-permute-start | bytes 1966088 | tf_op jit(solution)/shard_map/ppermute | solution.py:265
  39.6 8.0 %collective-permute-start.1 = (bf16[4,64,128]{2,1,0:T(8,128)(2,1)S(1)}, bf16[4,64,128]{2,1,0:T(8,128)(2,1)S(1)}, u32[]{:S(2)}, u32[]{:S(2)}) collective-permute-start(bf16[4,64,128]{2,1,0:T(8,128)(2,1)S(1)} %all_gather.13.cols_ref), channel_id=1, source_target_pairs={{0,1},{1,0},{2,3},{3,2},{4,5},{5,4},{6,7},{7,6},{8,9},{9,8},{10,11... | collective-permute-start | bytes 196616 | tf_op jit(solution)/shard_map/ppermute | solution.py:260
